TPU v7x, 32 devices: a whole 2x2x4 slice. The times are simulated.
32 devices in a mesh: groups: 2 (over y), ctx: 4 (over z), head: 2 (over x), sub: 2 (over core).
Axes of the slice: x: 2, y: 2, z: 4, core: 2. Of those that a mesh axis runs over, the one named last changes fastest.
Arguments:
- att_query: bfloat16 [1024, 4096], P(('groups', 'ctx'), ('head', 'sub')), parts along dimension 0, may hold values from -4 to 4
- att_gate: bfloat16 [1024, 4096], P(('groups', 'ctx'), ('head', 'sub')), parts along dimension 0, may hold values from -6 to 6
- att_kv: bfloat16 [1024, 1024], P(('groups', 'ctx')), parts along dimension 0, may hold values from -4 to 4
- residual: bfloat16 [1024, 2048], P(('groups', 'ctx'), ('head', 'sub')), parts along dimension 0, may hold values from -0.19921875 to 0.19921875
- out_weight: bfloat16 [4096, 2048], P(('head', 'sub')), may hold values from -0.5 to 0.5
- norm_gain: float32 [2048], replicated, may hold values from 0.1 to 1.9
- in_weight: bfloat16 [2048, 8192], P(None, ('head', 'sub')), may hold values from -0.125 to 0.125
- beta_weight: bfloat16 [2048, 32], P(None, ('head', 'sub')), may hold values from -0.125 to 0.125
- log_decay: float32 [1024, 32], P(('groups', 'ctx'), ('head', 'sub')), parts along dimension 0, may hold values from -0.7 to 0, as said below
- delta_gain: float32 [128], replicated, may hold values from 0.1 to 1.9
Outputs:
- new_residual: bfloat16 [1024, 2048], P(('groups', 'ctx'), ('head', 'sub')), parts along dimension 0
- delta_out: bfloat16 [1024, 4096], P(('groups', 'ctx'), ('head', 'sub')), parts along dimension 0
There are 2 independent parts, one for each index of `groups`. A program takes and returns all parts, laid end to end along the dimension named above; an argument that names none is the same for every part. Nothing has to cross between parts.
Inputs may be any that keep to these rules, and one draw needn't show every extreme that they name: `log_decay`: negative.
All inputs are finite; a program needn't handle non-finite values.
Results may differ from a plain program's by a relative error of at most 0.035.
Values may be sent and summed in bfloat16 or wider, within the bound.
No kernel may reach another device: no remote copies, remote signals or barrier semaphores. Data moves between devices by JAX's collectives and lax.ppermute only.
A program may use at most 64 MiB of HBM per device.

v0:
```python
import jax
import jax.numpy as jnp
from jax import lax
from jax.sharding import PartitionSpec as P

HEADS = 16
KV_HEADS = 2
HD = 256
DK = 128
DV = 128


TOP_PRECISION = lax.Precision.HIGHEST
EPSILON = 1e-06
NEGATIVE = -1e30


def passed_along(value, axis, steps):
    count = lax.axis_size(axis)
    initial, last = (max(0, -steps), min(count, count - steps))
    return lax.ppermute(value, axis, [(source, source + steps) for source in range(initial, last)])


def stored_positions(first_row, row_total, half_rows, ctx_count):
    row_index = first_row + jnp.arange(row_total, dtype=jnp.int32)
    device_of = row_index // (2 * half_rows)
    within_dev = row_index % (2 * half_rows)
    block_number = jnp.where(within_dev < half_rows, device_of, 2 * ctx_count - 1 - device_of)
    return block_number * half_rows + within_dev % half_rows


def unit_rows(matrix):
    return matrix * lax.rsqrt(jnp.sum(matrix * matrix, axis=-1, keepdims=True) + EPSILON)


def to_blocks(array, half_rows):
    heads_count = array.shape[1]
    width = array.shape[2]
    shaped = array.reshape(2, half_rows, heads_count, width).transpose(2, 0, 1, 3)
    return shaped.reshape(heads_count * 2, half_rows, width)


def block_terms(query_rows, key_rows, value_rows, beta_rows, decay_rows):
    length = query_rows.shape[0]
    cumulative = jnp.cumsum(decay_rows)
    position = jnp.arange(length)
    on_or_below = position[:, None] >= position[None, :]
    strictly_below = position[:, None] > position[None, :]
    decay_gap = cumulative[:, None] - cumulative[None, :]
    decay_grid = jnp.where(on_or_below, jnp.exp(jnp.where(on_or_below, decay_gap, 0.0)), 0.0)
    key_gram = jnp.dot(key_rows, key_rows.T, precision=TOP_PRECISION)
    system = jnp.eye(length, dtype=jnp.float32) + jnp.where(
        strictly_below, beta_rows[:, None] * key_gram * decay_grid, 0.0
    )
    growth = jnp.exp(cumulative)
    right_side = beta_rows[:, None] * jnp.concatenate(
        [value_rows, growth[:, None] * key_rows], axis=1
    )
    solved = jax.scipy.linalg.solve_triangular(system, right_side, lower=True, unit_diagonal=True)
    update_rows = solved[:, : value_rows.shape[1]]
    weight_rows = solved[:, value_rows.shape[1] :]
    attend_grid = jnp.where(
        on_or_below, jnp.dot(query_rows, key_rows.T, precision=TOP_PRECISION) * decay_grid, 0.0
    )
    local_out = jnp.dot(attend_grid, update_rows, precision=TOP_PRECISION)
    read_rows = growth[:, None] * query_rows - jnp.dot(
        attend_grid, weight_rows, precision=TOP_PRECISION
    )
    carried_keys = jnp.exp(cumulative[-1] - cumulative)[:, None] * key_rows
    identity_map = jnp.eye(key_rows.shape[1], dtype=jnp.float32)
    transition = jnp.exp(cumulative[-1]) * identity_map - jnp.dot(
        carried_keys.T, weight_rows, precision=TOP_PRECISION
    )
    offset_state = jnp.dot(carried_keys.T, update_rows, precision=TOP_PRECISION)
    return (local_out, read_rows, transition, offset_state)


def apply_map(matrix_maps, offsets, states):
    return jnp.einsum("hij,hjk->hik", matrix_maps, states, precision=TOP_PRECISION) + offsets


def attend_rows(running, query_block, key_block, value_block, visible, score_scale):
    run_max, run_sum, run_acc = running
    scores = (
        jnp.einsum("rhd,kd->rhk", query_block, key_block, preferred_element_type=jnp.float32)
        * score_scale
    )
    if visible is not None:
        scores = jnp.where(visible[:, None, :], scores, NEGATIVE)
    new_max = jnp.maximum(run_max, jnp.max(scores, axis=2))
    weights = jnp.exp(scores - new_max[:, :, None])
    if visible is not None:
        weights = jnp.where(visible[:, None, :], weights, 0.0)
    rescale = jnp.exp(run_max - new_max)
    run_sum = run_sum * rescale + jnp.sum(weights, axis=2)
    added = jnp.einsum(
        "rhk,kd->rhd", weights.astype(jnp.bfloat16), value_block, preferred_element_type=jnp.float32
    )
    run_acc = run_acc * rescale[:, :, None] + added
    return (new_max, run_sum, run_acc)


def local(
    att_query,
    att_gate,
    att_kv,
    residual,
    out_weight,
    norm_gain,
    in_weight,
    beta_weight,
    log_decay,
    delta_gain,
):
    ctx_count = lax.axis_size("ctx")
    ctx_rank = lax.axis_index("ctx")
    shard_rank = lax.axis_index(("head", "sub"))
    rows_here = att_query.shape[0]
    half_rows = rows_here // 2
    heads_here = att_query.shape[1] // HD
    kv_number = shard_rank * heads_here // (HEADS // KV_HEADS)
    key_local = lax.dynamic_slice_in_dim(att_kv, kv_number * 2 * HD, HD, 1)
    value_local = lax.dynamic_slice_in_dim(att_kv, kv_number * 2 * HD + HD, HD, 1)
    query_heads = att_query.reshape(rows_here, heads_here, HD)
    late_queries = query_heads[half_rows:]
    query_places = stored_positions(ctx_rank * rows_here, rows_here, half_rows, ctx_count)
    same_visible = query_places[:, None] >= query_places[None, :]
    score_scale = HD ** (-0.5)

    def earlier_shard(running, key_shard, value_shard):
        return attend_rows(
            running, query_heads, key_shard[:half_rows], value_shard[:half_rows], None, score_scale
        )

    def same_shard(running, key_shard, value_shard):
        return attend_rows(running, query_heads, key_shard, value_shard, same_visible, score_scale)

    def later_shard(running, key_shard, value_shard):
        late_part = tuple((member[half_rows:] for member in running))
        renewed = attend_rows(late_part, late_queries, key_shard, value_shard, None, score_scale)
        return tuple(
            (
                jnp.concatenate([member[:half_rows], latest], axis=0)
                for member, latest in zip(running, renewed)
            )
        )

    start_running = (
        jnp.full((rows_here, heads_here), NEGATIVE, jnp.float32),
        jnp.zeros((rows_here, heads_here), jnp.float32),
        jnp.zeros((rows_here, heads_here, HD), jnp.float32),
    )
    key_block = lax.all_gather(key_local, "ctx", axis=0, tiled=True)
    value_block = lax.all_gather(value_local, "ctx", axis=0, tiled=True)
    piece_rows = key_block.shape[0]

    def one_shard(number, current):
        offset = number * rows_here
        key_shard = lax.dynamic_slice_in_dim(key_block, offset, rows_here, 0)
        value_shard = lax.dynamic_slice_in_dim(value_block, offset, rows_here, 0)
        shard_number = offset // rows_here
        branch = jnp.clip(shard_number - ctx_rank, -1, 1) + 1
        return lax.switch(
            branch, [earlier_shard, same_shard, later_shard], current, key_shard, value_shard
        )

    run_max, run_sum, run_acc = lax.fori_loop(0, piece_rows // rows_here, one_shard, start_running)
    gate_heads = jax.nn.sigmoid(att_gate.reshape(rows_here, heads_here, HD).astype(jnp.float32))
    att_heads = (
        (run_acc / run_sum[:, :, None] * gate_heads)
        .astype(jnp.bfloat16)
        .reshape(rows_here, heads_here * HD)
    )
    partial_term = jnp.dot(att_heads, out_weight, preferred_element_type=jnp.float32)
    col_width = residual.shape[1]
    col_start = shard_rank * col_width
    placed = lax.dynamic_slice_in_dim(partial_term, col_start, col_width, 1) + residual.astype(
        jnp.float32
    )
    partial_term = lax.dynamic_update_slice_in_dim(partial_term, placed, col_start, 1)
    hidden = lax.psum(partial_term.astype(jnp.bfloat16), ("head", "sub")).astype(jnp.float32)
    mean_square = jnp.mean(hidden * hidden, axis=1, keepdims=True)
    normed = (hidden * lax.rsqrt(mean_square + EPSILON) * norm_gain).astype(jnp.bfloat16)
    new_residual = lax.dynamic_slice_in_dim(hidden, col_start, col_width, 1).astype(jnp.bfloat16)
    mixed_cols = jnp.dot(normed, in_weight, preferred_element_type=jnp.float32)
    beta_logits = jnp.dot(normed, beta_weight, preferred_element_type=jnp.float32)
    key_here = in_weight.shape[1] // (2 * DK + 2 * DV)
    value_here = 2 * key_here
    grouped = mixed_cols.reshape(rows_here, key_here, 2 * DK + 2 * DV)
    query_unit = jnp.repeat(unit_rows(jax.nn.silu(grouped[:, :, :DK])) * DK ** (-0.5), 2, axis=1)
    key_unit = jnp.repeat(unit_rows(jax.nn.silu(grouped[:, :, DK : 2 * DK])), 2, axis=1)
    value_all = jax.nn.silu(grouped[:, :, 2 * DK :]).reshape(rows_here, value_here, DV)
    beta_all = jax.nn.sigmoid(beta_logits)
    local_out, read_rows, transition, offset_state = jax.vmap(block_terms)(
        to_blocks(query_unit, half_rows),
        to_blocks(key_unit, half_rows),
        to_blocks(value_all, half_rows),
        to_blocks(beta_all[:, :, None], half_rows)[:, :, 0],
        to_blocks(log_decay[:, :, None], half_rows)[:, :, 0],
    )
    transition = transition.reshape(value_here, 2, DK, DK)
    offset_state = offset_state.reshape(value_here, 2, DK, DV)
    early_map, late_map = (transition[:, 0], transition[:, 1])
    early_offset, late_offset = (offset_state[:, 0], offset_state[:, 1])
    last_rank = ctx_count - 1
    zero_states = jnp.zeros_like(early_offset)

    def early_turn(number, incoming):
        return passed_along(
            apply_map(early_map, early_offset, incoming).astype(jnp.bfloat16), "ctx", 1
        ).astype(jnp.float32)

    early_in = lax.fori_loop(0, ctx_count - 1, early_turn, zero_states)
    early_end = apply_map(early_map, early_offset, early_in)
    late_start = jnp.where(ctx_rank == last_rank, early_end, zero_states)

    def late_turn(number, incoming):
        moved = passed_along(
            apply_map(late_map, late_offset, incoming).astype(jnp.bfloat16), "ctx", -1
        ).astype(jnp.float32)
        return jnp.where(ctx_rank == last_rank, early_end, moved)

    late_in = lax.fori_loop(0, ctx_count - 1, late_turn, late_start)
    states_in = jnp.stack([early_in, late_in], axis=1)
    block_out = local_out.reshape(value_here, 2, half_rows, DV) + jnp.einsum(
        "hbck,hbkv->hbcv",
        read_rows.reshape(value_here, 2, half_rows, DK),
        states_in,
        precision=TOP_PRECISION,
    )
    token_out = block_out.transpose(1, 2, 0, 3).reshape(rows_here, value_here, DV)
    out_square = jnp.mean(token_out * token_out, axis=2, keepdims=True)
    delta_out = (token_out * lax.rsqrt(out_square + EPSILON) * delta_gain).astype(jnp.bfloat16)
    return (new_residual, delta_out.reshape(rows_here, value_here * DV))


def solution(mesh):
    return jax.shard_map(
        local,
        mesh=mesh,
        in_specs=(
            P(("groups", "ctx"), ("head", "sub")),
            P(("groups", "ctx"), ("head", "sub")),
            P(("groups", "ctx"), None),
            P(("groups", "ctx"), ("head", "sub")),
            P(("head", "sub"), None),
            P(),
            P(None, ("head", "sub")),
            P(None, ("head", "sub")),
            P(("groups", "ctx"), ("head", "sub")),
            P(),
        ),
        out_specs=(P(("groups", "ctx"), ("head", "sub")), P(("groups", "ctx"), ("head", "sub"))),
        check_vma=False,
    )
```

profile of v0, /device:TPU:0, one launch (start us, length us, event | category | flops | bytes accessed | tf_op | source)
XLA Modules:
  0.0 271.1 jit_solution(5752099669577821620)
XLA Ops:
  7.2 1.1 copy.66
  8.4 0.9 slice.67
  9.3 1.1 copy.70
  10.6 0.9 constant_dynamic-slice_fusion.2
  11.5 15.6 %all_gather.6 = bf16[512,256]{1,0:T(8,128)(2,1)S(1)} all-gather(bf16[128,256]{1,0:T(8,128)(2,1)S(1)} %get-tuple-element.569), channel_id=1, replica_groups=mesh['groups'=2,'ctx'=4,'head'=2,'sub'=2] {'ctx'}, dimensions={0}, use_global_device_ids=true | all-gather | bytes 327680 | tf_op jit(solution)/shard_map/all_gather | solution.py:153
  27.1 14.6 %all_gather.7 = bf16[512,256]{1,0:T(8,128)(2,1)S(1)} all-gather(bf16[128,256]{1,0:T(8,128)(2,1)S(1)} %get-tuple-element.568), channel_id=1, replica_groups=mesh['groups'=2,'ctx'=4,'head'=2,'sub'=2] {'ctx'}, dimensions={0}, use_global_device_ids=true | all-gather | bytes 327680 | tf_op jit(solution)/shard_map/all_gather | solution.py:154
  42.0 11.3 %while.44 = (s32[]{:T(128)}, f32[128,4]{0,1:T(4,128)S(1)}, f32[128,4]{0,1:T(4,128)S(1)}, f32[128,4,256]{2,0,1:T(8,128)S(1)}, s32[]{:T(128)}, /*index=5*/bf16[512...) while((s32[]{:T(128)}, f32[128,4]{0,1:T(4,128)S(1)}, ...), condition=%wide.region_10.11_spmd.clone, body=%wide.region_0.10_spmd.clone.sunk | while | flops 67978264 | bytes 3045988 | solution.py:167
  42.0 3.5 %conditional.3 = (f32[128,4]{0,1:T(4,128)}, f32[128,4]{0,1:T(4,128)S(1)}, f32[128,4,256]{2,0,1:T(8,128)S(1)}) conditional(s32[]{:T(128)} %clamp.12, (bf16[128,256]{1,0:T(8,128)(2,1)S(1)}, bf16[128,4,256]{2,0,1:T(8,128)(2,1)S(1)}, f32[128,4]{0,1:T(4,128)S(1)}, f32[128,4]{0,1:T(4,128)S(1)}, f32[128,4,256]{2,0,1:T(8,128)S(1)}, ...), branch_computations={%region_1.3_spmd, %region_4.6_spmd, %region_7.9_spmd} | conditional | flops 67978240 | bytes 2779160 | solution.py:163
  43.0 0.7 fusion.12
  43.7 0.7 multiply_add_fusion.1
  44.4 1.1 convolution_add_fusion.1
  45.5 0.7 copy.118
  46.2 1.6 conditional.3
  47.9 0.7 copy.118
  48.6 1.6 conditional.3
  50.9 1.6 conditional.3
  53.5 2.9 %fusion.75 = f32[128,2048]{1,0:T(8,128)S(1)} fusion(bf16[128,1024]{0,1:T(8,128)(2,1)S(1)} %bitcast.150, bf16[1024,2048]{1,0:T(8,128)(2,1)} %param.23), kind=kOutput, calls=%fused_computation.153 | convolution fusion | flops 536870912 | bytes 5505024 | tf_op jit(solution)/shard_map/dot_general | solution.py:174
  56.5 0.9 convert_element_type.68
  59.9 36.8 %all-reduce.2.cloned.1.call-done = bf16[128,2048]{1,0:T(8,128)(2,1)} async-done(((bf16[128,2048]{1,0:T(8,128)(2,1)}), bf16[128,2048]{1,0:T(8,128)(2,1)}) %all-reduce.2.cloned.1.call-update) | async-done | bytes 524304 | tf_op jit(solution)/shard_map/psum | solution.py:181
  96.7 1.2 multiply_reduce_fusion
  98.0 7.1 %fusion.63 = f32[128,2048]{0,1:T(8,128)S(1)} fusion(bf16[2048,2048]{1,0:T(8,128)(2,1)} %param.25, f32[2048]{0:T(1024)S(1)} %copy-done.5, f32[128]{0:T(128)S(1)} %add_rsqrt_fusion.3, bf16[128,2048]{1,0:T(8,128)(2,1)} %all-reduce.2.cloned.1.call-done), kind=kOutput, calls=%fused_computation.113 | convolution fusion | flops 1074790400 | bytes 9970176 | tf_op jit(solution)/shard_map/dot_general | solution.py:185
  107.5 1.0 fusion.35
  108.4 2.6 fusion.39
  111.0 80.0 %custom-call.4 = f32[16,1,64,64]{2,3,1,0:T(8,128)} custom-call(f32[16,1,64,64]{3,2,1,0:T(8,128)} %fusion.39), custom_call_target="InvertDiagBlocksLowerTriangular" | custom-call | tf_op jit(solution)/shard_map/vmap(jit(_solve_triangular))/triangular_solve | solution.py:59
  191.0 2.3 fusion.43
  193.3 1.5 fusion.57
  194.8 1.5 convolution_subtract_fusion.1
  196.2 2.0 fusion.55
  198.2 2.0 convolution_subtract_fusion
  200.4 0.9 copy-done.1
  201.4 26.7 %while.45 = (s32[]{:T(128)}, f32[8,128,128]{2,1,0:T(8,128)S(1)}, f32[8,128,128]{2,1,0:T(8,128)S(1)}, f32[8,128,128]{2,1,0:T(8,128)S(1)}, s32[]{:T(128)}, /*index=5*/s32[]{:T(128)}) while((s32[]{:T(128)}, f32[8,128,128]{2,1,0:T(8,128)S(1)}, f32[8,128,128]{2,1,0:T(8,128)S(1)}, f32[8,128,128]{2,1,0:T(8,128)S(1)}, s32[]{:T(128)}, ...), condition=%wide.region_17.18_spmd.clone, body=%wide.region_16.17_spmd.clone.sunk | while | flops 201850880 | bytes 3670135 | solution.py:213
  202.0 3.4 %collective-permute-start.1 = (bf16[8,128,128]{2,1,0:T(8,128)(2,1)S(1)}, bf16[8,128,128]{2,1,0:T(8,128)(2,1)S(1)}, u32[]{:S(2)}, u32[]{:S(2)}) collective-permute-start(bf16[8,128,128]{2,1,0:T(8,128)(2,1)S(1)} %fusion.105), channel_id=1, source_target_pairs={{0,4},{4,8},{8,12},{1,5},{5,9},{9,13},{2,6},{6,10},{10,14},{3,7},{... | collective-permute-start | bytes 786440 | tf_op jit(solution)/shard_map/while/body/eval_jaxpr/ppermute | solution.py:21
  205.4 4.6 %collective-permute-done.1 = bf16[8,128,128]{2,1,0:T(8,128)(2,1)S(1)} collective-permute-done((bf16[8,128,128]{2,1,0:T(8,128)(2,1)S(1)}, bf16[8,128,128]{2,1,0:T(8,128)(2,1)S(1)}, u32[]{:S(2)}, u32[]{:S(2)}) %collective-permute-start.1) | collective-permute-done | bytes 262176 | tf_op jit(solution)/shard_map/while/body/eval_jaxpr/ppermute | solution.py:21
  210.8 4.4 %collective-permute-start.1 = (bf16[8,128,128]{2,1,0:T(8,128)(2,1)S(1)}, bf16[8,128,128]{2,1,0:T(8,128)(2,1)S(1)}, u32[]{:S(2)}, u32[]{:S(2)}) collective-permute-start(bf16[8,128,128]{2,1,0:T(8,128)(2,1)S(1)} %fusion.105), channel_id=1, source_target_pairs={{0,4},{4,8},{8,12},{1,5},{5,9},{9,13},{2,6},{6,10},{10,14},{3,7},{... | collective-permute-start | bytes 786440 | tf_op jit(solution)/shard_map/while/body/eval_jaxpr/ppermute | solution.py:21
  215.2 3.9 %collective-permute-done.1 = bf16[8,128,128]{2,1,0:T(8,128)(2,1)S(1)} collective-permute-done((bf16[8,128,128]{2,1,0:T(8,128)(2,1)S(1)}, bf16[8,128,128]{2,1,0:T(8,128)(2,1)S(1)}, u32[]{:S(2)}, u32[]{:S(2)}) %collective-permute-start.1) | collective-permute-done | bytes 262176 | tf_op jit(solution)/shard_map/while/body/eval_jaxpr/ppermute | solution.py:21
  219.7 4.4 %collective-permute-start.1 = (bf16[8,128,128]{2,1,0:T(8,128)(2,1)S(1)}, bf16[8,128,128]{2,1,0:T(8,128)(2,1)S(1)}, u32[]{:S(2)}, u32[]{:S(2)}) collective-permute-start(bf16[8,128,128]{2,1,0:T(8,128)(2,1)S(1)} %fusion.105), channel_id=1, source_target_pairs={{0,4},{4,8},{8,12},{1,5},{5,9},{9,13},{2,6},{6,10},{10,14},{3,7},{... | collective-permute-start | bytes 786440 | tf_op jit(solution)/shard_map/while/body/eval_jaxpr/ppermute | solution.py:21
  224.1 3.9 %collective-permute-done.1 = bf16[8,128,128]{2,1,0:T(8,128)(2,1)S(1)} collective-permute-done((bf16[8,128,128]{2,1,0:T(8,128)(2,1)S(1)}, bf16[8,128,128]{2,1,0:T(8,128)(2,1)S(1)}, u32[]{:S(2)}, u32[]{:S(2)}) %collective-permute-start.1) | collective-permute-done | bytes 262176 | tf_op jit(solution)/shard_map/while/body/eval_jaxpr/ppermute | solution.py:21
  228.0 1.9 broadcast_select_fusion
  229.9 28.9 %while.43 = (s32[]{:T(128)}, f32[8,128,128]{2,1,0:T(8,128)S(1)}, pred[]{:T(512)}, f32[8,128,128]{2,1,0:T(8,128)S(1)}, f32[8,128,128]{2,1,0:T(8,128)S(1)}, /*index=5*/f32[8,128,128]{2,1,0:T(8,128)S(1)}, s32[]{:T(128)}) while((s32[]{:T(128)}, f32[8,128,128]{2,1,0:T(8,128)S(1)}, pred[]{:T(512)}, f32[8,128,128]{2,1,0:T(8,128)S(1)}, ...), condition=%wide.region_19.20_spmd, body=%wide.region_18.19_spmd.sunk | while | flops 201850880 | bytes 4194422 | solution.py:223
  230.6 1.3 collective-permute-start
  231.9 7.4 %collective-permute-done = bf16[8,128,128]{2,1,0:T(8,128)(2,1)S(1)} collective-permute-done((bf16[8,128,128]{2,1,0:T(8,128)(2,1)S(1)}, bf16[8,128,128]{2,1,0:T(8,128)(2,1)S(1)}, u32[]{:S(2)}, u32[]{:S(2)}) %collective-permute-start) | collective-permute-done | bytes 262176 | tf_op jit(solution)/shard_map/while/body/eval_jaxpr/ppermute | solution.py:21
  240.0 1.3 collective-permute-start
  241.3 8.1 %collective-permute-done = bf16[8,128,128]{2,1,0:T(8,128)(2,1)S(1)} collective-permute-done((bf16[8,128,128]{2,1,0:T(8,128)(2,1)S(1)}, bf16[8,128,128]{2,1,0:T(8,128)(2,1)S(1)}, u32[]{:S(2)}, u32[]{:S(2)}) %collective-permute-start) | collective-permute-done | bytes 262176 | tf_op jit(solution)/shard_map/while/body/eval_jaxpr/ppermute | solution.py:21
  250.2 1.3 collective-permute-start
  251.5 7.2 %collective-permute-done = bf16[8,128,128]{2,1,0:T(8,128)(2,1)S(1)} collective-permute-done((bf16[8,128,128]{2,1,0:T(8,128)(2,1)S(1)}, bf16[8,128,128]{2,1,0:T(8,128)(2,1)S(1)}, u32[]{:S(2)}, u32[]{:S(2)}) %collective-permute-start) | collective-permute-done | bytes 262176 | tf_op jit(solution)/shard_map/while/body/eval_jaxpr/ppermute | solution.py:21
  258.8 2.4 multiply_reduce_fusion.1
  261.8 0.9 fusion.50
  262.7 1.6 dynamic-slice_convert_fusion
  (109 shorter events, 17.5 us)
Async XLA Ops:
  7.2 99.6 %copy-start = (bf16[2048,8]{0,1:T(8,128)(2,1)S(1)}, bf16[2048,8]{0,1:T(8,128)(2,1)}, u32[]{:S(2)}) copy-start(bf16[2048,8]{0,1:T(8,128)(2,1)} %param.26) | copy-start | bytes 98308
  7.2 89.5 %all-reduce.2.cloned.1.call-start = ((), (), s32[]{:S(2)}) async-start(), calls=%async_computation | async-start | bytes 1048576 | tf_op jit(solution)/shard_map/psum | solution.py:181
  42.0 14.5 %copy-start.4 = (bf16[128,512]{1,0:T(8,128)(2,1)S(1)}, bf16[128,512]{1,0:T(8,128)(2,1)}, u32[]{:S(2)}) copy-start(bf16[128,512]{1,0:T(8,128)(2,1)} %param.22) | copy-start | bytes 393220
  53.2 5.4 %copy-start.6 = (f32[128,8]{0,1:T(8,128)S(1)}, f32[128,8]{0,1:T(8,128)}, u32[]{:S(2)}) copy-start(f32[128,8]{0,1:T(8,128)} %param.27) | copy-start | bytes 12292
  53.2 6.4 %copy-start.7 = (f32[128]{0:T(128)S(1)}, f32[128]{0:T(128)}, u32[]{:S(2)}) copy-start(f32[128]{0:T(128)} %param.28) | copy-start | bytes 1540
  53.2 44.7 %copy-start.5 = (f32[2048]{0:T(1024)S(1)}, f32[2048]{0:T(1024)}, u32[]{:S(2)}) copy-start(f32[2048]{0:T(1024)} %param.24) | copy-start | bytes 24580
  98.0 8.8 %copy-start.3 = (bf16[128,2048]{1,0:T(8,128)(2,1)S(1)}, bf16[128,2048]{1,0:T(8,128)(2,1)}, u32[]{:S(2)}) copy-start(bf16[128,2048]{1,0:T(8,128)(2,1)} %all-reduce.2.cloned.1.call-done) | copy-start | bytes 1572868
  198.2 3.1 %copy-start.2 = (f32[16,128,128]{2,1,0:T(8,128)}, f32[16,128,128]{2,1,0:T(8,128)S(1)}, u32[]{:S(2)}) copy-start(f32[16,128,128]{2,1,0:T(8,128)S(1)} %fusion.55) | copy-start | bytes 3145732
  200.2 1.0 copy-start.1
  202.0 8.0 %collective-permute-start.1 = (bf16[8,128,128]{2,1,0:T(8,128)(2,1)S(1)}, bf16[8,128,128]{2,1,0:T(8,128)(2,1)S(1)}, u32[]{:S(2)}, u32[]{:S(2)}) collective-permute-start(bf16[8,128,128]{2,1,0:T(8,128)(2,1)S(1)} %fusion.105), channel_id=1, source_target_pairs={{0,4},{4,8},{8,12},{1,5},{5,9},{9,13},{2,6},{6,10},{10,14},{3,7},{... | collective-permute-start | bytes 786440 | tf_op jit(solution)/shard_map/while/body/eval_jaxpr/ppermute | solution.py:21
  210.8 8.3 %collective-permute-start.1 = (bf16[8,128,128]{2,1,0:T(8,128)(2,1)S(1)}, bf16[8,128,128]{2,1,0:T(8,128)(2,1)S(1)}, u32[]{:S(2)}, u32[]{:S(2)}) collective-permute-start(bf16[8,128,128]{2,1,0:T(8,128)(2,1)S(1)} %fusion.105), channel_id=1, source_target_pairs={{0,4},{4,8},{8,12},{1,5},{5,9},{9,13},{2,6},{6,10},{10,14},{3,7},{... | collective-permute-start | bytes 786440 | tf_op jit(solution)/shard_map/while/body/eval_jaxpr/ppermute | solution.py:21
  219.7 8.3 %collective-permute-start.1 = (bf16[8,128,128]{2,1,0:T(8,128)(2,1)S(1)}, bf16[8,128,128]{2,1,0:T(8,128)(2,1)S(1)}, u32[]{:S(2)}, u32[]{:S(2)}) collective-permute-start(bf16[8,128,128]{2,1,0:T(8,128)(2,1)S(1)} %fusion.105), channel_id=1, source_target_pairs={{0,4},{4,8},{8,12},{1,5},{5,9},{9,13},{2,6},{6,10},{10,14},{3,7},{... | collective-permute-start | bytes 786440 | tf_op jit(solution)/shard_map/while/body/eval_jaxpr/ppermute | solution.py:21
  230.6 8.7 %collective-permute-start = (bf16[8,128,128]{2,1,0:T(8,128)(2,1)S(1)}, bf16[8,128,128]{2,1,0:T(8,128)(2,1)S(1)}, u32[]{:S(2)}, u32[]{:S(2)}) collective-permute-start(bf16[8,128,128]{2,1,0:T(8,128)(2,1)S(1)} %fusion.102), channel_id=1, source_target_pairs={{4,0},{8,4},{12,8},{5,1},{9,5},{13,9},{6,2},{10,6},{14,10},{7,3},{... | collective-permute-start | bytes 786440 | tf_op jit(solution)/shard_map/while/body/eval_jaxpr/ppermute | solution.py:21
  240.0 9.4 %collective-permute-start = (bf16[8,128,128]{2,1,0:T(8,128)(2,1)S(1)}, bf16[8,128,128]{2,1,0:T(8,128)(2,1)S(1)}, u32[]{:S(2)}, u32[]{:S(2)}) collective-permute-start(bf16[8,128,128]{2,1,0:T(8,128)(2,1)S(1)} %fusion.102), channel_id=1, source_target_pairs={{4,0},{8,4},{12,8},{5,1},{9,5},{13,9},{6,2},{10,6},{14,10},{7,3},{... | collective-permute-start | bytes 786440 | tf_op jit(solution)/shard_map/while/body/eval_jaxpr/ppermute | solution.py:21
  250.2 8.5 %collective-permute-start = (bf16[8,128,128]{2,1,0:T(8,128)(2,1)S(1)}, bf16[8,128,128]{2,1,0:T(8,128)(2,1)S(1)}, u32[]{:S(2)}, u32[]{:S(2)}) collective-permute-start(bf16[8,128,128]{2,1,0:T(8,128)(2,1)S(1)} %fusion.102), channel_id=1, source_target_pairs={{4,0},{8,4},{12,8},{5,1},{9,5},{13,9},{6,2},{10,6},{14,10},{7,3},{... | collective-permute-start | bytes 786440 | tf_op jit(solution)/shard_map/while/body/eval_jaxpr/ppermute | solution.py:21
Sparse Core Ops, SparseCore 0:
  57.5 39.1 all-reduce.1
where the time goes:
time: 272 us; the launch traced here: 271 us
  other arithmetic  92 us (34%)
  waiting for transfers between devices  72 us (26%)
  matrix products  34 us (12%)
  blocking collectives  30.2 us (11%)
  starting transfers between devices  16.1 us (6%)
  between operations  14.5 us (5%)
  local copies, waits for them, and re-layouts  11.8 us (4%)
    another operation x3, other arithmetic, block_terms(): jax.scipy.linalg.solve_triangular(system, right_side, lower=True, unit_di...  80.6 us
    psum x1, waiting for transfers between devices, local(): lax.psum(partial_term.astype(jnp.bfloat16), ('head', 'sub'))  36.8 us
    ppermute x6, waiting for transfers between devices, passed_along(): lax.ppermute(value, axis, [(source, source + steps) for source in range(i...  35.1 us
    ppermute x6, starting transfers between devices, passed_along(): lax.ppermute(value, axis, [(source, source + steps) for source in range(i...  16.1 us
    all_gather x1, blocking collectives, local(): key_block = lax.all_gather(key_local, 'ctx', axis=0, tiled=True)  15.6 us
    all_gather x1, blocking collectives, local(): value_block = lax.all_gather(value_local, 'ctx', axis=0, tiled=True)  14.6 us
    dot_general x1, matrix products, local(): mixed_cols = jnp.dot(normed, in_weight, preferred_element_type=jnp.float32)  7.08 us
    dot_general x7, matrix products, apply_map(): jnp.einsum('hij,hjk->hik', matrix_maps, states, precision=TOP_PRECISION)  5.74 us
  transfers between devices with their start and end apart: 7, of which 7 were waited for; matrix products, arithmetic and copies ran while one was open for 1% of the time, Pallas kernels for 0%

commit v1 on v0

--- a/solution.py
+++ b/solution.py
@@ -1,6 +1,10 @@
+import functools
+
 import jax
 import jax.numpy as jnp
 from jax import lax
+from jax.experimental import pallas as pl
+from jax.experimental.pallas import tpu as pltpu
 from jax.sharding import PartitionSpec as P
 
 HEADS = 16
@@ -100,7 +104,7 @@
     return (new_max, run_sum, run_acc)
 
 
-def local(
+def hop_local(
     att_query,
     att_gate,
     att_kv,
@@ -234,7 +238,370 @@
     return (new_residual, delta_out.reshape(rows_here, value_here * DV))
 
 
+KEY_HEADS = 16
+IN_VMEM = pl.BlockSpec(memory_space=pltpu.VMEM)
+IN_HBM = pl.BlockSpec(memory_space=pl.ANY)
+MIB = 2**20
+LANES = 128
+
+
+def owners_fit(mesh):
+    shards = mesh.shape["head"] * mesh.shape["sub"]
+    key_here = KEY_HEADS // shards
+    return mesh.shape["head"] == 2 and mesh.shape["sub"] == 2 and key_here == mesh.shape["ctx"]
+
+
+def in_vmem(array):
+    return pltpu.with_memory_space_constraint(array, pltpu.VMEM)
+
+
+def in_hbm(array):
+    return pltpu.with_memory_space_constraint(array, pltpu.HBM)
+
+
+def vmem_call(kernel, outs, operands, scratch=(), limit=16, aliases=None, last=False, cost=None):
+    make = jax.ShapeDtypeStruct if last else pltpu.VMEM
+    return pl.pallas_call(
+        kernel,
+        out_shape=[make(shape, dtype) for shape, dtype in outs],
+        in_specs=[IN_VMEM] * len(operands),
+        out_specs=[IN_VMEM] * len(outs),
+        scratch_shapes=list(scratch),
+        input_output_aliases=aliases or {},
+        cost_estimate=cost,
+        compiler_params=pltpu.CompilerParams(vmem_limit_bytes=limit * MIB),
+    )(*[in_vmem(operand) for operand in operands])
+
+
+def rotated(value, axis, steps):
+    count = lax.axis_size(axis)
+    return lax.ppermute(value, axis, [(i, (i + steps) % count) for i in range(count)])
+
+
+def dot(left, right, dims=((1,), (0,))):
+    return lax.dot_general(left, right, (dims, ((), ())), preferred_element_type=jnp.float32)
+
+
+def halves(value):
+    high = value.astype(jnp.bfloat16)
+    return high, (value - high.astype(jnp.float32)).astype(jnp.bfloat16)
+
+
+def dot3(left, right):
+    left_high, left_low = halves(left)
+    right_high, right_low = halves(right)
+    return dot(left_high, right_high) + (dot(left_high, right_low) + dot(left_low, right_high))
+
+
+def sigmoid(value):
+    return 1.0 / (1.0 + jnp.exp(-value))
+
+
+def silu(value):
+    return value / (1.0 + jnp.exp(-value))
+
+
+def piece_kernel(kv_ref, piece_ref, own_ref, sems):
+    start = pl.multiple_of(lax.axis_index("head") * 2 * HD, 2 * HD)
+    share = pl.multiple_of(start + lax.axis_index("sub") * HD, HD)
+    first = pltpu.make_async_copy(kv_ref.at[:, pl.ds(share, HD)], piece_ref, sems.at[0])
+    second = pltpu.make_async_copy(kv_ref.at[:, pl.ds(start, 2 * HD)], own_ref, sems.at[1])
+    first.start()
+    second.start()
+    first.wait()
+    second.wait()
+
+
+def attention_kernel(
+    query_ref, gate_ref, own_ref, mine1, mine2, mine3, twin1, twin2, twin3, weight_ref, residual_ref,
+    keep_ref, send_ref, keys, values, heads, partial,
+):
+    rows, head_columns = query_ref.shape
+    half = rows // 2
+    ctx_rank, head_rank, sub_rank = (lax.axis_index(name) for name in ("ctx", "head", "sub"))
+    count = 4
+    keys[0:rows] = own_ref[:, 0:HD]
+    values[0:rows] = own_ref[:, HD : 2 * HD]
+
+    @pl.when(sub_rank == 0)
+    def _():
+        for step, (mine, twin) in enumerate(((mine1, twin1), (mine2, twin2), (mine3, twin3)), 1):
+            keys[step * rows : (step + 1) * rows] = mine[...]
+            values[step * rows : (step + 1) * rows] = twin[...]
+
+    @pl.when(sub_rank != 0)
+    def _():
+        for step, (mine, twin) in enumerate(((mine1, twin1), (mine2, twin2), (mine3, twin3)), 1):
+            keys[step * rows : (step + 1) * rows] = twin[...]
+            values[step * rows : (step + 1) * rows] = mine[...]
+
+    def places(row, device):
+        within = row % rows
+        block = jnp.where(within < half, device, 2 * count - 1 - device)
+        return block * half + within % half
+
+    query_place = places(lax.broadcasted_iota(jnp.int32, (rows, 1), 0), ctx_rank)
+    key_row = lax.broadcasted_iota(jnp.int32, (1, count * rows), 1)
+    key_place = places(key_row, (ctx_rank - key_row // rows + count) % count)
+    visible = query_place >= key_place
+    for head in range(head_columns // HD):
+        columns = slice(head * HD, (head + 1) * HD)
+        scores = dot(query_ref[:, columns], keys[...], ((1,), (1,))) * HD ** (-0.5)
+        scores = jnp.where(visible, scores, NEGATIVE)
+        weights = jnp.exp(scores - jnp.max(scores, axis=1, keepdims=True))
+        total = jnp.sum(weights, axis=1, keepdims=True)
+        gathered = dot(weights.astype(jnp.bfloat16), values[...])
+        gate = sigmoid(gate_ref[:, columns].astype(jnp.float32))
+        heads[:, columns] = (gathered / total * gate).astype(jnp.bfloat16)
+    partial[...] = dot(heads[...], weight_ref[...])
+    width = residual_ref.shape[1]
+    mid = partial.shape[1] // 2
+    own_columns = pl.ds(pl.multiple_of((head_rank * 2 + sub_rank) * width, width), width)
+    partial[:, own_columns] += residual_ref[...].astype(jnp.float32)
+    keep_ref[...] = partial[:, pl.ds(pl.multiple_of(sub_rank * mid, mid), mid)]
+    send_ref[...] = partial[:, pl.ds(pl.multiple_of((1 - sub_rank) * mid, mid), mid)].astype(jnp.bfloat16)
+
+
+def chip_sum_kernel(keep_ref, came_ref, sum_ref, send_ref):
+    total = keep_ref[...] + came_ref[...].astype(jnp.float32)
+    sum_ref[...] = total
+    send_ref[...] = total.astype(jnp.bfloat16)
+
+
+def hidden_kernel(keep_ref, came_ref, hidden_ref):
+    hidden_ref[...] = (keep_ref[...] + came_ref[...].astype(jnp.float32)).astype(jnp.bfloat16)
+
+
+def norm_kernel(own_ref, twin_ref, gain_ref, beta_ref, decay_ref, residual_ref, normed_ref, extra_ref):
+    head_rank, sub_rank = lax.axis_index("head"), lax.axis_index("sub")
+    mid = own_ref.shape[1]
+    width = residual_ref.shape[1]
+    columns = pl.ds(pl.multiple_of(sub_rank * width, width), width)
+
+    @pl.when(sub_rank == head_rank)
+    def _():
+        residual_ref[...] = own_ref[:, columns]
+
+    @pl.when(sub_rank != head_rank)
+    def _():
+        residual_ref[...] = twin_ref[:, columns]
+
+    own, twin = own_ref[...].astype(jnp.float32), twin_ref[...].astype(jnp.float32)
+    squares = jnp.sum(own * own, axis=1, keepdims=True) + jnp.sum(twin * twin, axis=1, keepdims=True)
+    scale = lax.rsqrt(squares / (2 * mid) + EPSILON)
+    own_half = pl.ds(pl.multiple_of(sub_rank * mid, mid), mid)
+    twin_half = pl.ds(pl.multiple_of((1 - sub_rank) * mid, mid), mid)
+    normed_ref[:, own_half] = (own * scale * gain_ref[:, own_half]).astype(jnp.bfloat16)
+    normed_ref[:, twin_half] = (twin * scale * gain_ref[:, twin_half]).astype(jnp.bfloat16)
+    values = decay_ref.shape[0]
+    extra_ref[0:values] = decay_ref[...]
+    extra_ref[values : 2 * values] = sigmoid(dot(beta_ref[...], normed_ref[...], ((1,), (1,))))
+
+
+def payload_kernel(step, normed_ref, weight_ref, extra_ref, payload_ref, small):
+    rows = normed_ref.shape[0]
+    group = 2 * DK + 2 * DV
+    count = 4
+    target = (lax.axis_index("ctx") + step) % count
+    columns = pl.ds(pl.multiple_of(target * group, group), group)
+    mixed = silu(dot(normed_ref[...], weight_ref[:, columns]))
+    query, key = mixed[:, :DK], mixed[:, DK : 2 * DK]
+    payload_ref[0:rows] = (unit_rows(query) * DK ** (-0.5)).astype(jnp.bfloat16)
+    payload_ref[rows : 2 * rows] = unit_rows(key).astype(jnp.bfloat16)
+    payload_ref[2 * rows : 3 * rows] = mixed[:, 2 * DK : 2 * DK + DV].astype(jnp.bfloat16)
+    payload_ref[3 * rows : 4 * rows] = mixed[:, 2 * DK + DV :].astype(jnp.bfloat16)
+    values = extra_ref.shape[0] // 2
+    small[...] = jnp.zeros_like(small)
+    for place, base in ((0, 0), (4, values)):
+        full = extra_ref[pl.ds(base + 2 * target, 2), :]
+        high = full.astype(jnp.bfloat16).astype(jnp.float32)
+        small[place : place + 2] = high
+        small[place + 2 : place + 4] = full - high
+    payload_ref[4 * rows : 4 * rows + 16] = small[...].astype(jnp.bfloat16)
+
+
+def unit_lower_inverse(strict, row, column):
+    same = lambda size: (row // size) == (column // size)
+    small = jnp.where(same(8), strict, 0.0)
+    second = dot3(small, small)
+    start = jnp.where(row == column, 1.0, 0.0) - small
+    start = start + dot3(start, second)
+    inverse = start + dot3(start, dot3(second, second))
+    for size in (8, 16, 32):
+        corner = jnp.where(same(2 * size) & jnp.logical_not(same(size)), strict, 0.0)
+        inverse = inverse - dot3(inverse, dot3(corner, inverse))
+    return inverse
+
+
+def block_kernel(step, payload_ref, *refs):
+    offset_ref, linear_ref, local_ref, growth_ref = refs[-4:]
+    count = 4
+    source = (lax.axis_index("ctx") + count - step) % count
+    rows = (payload_ref.shape[0] - 16) // 4
+    half = rows // 2
+    query, key = payload_ref[0:rows], payload_ref[rows : 2 * rows]
+    extra = payload_ref[4 * rows : 4 * rows + 16]
+    row = lax.broadcasted_iota(jnp.int32, (rows, rows), 0)
+    column = lax.broadcasted_iota(jnp.int32, (rows, rows), 1)
+    together = (row // half) == (column // half)
+    inclusive = together & (row >= column)
+    strictly = together & (row > column)
+    below = jnp.where(inclusive, 1.0, 0.0).astype(jnp.bfloat16)
+    diagonal = jnp.where(row == column, 1.0, 0.0).astype(jnp.bfloat16)
+    sums_row = dot(extra, below, ((1,), (1,)))
+    sums_column = dot(below, extra, ((1,), (1,)))
+    plain_column = dot(diagonal, extra, ((1,), (1,)))
+    key_wide = key.astype(jnp.float32)
+    key_turned = jnp.transpose(key_wide)
+    key_gram = dot(key, key, ((1,), (1,)))
+    query_gram = dot(query, key, ((1,), (1,)))
+    early_lane = lax.broadcasted_iota(jnp.int32, (1, rows), 1) < half
+    for head in range(2):
+        total_row = sums_row[head : head + 1] + sums_row[head + 2 : head + 3]
+        total = sums_column[:, head : head + 1] + sums_column[:, head + 2 : head + 3]
+        beta = plain_column[:, head + 4 : head + 5] + plain_column[:, head + 6 : head + 7]
+        decay = jnp.exp(jnp.where(inclusive, total - total_row, NEGATIVE))
+        strict = jnp.where(strictly, beta * key_gram * decay, 0.0)
+        inverse_high, inverse_low = halves(unit_lower_inverse(strict, row, column))
+        growth = jnp.exp(total)
+        value = payload_ref[(2 + head) * rows : (3 + head) * rows].astype(jnp.float32)
+        right = jnp.concatenate([beta * value, (beta * growth) * key_wide], axis=1).astype(jnp.bfloat16)
+        solved = (dot(inverse_high, right) + dot(inverse_low, right)).astype(jnp.bfloat16)
+        attended = dot((query_gram * decay).astype(jnp.bfloat16), solved)
+        local_ref[source, head] = attended[:, :DV]
+        reads = (growth * query.astype(jnp.float32) - attended[:, DV:]).astype(jnp.bfloat16)
+        end_row = jnp.where(early_lane, total_row[:, half - 1 : half], total_row[:, rows - 1 : rows])
+        carried = key_turned * jnp.exp(end_row - total_row)
+        ends = jnp.exp(end_row)
+        for block in range(2):
+            inside = early_lane if block == 0 else jnp.logical_not(early_lane)
+            moved = dot(jnp.where(inside, carried, 0.0).astype(jnp.bfloat16), solved)
+            offset_ref[source, head, block] = moved[:, :DV]
+            linear_ref[source, head, block, 0:DK] = moved[:, DV:].astype(jnp.bfloat16)
+            linear_ref[source, head, block, DK : DK + half] = reads[block * half : (block + 1) * half]
+            last = (block + 1) * half - 1
+            growth_ref[source, head, block] = jnp.broadcast_to(ends[:, last : last + 1], growth_ref.shape[3:])
+
+
+def scan_kernel(offset_ref, linear_ref, local_ref, growth_ref, gain_ref, own_ref, back1, back2, back3, outs):
+    count = offset_ref.shape[0]
+    half = local_ref.shape[2] // 2
+    rank = lax.axis_index("ctx")
+    states = [None, None]
+    for number in range(2 * count):
+        source, block = (number, 0) if number < count else (2 * count - 1 - number, 1)
+        block_rows = slice(block * half, (block + 1) * half)
+        for head in range(2):
+            out = local_ref[source, head, block_rows]
+            state = offset_ref[source, head, block]
+            if states[head] is not None:
+                moved = dot(linear_ref[source, head, block], states[head].astype(jnp.bfloat16))
+                out = out + moved[DK:]
+                state = state - moved[:DK] + growth_ref[source, head, block, 0:1] * states[head]
+            states[head] = state
+            scale = lax.rsqrt(jnp.mean(out * out, axis=1, keepdims=True) + EPSILON)
+            outs[source, block_rows, head * DV : (head + 1) * DV] = (out * scale * gain_ref[...]).astype(jnp.bfloat16)
+    own_ref[...] = outs[rank]
+    for step, back in enumerate((back1, back2, back3), 1):
+        back[...] = outs[(rank + count - step) % count]
+
+
+def place_kernel(own_ref, back1, back2, back3, out_ref):
+    count = 4
+    width = own_ref.shape[1]
+    rank = lax.axis_index("ctx")
+    for step, back in enumerate((own_ref, back1, back2, back3)):
+        columns = pl.ds(pl.multiple_of((rank + step) % count * width, width), width)
+        out_ref[:, columns] = back[...]
+
+
+def owner_local(
+    att_query,
+    att_gate,
+    att_kv,
+    residual,
+    out_weight,
+    norm_gain,
+    in_weight,
+    beta_weight,
+    log_decay,
+    delta_gain,
+):
+    bf16, f32 = jnp.bfloat16, jnp.float32
+    rows, head_columns = att_query.shape
+    model = out_weight.shape[1]
+    half_model = model // 2
+    steps = (1, 2, 3)
+    piece, own_kv = pl.pallas_call(
+        piece_kernel,
+        out_shape=[pltpu.VMEM((rows, HD), bf16), pltpu.VMEM((rows, 2 * HD), bf16)],
+        in_specs=[IN_HBM],
+        out_specs=[IN_VMEM] * 2,
+        scratch_shapes=[pltpu.SemaphoreType.DMA((2,))],
+    )(in_hbm(att_kv))
+    mine = [rotated(piece, "ctx", step) for step in steps]
+    twin = [rotated(part, "sub", 1) for part in mine]
+    keep, send = vmem_call(
+        attention_kernel,
+        [((rows, half_model), f32), ((rows, half_model), bf16)],
+        [att_query, att_gate, own_kv, *mine, *twin, out_weight, residual],
+        [
+            pltpu.VMEM((4 * rows, HD), bf16),
+            pltpu.VMEM((4 * rows, HD), bf16),
+            pltpu.VMEM((rows, head_columns), bf16),
+            pltpu.VMEM((rows, model), f32),
+        ],
+    )
+    chip_sum, send = vmem_call(
+        chip_sum_kernel,
+        [((rows, half_model), f32), ((rows, half_model), bf16)],
+        [keep, rotated(send, "sub", 1)],
+    )
+    hidden = vmem_call(hidden_kernel, [((rows, half_model), bf16)], [chip_sum, rotated(send, "head", 1)])[0]
+    value_here = log_decay.shape[1]
+    new_residual, normed, extra = vmem_call(
+        norm_kernel,
+        [(residual.shape, bf16), ((rows, model), bf16), ((2 * value_here, rows), f32)],
+        [hidden, rotated(hidden, "sub", 1), norm_gain[None, :], beta_weight.T, log_decay.T],
+    )
+    payloads = [
+        vmem_call(
+            functools.partial(payload_kernel, step),
+            [((4 * rows + 16, LANES), bf16)],
+            [normed, in_weight, extra],
+            [pltpu.VMEM((16, LANES), f32)],
+        )[0]
+        for step in range(4)
+    ]
+    came = [payloads[0]] + [rotated(payloads[step], "ctx", step) for step in steps]
+    half = rows // 2
+    terms_shapes = [
+        ((4, 2, 2, DK, DV), f32),
+        ((4, 2, 2, DK + half, DK), bf16),
+        ((4, 2, rows, DV), f32),
+        ((4, 2, 2, 8, LANES), f32),
+    ]
+    terms = []
+    for step in range(4):
+        terms = vmem_call(
+            functools.partial(block_kernel, step),
+            terms_shapes,
+            [came[step], *terms],
+            aliases={1 + i: i for i in range(4)} if terms else None,
+        )
+    own, *backs = vmem_call(
+        scan_kernel,
+        [((rows, 2 * DV), bf16)] * 4,
+        [*terms, delta_gain[None, :]],
+        [pltpu.VMEM((4, rows, 2 * DV), bf16)],
+    )
+    backs = [rotated(back, "ctx", -step) for step, back in zip(steps, backs)]
+    delta_out = vmem_call(place_kernel, [((rows, value_here * DV), bf16)], [own, *backs], last=True)[0]
+    return (new_residual, delta_out)
+
+
 def solution(mesh):
+    local = owner_local if owners_fit(mesh) else hop_local
     return jax.shard_map(
         local,
         mesh=mesh,

time: 272 us -> 74.7 us (0.27)
  other arithmetic: 92 us -> 0 us
  waiting for transfers between devices: 72 us -> 20 us
  matrix products: 34 us -> 0 us
  blocking collectives: 30.2 us -> 0 us
  Pallas kernels: 0 us -> 24.3 us
  between operations: 14.5 us -> 0.79 us
    another operation x4 -> x0, other arithmetic: 80.9 us -> none  [the longest x3 80.6 us: block_terms(): jax.scipy.linalg.solve_triangular(system, right_side, lower=True, unit_di...]
    psum x1 -> x0, waiting for transfers between devices: 36.8 us -> none  [local(): lax.psum(partial_term.astype(jnp.bfloat16), ('head', 'sub'))]
    dot_general x25 -> x0, matrix products: 31.7 us -> none  [the longest x1 7.08 us: local(): mixed_cols = jnp.dot(normed, in_weight, preferred_element_type=jnp.float32)]
    all_gather x2 -> x0, blocking collectives: 30.2 us -> none  [the longest x1 15.6 us: local(): key_block = lax.all_gather(key_local, 'ctx', axis=0, tiled=True)]
    pallas_call x0 -> x15, Pallas kernels: none -> 24.3 us  [the longest x14 23.3 us: vmem_call(): pl.pallas_call(kernel, out_shape=[make(shape, dtype) for shape, dtype in...]
    ppermute x6 -> x15, waiting for transfers between devices: 35.1 us -> 20 us  [rotated(): lax.ppermute(value, axis, [(i, (i + steps) % count) for i in range(count)])]
    unnamed x21 -> x19, local copies, waits for them, and re-layouts: 3.6 us -> 11.2 us
    while x5 -> x0, local copies, waits for them, and re-layouts: 2.93 us -> none
  transfers between devices with their start and end apart: 7 -> 15, of which waited for: 7 -> 8; matrix products, arithmetic and copies ran while one was open for 1% -> 1% of each run, Pallas kernels for 0% -> 19%
where the time goes in v1:
time: 74.7 us; the launch traced here: 74.2 us
  Pallas kernels  24.3 us (33%)
  waiting for transfers between devices  20 us (27%)
  starting transfers between devices  18 us (24%)
  local copies, waits for them, and re-layouts  11.2 us (15%)
  between operations  0.79 us (1%)
    pallas_call x14, Pallas kernels, vmem_call(): pl.pallas_call(kernel, out_shape=[make(shape, dtype) for shape, dtype in...  23.3 us
    ppermute x15, waiting for transfers between devices, rotated(): lax.ppermute(value, axis, [(i, (i + steps) % count) for i in range(count)])  20 us
    ppermute x15, starting transfers between devices, rotated(): lax.ppermute(value, axis, [(i, (i + steps) % count) for i in range(count)])  18 us
    unnamed x19, local copies, waits for them, and re-layouts  11.2 us
  transfers between devices with their start and end apart: 15, of which 8 were waited for; matrix products, arithmetic and copies ran while one was open for 1% of the time, Pallas kernels for 19%

profile of v1, /device:TPU:0, one launch (start us, length us, event | category | flops | bytes accessed | tf_op | source)
XLA Modules:
  0.0 74.2 jit_solution(129083182872230308)
XLA Ops:
  0.6 1.0 %shard_map.113 = (bf16[128,256]{1,0:T(8,128)(2,1)S(1)}, bf16[128,512]{1,0:T(8,128)(2,1)S(1)}) custom-call(bf16[128,1024]{1,0:T(8,128)(2,1)} %kv_ref.1), custom_call_target="tpu_custom_call" | custom-call | tf_op jit(solution)/shard_map/pallas_call | solution.py:535
  1.7 5.1 %collective-permute-start.2 = (bf16[128,256]{1,0:T(8,128)(2,1)S(1)}, bf16[128,256]{1,0:T(8,128)(2,1)S(1)}, u32[]{:S(2)}, u32[]{:S(2)}) collective-permute-start(bf16[128,256]{1,0:T(8,128)(2,1)S(1)} %get-tuple-element.32), channel_id=1, source_target_pairs={{0,12},{4,0},{8,4},{12,8},{1,13},{5,1},{9,5},{13,9},{2,14},{6,2},{... | collective-permute-start | bytes 196616 | tf_op jit(solution)/shard_map/ppermute | solution.py:278
  6.8 0.0 collective-permute-start.1
  6.8 1.0 %collective-permute-start = (bf16[128,256]{1,0:T(8,128)(2,1)S(1)}, bf16[128,256]{1,0:T(8,128)(2,1)S(1)}, u32[]{:S(2)}, u32[]{:S(2)}) collective-permute-start(bf16[128,256]{1,0:T(8,128)(2,1)S(1)} %get-tuple-element.32), channel_id=1, source_target_pairs={{0,4},{4,8},{8,12},{12,0},{1,5},{5,9},{9,13},{13,1},{2,6},{6,10},{... | collective-permute-start | bytes 196616 | tf_op jit(solution)/shard_map/ppermute | solution.py:278
  7.8 1.5 %collective-permute-done.2.mine3 = bf16[128,256]{1,0:T(8,128)(2,1)S(1)} collective-permute-done((bf16[128,256]{1,0:T(8,128)(2,1)S(1)}, bf16[128,256]{1,0:T(8,128)(2,1)S(1)}, u32[]{:S(2)}, u32[]{:S(2)}) %collective-permute-start.2) | collective-permute-done | bytes 65568 | tf_op jit(solution)/shard_map/ppermute | solution.py:278
  9.3 4.0 %collective-permute-done.1.mine2 = bf16[128,256]{1,0:T(8,128)(2,1)S(1)} collective-permute-done((bf16[128,256]{1,0:T(8,128)(2,1)S(1)}, bf16[128,256]{1,0:T(8,128)(2,1)S(1)}, u32[]{:S(2)}, u32[]{:S(2)}) %collective-permute-start.1) | collective-permute-done | bytes 65568 | tf_op jit(solution)/shard_map/ppermute | solution.py:278
  13.2 0.0 collective-permute-start.4
  13.2 0.5 collective-permute-start.3
  13.8 0.7 collective-permute-done.4.twin2
  14.5 0.2 collective-permute-done.3.twin1
  14.7 2.2 %copy-done.1 = bf16[1024,2048]{1,0:T(8,128)(2,1)S(1)} copy-done((bf16[1024,2048]{1,0:T(8,128)(2,1)S(1)}, bf16[1024,2048]{1,0:T(8,128)(2,1)}, u32[]{:S(2)}) %copy-start.1) | copy-done | bytes 4194328
  16.8 0.9 %copy-done.2 = bf16[128,1024]{1,0:T(8,128)(2,1)S(1)} copy-done((bf16[128,1024]{1,0:T(8,128)(2,1)S(1)}, bf16[128,1024]{1,0:T(8,128)(2,1)}, u32[]{:S(2)}) %copy-start.2) | copy-done | bytes 262168
  17.8 0.9 %copy-done.3 = bf16[128,1024]{1,0:T(8,128)(2,1)S(1)} copy-done((bf16[128,1024]{1,0:T(8,128)(2,1)S(1)}, bf16[128,1024]{1,0:T(8,128)(2,1)}, u32[]{:S(2)}) %copy-start.3) | copy-done | bytes 262168
  18.7 0.9 %copy-done.4 = bf16[128,512]{1,0:T(8,128)(2,1)S(1)} copy-done((bf16[128,512]{1,0:T(8,128)(2,1)S(1)}, bf16[128,512]{1,0:T(8,128)(2,1)}, u32[]{:S(2)}) %copy-start.4) | copy-done | bytes 131096
  19.6 2.2 %shard_map.114 = (f32[128,1024]{1,0:T(8,128)S(1)}, bf16[128,1024]{1,0:T(8,128)(2,1)S(1)}) custom-call(bf16[128,1024]{1,0:T(8,128)(2,1)S(1)} %copy-done.2, bf16[128,1024]{1,0:T(8,128)(2,1)S(1)} %copy-done.3, bf16[128,512]{1,0:T(8,128)(2,1)S(1)} %get-tuple-element.31.own_ref, bf16[128,256]{1,0:T(8,128)(2,1)S(1)} %collective-permute-done.mine1, ...), custom_call_target="tpu_custom_call" | custom-call | tf_op jit(solution)/shard_map/pallas_call | solution.py:264
  21.8 0.4 collective-permute-start.6
  22.3 1.2 %collective-permute-done.6.came_ref = bf16[128,1024]{1,0:T(8,128)(2,1)S(1)} collective-permute-done((bf16[128,1024]{1,0:T(8,128)(2,1)S(1)}, bf16[128,1024]{1,0:T(8,128)(2,1)S(1)}, u32[]{:S(2)}, u32[]{:S(2)}) %collective-permute-start.6) | collective-permute-done | bytes 262176 | tf_op jit(solution)/shard_map/ppermute | solution.py:278
  23.5 0.1 shard_map.115
  23.5 1.6 %collective-permute-start.7 = (bf16[128,1024]{1,0:T(8,128)(2,1)S(1)}, bf16[128,1024]{1,0:T(8,128)(2,1)S(1)}, u32[]{:S(2)}, u32[]{:S(2)}) collective-permute-start(bf16[128,1024]{1,0:T(8,128)(2,1)S(1)} %get-tuple-element.36), channel_id=1, source_target_pairs={{0,2},{2,0},{1,3},{3,1},{4,6},{6,4},{5,7},{7,5},{8,10},{10,8},{9,1... | collective-permute-start | bytes 786440 | tf_op jit(solution)/shard_map/ppermute | solution.py:278
  25.1 7.1 %collective-permute-done.7.came_ref = bf16[128,1024]{1,0:T(8,128)(2,1)S(1)} collective-permute-done((bf16[128,1024]{1,0:T(8,128)(2,1)S(1)}, bf16[128,1024]{1,0:T(8,128)(2,1)S(1)}, u32[]{:S(2)}, u32[]{:S(2)}) %collective-permute-start.7) | collective-permute-done | bytes 262176 | tf_op jit(solution)/shard_map/ppermute | solution.py:278
  32.2 0.1 collective-permute-start.8
  32.3 1.5 %collective-permute-done.8.twin_ref = bf16[128,1024]{1,0:T(8,128)(2,1)S(1)} collective-permute-done((bf16[128,1024]{1,0:T(8,128)(2,1)S(1)}, bf16[128,1024]{1,0:T(8,128)(2,1)S(1)}, u32[]{:S(2)}, u32[]{:S(2)}) %collective-permute-start.8) | collective-permute-done | bytes 262176 | tf_op jit(solution)/shard_map/ppermute | solution.py:278
  33.8 0.8 %copy-done.5 = bf16[2048,8]{0,1:T(8,128)(2,1)S(1)} copy-done((bf16[2048,8]{0,1:T(8,128)(2,1)S(1)}, bf16[2048,8]{0,1:T(8,128)(2,1)}, u32[]{:S(2)}) %copy-start.5) | copy-done | bytes 32792
  34.6 0.7 copy-done.6
  35.3 0.7 copy-done.7
  36.0 0.5 shard_map.117
  36.4 3.4 %copy-done = bf16[2048,2048]{1,0:T(8,128)(2,1)S(1)} copy-done((bf16[2048,2048]{1,0:T(8,128)(2,1)S(1)}, bf16[2048,2048]{1,0:T(8,128)(2,1)}, u32[]{:S(2)}) %copy-start) | copy-done | bytes 8388632
  39.8 0.6 shard_map.120
  40.4 0.1 collective-permute-start.11
  40.5 0.6 shard_map.119
  41.1 2.5 %collective-permute-start.10 = (bf16[528,128]{1,0:T(8,128)(2,1)S(1)}, bf16[528,128]{1,0:T(8,128)(2,1)S(1)}, u32[]{:S(2)}, u32[]{:S(2)}) collective-permute-start(bf16[528,128]{1,0:T(8,128)(2,1)S(1)} %shard_map.119), channel_id=1, source_target_pairs={{0,8},{4,12},{8,0},{12,4},{1,9},{5,13},{9,1},{13,5},{2,10},{6,14},... | collective-permute-start | bytes 405512 | tf_op jit(solution)/shard_map/ppermute | solution.py:278
  43.6 0.6 shard_map.118
  44.2 0.0 copy-start.8
  44.2 2.1 %collective-permute-start.9 = (bf16[528,128]{1,0:T(8,128)(2,1)S(1)}, bf16[528,128]{1,0:T(8,128)(2,1)S(1)}, u32[]{:S(2)}, u32[]{:S(2)}) collective-permute-start(bf16[528,128]{1,0:T(8,128)(2,1)S(1)} %shard_map.118), channel_id=1, source_target_pairs={{0,12},{4,0},{8,4},{12,8},{1,13},{5,1},{9,5},{13,9},{2,14},{6,2},{... | collective-permute-start | bytes 405512 | tf_op jit(solution)/shard_map/ppermute | solution.py:278
  46.4 0.6 shard_map.121.payload_ref
  47.0 4.0 %shard_map.122 = (f32[4,2,2,128,128]{4,3,2,1,0:T(8,128)S(1)}, bf16[4,2,2,192,128]{4,3,2,1,0:T(8,128)(2,1)S(1)}, f32[4,2,128,128]{3,2,1,0:T(8,128)S(1)}, f32[4,2,2,8,128]{4,3,2,1,0:T(8,128)S(1)}) custom-call(bf16[528,128]{1,0:T(8,128)(2,1)S(1)} %shard_map.121.payload_ref), custom_call_target="tpu_custom_call" | custom-call | tf_op jit(solution)/shard_map/pallas_call | solution.py:264
  51.0 0.0 collective-permute-done.11.payload_ref
  51.0 4.0 %shard_map.123 = (f32[4,2,2,128,128]{4,3,2,1,0:T(8,128)S(1)}, bf16[4,2,2,192,128]{4,3,2,1,0:T(8,128)(2,1)S(1)}, f32[4,2,128,128]{3,2,1,0:T(8,128)S(1)}, f32[4,2,2,8,128]{4,3,2,1,0:T(8,128)S(1)}) custom-call(bf16[528,128]{1,0:T(8,128)(2,1)S(1)} %collective-permute-done.11.payload_ref, ...), custom_call_target="tpu_custom_call", output_to_operand_aliasing={{0}: (1, {}), {1}: (2, {}), {2}: (3, {}), {3}: (4, {})} | custom-call | tf_op jit(solution)/shard_map/pallas_call | solution.py:264
  55.1 0.0 collective-permute-done.10.payload_ref
  55.1 4.1 %shard_map.124 = (f32[4,2,2,128,128]{4,3,2,1,0:T(8,128)S(1)}, bf16[4,2,2,192,128]{4,3,2,1,0:T(8,128)(2,1)S(1)}, f32[4,2,128,128]{3,2,1,0:T(8,128)S(1)}, f32[4,2,2,8,128]{4,3,2,1,0:T(8,128)S(1)}) custom-call(bf16[528,128]{1,0:T(8,128)(2,1)S(1)} %collective-permute-done.10.payload_ref, ...), custom_call_target="tpu_custom_call", output_to_operand_aliasing={{0}: (1, {}), {1}: (2, {}), {2}: (3, {}), {3}: (4, {})} | custom-call | tf_op jit(solution)/shard_map/pallas_call | solution.py:264
  59.2 4.1 %shard_map.125 = (f32[4,2,2,128,128]{4,3,2,1,0:T(8,128)S(1)}, bf16[4,2,2,192,128]{4,3,2,1,0:T(8,128)(2,1)S(1)}, f32[4,2,128,128]{3,2,1,0:T(8,128)S(1)}, f32[4,2,2,8,128]{4,3,2,1,0:T(8,128)S(1)}) custom-call(bf16[528,128]{1,0:T(8,128)(2,1)S(1)} %collective-permute-done.9.payload_ref, ...), custom_call_target="tpu_custom_call", output_to_operand_aliasing={{0}: (1, {}), {1}: (2, {}), {2}: (3, {}), {3}: (4, {})} | custom-call | tf_op jit(solution)/shard_map/pallas_call | solution.py:264
  63.2 1.2 %shard_map.126 = (bf16[128,256]{1,0:T(8,128)(2,1)S(1)}, bf16[128,256]{1,0:T(8,128)(2,1)S(1)}, bf16[128,256]{1,0:T(8,128)(2,1)S(1)}, bf16[128,256]{1,0:T(8,128)(2,1)S(1)}) custom-call(f32[4,2,2,128,128]{4,3,2,1,0:T(8,128)S(1)} %get-tuple-element.52.offset_ref, bf16[4,2,2,192,128]{4,3,2,1,0:T(8,128)(2,1)S(1)} %get-tuple-element.53.linear_ref, ...), custom_call_target="tpu_custom_call" | custom-call | tf_op jit(solution)/shard_map/pallas_call | solution.py:264
  64.4 2.1 %collective-permute-start.12 = (bf16[128,256]{1,0:T(8,128)(2,1)S(1)}, bf16[128,256]{1,0:T(8,128)(2,1)S(1)}, u32[]{:S(2)}, u32[]{:S(2)}) collective-permute-start(bf16[128,256]{1,0:T(8,128)(2,1)S(1)} %get-tuple-element.57), channel_id=1, source_target_pairs={{0,12},{4,0},{8,4},{12,8},{1,13},{5,1},{9,5},{13,9},{2,14},{6,2},{... | collective-permute-start | bytes 196616 | tf_op jit(solution)/shard_map/ppermute | solution.py:278
  66.5 0.6 collective-permute-start.13
  67.1 1.9 %collective-permute-start.14 = (bf16[128,256]{1,0:T(8,128)(2,1)S(1)}, bf16[128,256]{1,0:T(8,128)(2,1)S(1)}, u32[]{:S(2)}, u32[]{:S(2)}) collective-permute-start(bf16[128,256]{1,0:T(8,128)(2,1)S(1)} %get-tuple-element.59), channel_id=1, source_target_pairs={{0,4},{4,8},{8,12},{12,0},{1,5},{5,9},{9,13},{13,1},{2,6},{6,10},{... | collective-permute-start | bytes 196616 | tf_op jit(solution)/shard_map/ppermute | solution.py:278
  69.0 0.7 copy.36
  69.7 3.8 %collective-permute-done.13.back2 = bf16[128,256]{1,0:T(8,128)(2,1)S(1)} collective-permute-done((bf16[128,256]{1,0:T(8,128)(2,1)S(1)}, bf16[128,256]{1,0:T(8,128)(2,1)S(1)}, u32[]{:S(2)}, u32[]{:S(2)}) %collective-permute-start.13) | collective-permute-done | bytes 65568 | tf_op jit(solution)/shard_map/ppermute | solution.py:278
  73.5 0.7 shard_map.127
  (16 shorter events, 0.1 us)
Async XLA Ops:
  1.7 7.6 %collective-permute-start.2 = (bf16[128,256]{1,0:T(8,128)(2,1)S(1)}, bf16[128,256]{1,0:T(8,128)(2,1)S(1)}, u32[]{:S(2)}, u32[]{:S(2)}) collective-permute-start(bf16[128,256]{1,0:T(8,128)(2,1)S(1)} %get-tuple-element.32), channel_id=1, source_target_pairs={{0,12},{4,0},{8,4},{12,8},{1,13},{5,1},{9,5},{13,9},{2,14},{6,2},{... | collective-permute-start | bytes 196616 | tf_op jit(solution)/shard_map/ppermute | solution.py:278
  6.8 6.5 %collective-permute-start.1 = (bf16[128,256]{1,0:T(8,128)(2,1)S(1)}, bf16[128,256]{1,0:T(8,128)(2,1)S(1)}, u32[]{:S(2)}, u32[]{:S(2)}) collective-permute-start(bf16[128,256]{1,0:T(8,128)(2,1)S(1)} %get-tuple-element.32), channel_id=1, source_target_pairs={{0,8},{4,12},{8,0},{12,4},{1,9},{5,13},{9,1},{13,5},{2,10},{6,14},... | collective-permute-start | bytes 196616 | tf_op jit(solution)/shard_map/ppermute | solution.py:278
  6.8 6.5 %collective-permute-start = (bf16[128,256]{1,0:T(8,128)(2,1)S(1)}, bf16[128,256]{1,0:T(8,128)(2,1)S(1)}, u32[]{:S(2)}, u32[]{:S(2)}) collective-permute-start(bf16[128,256]{1,0:T(8,128)(2,1)S(1)} %get-tuple-element.32), channel_id=1, source_target_pairs={{0,4},{4,8},{8,12},{12,0},{1,5},{5,9},{9,13},{13,1},{2,6},{6,10},{... | collective-permute-start | bytes 196616 | tf_op jit(solution)/shard_map/ppermute | solution.py:278
  9.3 4.5 %collective-permute-start.5 = (bf16[128,256]{1,0:T(8,128)(2,1)S(1)}, bf16[128,256]{1,0:T(8,128)(2,1)S(1)}, u32[]{:S(2)}, u32[]{:S(2)}) collective-permute-start(bf16[128,256]{1,0:T(8,128)(2,1)S(1)} %collective-permute-done.2.mine3), channel_id=1, source_target_pairs={{0,1},{1,0},{2,3},{3,2},{4,5},{5,4},{6,7},{7,6},{8,9},{9,8},{10,11... | collective-permute-start | bytes 196616 | tf_op jit(solution)/shard_map/ppermute | solution.py:278
  13.2 1.3 %collective-permute-start.4 = (bf16[128,256]{1,0:T(8,128)(2,1)S(1)}, bf16[128,256]{1,0:T(8,128)(2,1)S(1)}, u32[]{:S(2)}, u32[]{:S(2)}) collective-permute-start(bf16[128,256]{1,0:T(8,128)(2,1)S(1)} %collective-permute-done.1.mine2), channel_id=1, source_target_pairs={{0,1},{1,0},{2,3},{3,2},{4,5},{5,4},{6,7},{7,6},{8,9},{9,8},{10,11... | collective-permute-start | bytes 196616 | tf_op jit(solution)/shard_map/ppermute | solution.py:278
  13.2 1.4 %collective-permute-start.3 = (bf16[128,256]{1,0:T(8,128)(2,1)S(1)}, bf16[128,256]{1,0:T(8,128)(2,1)S(1)}, u32[]{:S(2)}, u32[]{:S(2)}) collective-permute-start(bf16[128,256]{1,0:T(8,128)(2,1)S(1)} %collective-permute-done.mine1), channel_id=1, source_target_pairs={{0,1},{1,0},{2,3},{3,2},{4,5},{5,4},{6,7},{7,6},{8,9},{9,8},{10,11... | collective-permute-start | bytes 196616 | tf_op jit(solution)/shard_map/ppermute | solution.py:278
  14.6 2.2 %copy-start.1 = (bf16[1024,2048]{1,0:T(8,128)(2,1)S(1)}, bf16[1024,2048]{1,0:T(8,128)(2,1)}, u32[]{:S(2)}) copy-start(bf16[1024,2048]{1,0:T(8,128)(2,1)} %weight_ref.5) | copy-start | bytes 12582916
  16.8 0.9 %copy-start.2 = (bf16[128,1024]{1,0:T(8,128)(2,1)S(1)}, bf16[128,1024]{1,0:T(8,128)(2,1)}, u32[]{:S(2)}) copy-start(bf16[128,1024]{1,0:T(8,128)(2,1)} %query_ref.1) | copy-start | bytes 786436
  17.8 0.9 %copy-start.3 = (bf16[128,1024]{1,0:T(8,128)(2,1)S(1)}, bf16[128,1024]{1,0:T(8,128)(2,1)}, u32[]{:S(2)}) copy-start(bf16[128,1024]{1,0:T(8,128)(2,1)} %gate_ref.1) | copy-start | bytes 786436
  18.7 0.9 %copy-start.4 = (bf16[128,512]{1,0:T(8,128)(2,1)S(1)}, bf16[128,512]{1,0:T(8,128)(2,1)}, u32[]{:S(2)}) copy-start(bf16[128,512]{1,0:T(8,128)(2,1)} %residual_ref.1) | copy-start | bytes 393220
  21.8 1.6 %collective-permute-start.6 = (bf16[128,1024]{1,0:T(8,128)(2,1)S(1)}, bf16[128,1024]{1,0:T(8,128)(2,1)S(1)}, u32[]{:S(2)}, u32[]{:S(2)}) collective-permute-start(bf16[128,1024]{1,0:T(8,128)(2,1)S(1)} %get-tuple-element.34), channel_id=1, source_target_pairs={{0,1},{1,0},{2,3},{3,2},{4,5},{5,4},{6,7},{7,6},{8,9},{9,8},{10,11... | collective-permute-start | bytes 786440 | tf_op jit(solution)/shard_map/ppermute | solution.py:278
  23.5 8.6 %collective-permute-start.7 = (bf16[128,1024]{1,0:T(8,128)(2,1)S(1)}, bf16[128,1024]{1,0:T(8,128)(2,1)S(1)}, u32[]{:S(2)}, u32[]{:S(2)}) collective-permute-start(bf16[128,1024]{1,0:T(8,128)(2,1)S(1)} %get-tuple-element.36), channel_id=1, source_target_pairs={{0,2},{2,0},{1,3},{3,1},{4,6},{6,4},{5,7},{7,5},{8,10},{10,8},{9,1... | collective-permute-start | bytes 786440 | tf_op jit(solution)/shard_map/ppermute | solution.py:278
  32.2 1.6 %collective-permute-start.8 = (bf16[128,1024]{1,0:T(8,128)(2,1)S(1)}, bf16[128,1024]{1,0:T(8,128)(2,1)S(1)}, u32[]{:S(2)}, u32[]{:S(2)}) collective-permute-start(bf16[128,1024]{1,0:T(8,128)(2,1)S(1)} %shard_map.116.own_ref), channel_id=1, source_target_pairs={{0,1},{1,0},{2,3},{3,2},{4,5},{5,4},{6,7},{7,6},{8,9},{9,8},{10,11... | collective-permute-start | bytes 786440 | tf_op jit(solution)/shard_map/ppermute | solution.py:278
  33.8 0.8 %copy-start.5 = (bf16[2048,8]{0,1:T(8,128)(2,1)S(1)}, bf16[2048,8]{0,1:T(8,128)(2,1)}, u32[]{:S(2)}) copy-start(bf16[2048,8]{0,1:T(8,128)(2,1)} %param.17) | copy-start | bytes 98308
  34.6 0.7 copy-start.6
  35.3 0.7 copy-start.7
  36.4 3.4 %copy-start = (bf16[2048,2048]{1,0:T(8,128)(2,1)S(1)}, bf16[2048,2048]{1,0:T(8,128)(2,1)}, u32[]{:S(2)}) copy-start(bf16[2048,2048]{1,0:T(8,128)(2,1)} %weight_ref.9) | copy-start | bytes 25165828
  40.4 10.6 %collective-permute-start.11 = (bf16[528,128]{1,0:T(8,128)(2,1)S(1)}, bf16[528,128]{1,0:T(8,128)(2,1)S(1)}, u32[]{:S(2)}, u32[]{:S(2)}) collective-permute-start(bf16[528,128]{1,0:T(8,128)(2,1)S(1)} %shard_map.120), channel_id=1, source_target_pairs={{0,4},{4,8},{8,12},{12,0},{1,5},{5,9},{9,13},{13,1},{2,6},{6,10},{... | collective-permute-start | bytes 405512 | tf_op jit(solution)/shard_map/ppermute | solution.py:278
  41.1 14.0 %collective-permute-start.10 = (bf16[528,128]{1,0:T(8,128)(2,1)S(1)}, bf16[528,128]{1,0:T(8,128)(2,1)S(1)}, u32[]{:S(2)}, u32[]{:S(2)}) collective-permute-start(bf16[528,128]{1,0:T(8,128)(2,1)S(1)} %shard_map.119), channel_id=1, source_target_pairs={{0,8},{4,12},{8,0},{12,4},{1,9},{5,13},{9,1},{13,5},{2,10},{6,14},... | collective-permute-start | bytes 405512 | tf_op jit(solution)/shard_map/ppermute | solution.py:278
  44.2 19.0 %copy-start.8 = (f32[128]{0:T(128)S(1)}, f32[128]{0:T(128)}, u32[]{:S(2)}) copy-start(f32[128]{0:T(128)} %param.19) | copy-start | bytes 1540
  44.2 14.9 %collective-permute-start.9 = (bf16[528,128]{1,0:T(8,128)(2,1)S(1)}, bf16[528,128]{1,0:T(8,128)(2,1)S(1)}, u32[]{:S(2)}, u32[]{:S(2)}) collective-permute-start(bf16[528,128]{1,0:T(8,128)(2,1)S(1)} %shard_map.118), channel_id=1, source_target_pairs={{0,12},{4,0},{8,4},{12,8},{1,13},{5,1},{9,5},{13,9},{2,14},{6,2},{... | collective-permute-start | bytes 405512 | tf_op jit(solution)/shard_map/ppermute | solution.py:278
  64.4 5.2 %collective-permute-start.12 = (bf16[128,256]{1,0:T(8,128)(2,1)S(1)}, bf16[128,256]{1,0:T(8,128)(2,1)S(1)}, u32[]{:S(2)}, u32[]{:S(2)}) collective-permute-start(bf16[128,256]{1,0:T(8,128)(2,1)S(1)} %get-tuple-element.57), channel_id=1, source_target_pairs={{0,12},{4,0},{8,4},{12,8},{1,13},{5,1},{9,5},{13,9},{2,14},{6,2},{... | collective-permute-start | bytes 196616 | tf_op jit(solution)/shard_map/ppermute | solution.py:278
  66.5 7.0 %collective-permute-start.13 = (bf16[128,256]{1,0:T(8,128)(2,1)S(1)}, bf16[128,256]{1,0:T(8,128)(2,1)S(1)}, u32[]{:S(2)}, u32[]{:S(2)}) collective-permute-start(bf16[128,256]{1,0:T(8,128)(2,1)S(1)} %get-tuple-element.58), channel_id=1, source_target_pairs={{0,8},{4,12},{8,0},{12,4},{1,9},{5,13},{9,1},{13,5},{2,10},{6,14},... | collective-permute-start | bytes 196616 | tf_op jit(solution)/shard_map/ppermute | solution.py:278
  67.1 6.4 %collective-permute-start.14 = (bf16[128,256]{1,0:T(8,128)(2,1)S(1)}, bf16[128,256]{1,0:T(8,128)(2,1)S(1)}, u32[]{:S(2)}, u32[]{:S(2)}) collective-permute-start(bf16[128,256]{1,0:T(8,128)(2,1)S(1)} %get-tuple-element.59), channel_id=1, source_target_pairs={{0,4},{4,8},{8,12},{12,0},{1,5},{5,9},{9,13},{13,1},{2,6},{6,10},{... | collective-permute-start | bytes 196616 | tf_op jit(solution)/shard_map/ppermute | solution.py:278

commit v2 on v1

--- a/solution.py
+++ b/solution.py
@@ -312,6 +312,30 @@
     second.wait()
 
 
+def fetch_kernel(*refs):
+    count = len(refs) // 2
+    copies = [
+        pltpu.make_async_copy(refs[n], refs[count + n], refs[-1].at[n]) for n in range(count)
+    ]
+    for copy in copies:
+        copy.start()
+    for copy in copies:
+        copy.wait()
+
+
+def fetched(*arrays):
+    moved = sum(array.size * array.dtype.itemsize for array in arrays)
+    return pl.pallas_call(
+        fetch_kernel,
+        out_shape=[pltpu.VMEM(array.shape, array.dtype) for array in arrays],
+        in_specs=[IN_HBM] * len(arrays),
+        out_specs=[IN_VMEM] * len(arrays),
+        scratch_shapes=[pltpu.SemaphoreType.DMA((len(arrays),))],
+        compiler_params=pltpu.CompilerParams(vmem_limit_bytes=4 * MIB),
+        cost_estimate=pl.CostEstimate(flops=0, bytes_accessed=moved, transcendentals=0),
+    )(*[in_hbm(array) for array in arrays])
+
+
 def attention_kernel(
     query_ref, gate_ref, own_ref, mine1, mine2, mine3, twin1, twin2, twin3, weight_ref, residual_ref,
     keep_ref, send_ref, keys, values, heads, partial,
@@ -420,17 +444,22 @@
     payload_ref[4 * rows : 4 * rows + 16] = small[...].astype(jnp.bfloat16)
 
 
-def unit_lower_inverse(strict, row, column):
-    same = lambda size: (row // size) == (column // size)
-    small = jnp.where(same(8), strict, 0.0)
-    second = dot3(small, small)
-    start = jnp.where(row == column, 1.0, 0.0) - small
-    start = start + dot3(start, second)
-    inverse = start + dot3(start, dot3(second, second))
-    for size in (8, 16, 32):
-        corner = jnp.where(same(2 * size) & jnp.logical_not(same(size)), strict, 0.0)
-        inverse = inverse - dot3(inverse, dot3(corner, inverse))
-    return inverse
+def unit_lower_inverses(stricts, row, column):
+    inner = (row >> 3) == (column >> 3)
+    identity = jnp.where(row == column, 1.0, 0.0)
+    smalls = [jnp.where(inner, strict, 0.0) for strict in stricts]
+    rests = [jnp.where(inner, 0.0, strict) for strict in stricts]
+    seconds = [dot3(small, small) for small in smalls]
+    inverses = [identity - small for small in smalls]
+    fourths = [dot3(second, second) for second in seconds]
+    inverses = [inverse + dot3(inverse, second) for inverse, second in zip(inverses, seconds)]
+    inverses = [inverse + dot3(inverse, fourth) for inverse, fourth in zip(inverses, fourths)]
+    steps = [dot3(inverse, rest) for inverse, rest in zip(inverses, rests)]
+    results = [inverse - dot3(step, inverse) for inverse, step in zip(inverses, steps)]
+    doubles = [dot3(step, step) for step in steps]
+    quads = [dot3(double, double) for double in doubles]
+    results = [result + dot3(double, result) for result, double in zip(results, doubles)]
+    return [result + dot3(quad, result) for result, quad in zip(results, quads)]
 
 
 def block_kernel(step, payload_ref, *refs):
@@ -439,48 +468,59 @@
     source = (lax.axis_index("ctx") + count - step) % count
     rows = (payload_ref.shape[0] - 16) // 4
     half = rows // 2
+    shift = half.bit_length() - 1
+    row = lax.broadcasted_iota(jnp.int32, (rows, 1), 0)
+    column = lax.broadcasted_iota(jnp.int32, (1, rows), 1)
+    together = (row >> shift) == (column >> shift)
+    inclusive = together & (row >= column)
+    strictly = together & (row > column)
+    early = column < half
+    below = jnp.where(inclusive, 1.0, 0.0).astype(jnp.bfloat16)
+    diagonal = jnp.where(row == column, 1.0, 0.0).astype(jnp.bfloat16)
+    heads = range(2)
     query, key = payload_ref[0:rows], payload_ref[rows : 2 * rows]
     extra = payload_ref[4 * rows : 4 * rows + 16]
-    row = lax.broadcasted_iota(jnp.int32, (rows, rows), 0)
-    column = lax.broadcasted_iota(jnp.int32, (rows, rows), 1)
-    together = (row // half) == (column // half)
-    inclusive = together & (row >= column)
-    strictly = together & (row > column)
-    below = jnp.where(inclusive, 1.0, 0.0).astype(jnp.bfloat16)
-    diagonal = jnp.where(row == column, 1.0, 0.0).astype(jnp.bfloat16)
     sums_row = dot(extra, below, ((1,), (1,)))
-    sums_column = dot(below, extra, ((1,), (1,)))
-    plain_column = dot(diagonal, extra, ((1,), (1,)))
+    turned = dot(jnp.concatenate([below, diagonal], axis=0), extra, ((1,), (1,)))
+    key_gram = dot(key, key, ((1,), (1,)))
+    total_rows = [sums_row[h : h + 1] + sums_row[h + 2 : h + 3] for h in heads]
+    totals = [turned[:rows, h : h + 1] + turned[:rows, h + 2 : h + 3] for h in heads]
+    betas = [turned[rows:, h + 4 : h + 5] + turned[rows:, h + 6 : h + 7] for h in heads]
+    decays = [jnp.exp(jnp.where(inclusive, totals[h] - total_rows[h], NEGATIVE)) for h in heads]
+    stricts = [jnp.where(strictly, betas[h] * key_gram * decays[h], 0.0) for h in heads]
+    query_gram = dot(query, key, ((1,), (1,)))
     key_wide = key.astype(jnp.float32)
     key_turned = jnp.transpose(key_wide)
-    key_gram = dot(key, key, ((1,), (1,)))
-    query_gram = dot(query, key, ((1,), (1,)))
-    early_lane = lax.broadcasted_iota(jnp.int32, (1, rows), 1) < half
-    for head in range(2):
-        total_row = sums_row[head : head + 1] + sums_row[head + 2 : head + 3]
-        total = sums_column[:, head : head + 1] + sums_column[:, head + 2 : head + 3]
-        beta = plain_column[:, head + 4 : head + 5] + plain_column[:, head + 6 : head + 7]
-        decay = jnp.exp(jnp.where(inclusive, total - total_row, NEGATIVE))
-        strict = jnp.where(strictly, beta * key_gram * decay, 0.0)
-        inverse_high, inverse_low = halves(unit_lower_inverse(strict, row, column))
-        growth = jnp.exp(total)
-        value = payload_ref[(2 + head) * rows : (3 + head) * rows].astype(jnp.float32)
-        right = jnp.concatenate([beta * value, (beta * growth) * key_wide], axis=1).astype(jnp.bfloat16)
-        solved = (dot(inverse_high, right) + dot(inverse_low, right)).astype(jnp.bfloat16)
-        attended = dot((query_gram * decay).astype(jnp.bfloat16), solved)
-        local_ref[source, head] = attended[:, :DV]
-        reads = (growth * query.astype(jnp.float32) - attended[:, DV:]).astype(jnp.bfloat16)
-        end_row = jnp.where(early_lane, total_row[:, half - 1 : half], total_row[:, rows - 1 : rows])
-        carried = key_turned * jnp.exp(end_row - total_row)
-        ends = jnp.exp(end_row)
+    growths = [jnp.exp(total) for total in totals]
+    values = [payload_ref[(2 + h) * rows : (3 + h) * rows].astype(jnp.float32) for h in heads]
+    rights = [
+        jnp.concatenate([betas[h] * values[h], (betas[h] * growths[h]) * key_wide], axis=1).astype(jnp.bfloat16)
+        for h in heads
+    ]
+    grams = [(query_gram * decays[h]).astype(jnp.bfloat16) for h in heads]
+    ends = [jnp.where(early, total[:, half - 1 : half], total[:, rows - 1 : rows]) for total in total_rows]
+    carried = [key_turned * jnp.exp(ends[h] - total_rows[h]) for h in heads]
+    lefts = [
+        jnp.concatenate([jnp.where(early, keys, 0.0), jnp.where(early, 0.0, keys)], axis=0).astype(jnp.bfloat16)
+        for keys in carried
+    ]
+    inverses = [halves(inverse) for inverse in unit_lower_inverses(stricts, row, column)]
+    solved = [
+        (dot(high, right) + dot(low, right)).astype(jnp.bfloat16) for (high, low), right in zip(inverses, rights)
+    ]
+    moved = [dot(jnp.concatenate([lefts[h], grams[h]], axis=0), solved[h]) for h in heads]
+    for h in heads:
+        attended = moved[h][2 * DK :]
+        local_ref[source, h] = attended[:, :DV]
+        reads = (growths[h] * query.astype(jnp.float32) - attended[:, DV:]).astype(jnp.bfloat16)
+        growth = jnp.exp(ends[h])
         for block in range(2):
-            inside = early_lane if block == 0 else jnp.logical_not(early_lane)
-            moved = dot(jnp.where(inside, carried, 0.0).astype(jnp.bfloat16), solved)
-            offset_ref[source, head, block] = moved[:, :DV]
-            linear_ref[source, head, block, 0:DK] = moved[:, DV:].astype(jnp.bfloat16)
-            linear_ref[source, head, block, DK : DK + half] = reads[block * half : (block + 1) * half]
+            state = moved[h][block * DK : (block + 1) * DK]
+            offset_ref[source, h, block] = state[:, :DV]
+            linear_ref[source, h, block, 0:DK] = state[:, DV:].astype(jnp.bfloat16)
+            linear_ref[source, h, block, DK : DK + half] = reads[block * half : (block + 1) * half]
             last = (block + 1) * half - 1
-            growth_ref[source, head, block] = jnp.broadcast_to(ends[:, last : last + 1], growth_ref.shape[3:])
+            growth_ref[source, h, block] = jnp.broadcast_to(growth[:, last : last + 1], growth_ref.shape[3:])
 
 
 def scan_kernel(offset_ref, linear_ref, local_ref, growth_ref, gain_ref, own_ref, back1, back2, back3, outs):
@@ -538,8 +578,12 @@
         in_specs=[IN_HBM],
         out_specs=[IN_VMEM] * 2,
         scratch_shapes=[pltpu.SemaphoreType.DMA((2,))],
+        compiler_params=pltpu.CompilerParams(vmem_limit_bytes=4 * MIB),
     )(in_hbm(att_kv))
     mine = [rotated(piece, "ctx", step) for step in steps]
+    piece, *late = lax.optimization_barrier((piece, att_query, att_gate, out_weight, residual))
+    late = fetched(*late)
+    mine[2], (att_query, att_gate, out_weight, residual) = lax.optimization_barrier((mine[2], late))
     twin = [rotated(part, "sub", 1) for part in mine]
     keep, send = vmem_call(
         attention_kernel,
@@ -557,12 +601,16 @@
         [((rows, half_model), f32), ((rows, half_model), bf16)],
         [keep, rotated(send, "sub", 1)],
     )
-    hidden = vmem_call(hidden_kernel, [((rows, half_model), bf16)], [chip_sum, rotated(send, "head", 1)])[0]
-    value_here = log_decay.shape[1]
+    other_sum = rotated(send, "head", 1)
+    send, *late = lax.optimization_barrier((send, in_weight, norm_gain[None, :], beta_weight.T, log_decay.T))
+    late = fetched(*late)
+    other_sum, (in_weight, norm_gain, beta_weight, log_decay) = lax.optimization_barrier((other_sum, late))
+    hidden = vmem_call(hidden_kernel, [((rows, half_model), bf16)], [chip_sum, other_sum])[0]
+    value_here = log_decay.shape[0]
     new_residual, normed, extra = vmem_call(
         norm_kernel,
         [(residual.shape, bf16), ((rows, model), bf16), ((2 * value_here, rows), f32)],
-        [hidden, rotated(hidden, "sub", 1), norm_gain[None, :], beta_weight.T, log_decay.T],
+        [hidden, rotated(hidden, "sub", 1), norm_gain, beta_weight, log_decay],
     )
     payloads = [
         vmem_call(

time: 74.7 us -> 59.4 us (0.80)
  local copies, waits for them, and re-layouts: 11.2 us -> 0.66 us
  waiting for transfers between devices: 20 us -> 18 us
  Pallas kernels: 24.3 us -> 22.4 us
    unnamed x19 -> x3, local copies, waits for them, and re-layouts: 11.2 us -> 0.66 us
    pallas_call x14, Pallas kernels: 23.3 us -> 15.5 us  [vmem_call(): pl.pallas_call(kernel, out_shape=[make(shape, dtype) for shape, dtype in...]
    pallas_call x0 -> x2, Pallas kernels: none -> 5.81 us  [fetched(): pl.pallas_call(fetch_kernel, out_shape=[pltpu.VMEM(array.shape, array.dty...]
    ppermute x15, waiting for transfers between devices: 20 us -> 18 us  [rotated(): lax.ppermute(value, axis, [(i, (i + steps) % count) for i in range(count)])]
  transfers between devices with their start and end apart: 15 -> 15, of which waited for: 8 -> 11; matrix products, arithmetic and copies ran while one was open for 1% -> 1% of each run, Pallas kernels for 19% -> 23%
where the time goes in v2:
time: 59.4 us; the launch traced here: 59.3 us
  Pallas kernels  22.4 us (38%)
  waiting for transfers between devices  18 us (30%)
  starting transfers between devices  17.5 us (29%)
  between operations  0.79 us (1%)
  local copies, waits for them, and re-layouts  0.66 us (1%)
    ppermute x15, waiting for transfers between devices, rotated(): lax.ppermute(value, axis, [(i, (i + steps) % count) for i in range(count)])  18 us
    ppermute x15, starting transfers between devices, rotated(): lax.ppermute(value, axis, [(i, (i + steps) % count) for i in range(count)])  17.5 us
    pallas_call x14, Pallas kernels, vmem_call(): pl.pallas_call(kernel, out_shape=[make(shape, dtype) for shape, dtype in...  15.5 us
    pallas_call x2, Pallas kernels, fetched(): pl.pallas_call(fetch_kernel, out_shape=[pltpu.VMEM(array.shape, array.dty...  5.81 us
  transfers between devices with their start and end apart: 15, of which 11 were waited for; matrix products, arithmetic and copies ran while one was open for 1% of the time, Pallas kernels for 23%

profile of v2, /device:TPU:0, one launch (start us, length us, event | category | flops | bytes accessed | tf_op | source)
XLA Modules:
  0.0 59.3 jit_solution(4562453101984789107)
XLA Ops:
  0.6 1.0 %shard_map.113 = (bf16[128,256]{1,0:T(8,128)(2,1)S(1)}, bf16[128,512]{1,0:T(8,128)(2,1)S(1)}) custom-call(bf16[128,1024]{1,0:T(8,128)(2,1)} %kv_ref.1), custom_call_target="tpu_custom_call" | custom-call | tf_op jit(solution)/shard_map/pallas_call | solution.py:575
  1.7 5.1 %collective-permute-start = (bf16[128,256]{1,0:T(8,128)(2,1)S(1)}, bf16[128,256]{1,0:T(8,128)(2,1)S(1)}, u32[]{:S(2)}, u32[]{:S(2)}) collective-permute-start(bf16[128,256]{1,0:T(8,128)(2,1)S(1)} %get-tuple-element.57), channel_id=1, source_target_pairs={{0,12},{4,0},{8,4},{12,8},{1,13},{5,1},{9,5},{13,9},{2,14},{6,2},{... | collective-permute-start | bytes 196616 | tf_op jit(solution)/shard_map/ppermute | solution.py:278
  6.8 0.0 collective-permute-start.2
  6.8 1.0 %collective-permute-start.1 = (bf16[128,256]{1,0:T(8,128)(2,1)S(1)}, bf16[128,256]{1,0:T(8,128)(2,1)S(1)}, u32[]{:S(2)}, u32[]{:S(2)}) collective-permute-start(bf16[128,256]{1,0:T(8,128)(2,1)S(1)} %get-tuple-element.57), channel_id=1, source_target_pairs={{0,4},{4,8},{8,12},{12,0},{1,5},{5,9},{9,13},{13,1},{2,6},{6,10},{... | collective-permute-start | bytes 196616 | tf_op jit(solution)/shard_map/ppermute | solution.py:278
  7.8 2.4 %shard_map.114 = (bf16[128,1024]{1,0:T(8,128)(2,1)S(1)}, bf16[128,1024]{1,0:T(8,128)(2,1)S(1)}, bf16[1024,2048]{1,0:T(8,128)(2,1)S(1)}, bf16[128,512]{1,0:T(8,128)(2,1)S(1)}) custom-call(bf16[128,1024]{1,0:T(8,128)(2,1)} %refs_0_, bf16[128,1024]{1,0:T(8,128)(2,1)} %refs_1_, bf16[1024,2048]{1,0:T(8,128)(2,1)} %refs_2_, bf16[128,512]{1,0:T(8,128)(2,1)} %refs_3_), custom_call_target="tpu_custom_call" | custom-call | bytes 4849664 | tf_op jit(solution)/shard_map/pallas_call | solution.py:328
  10.2 0.0 collective-permute-done.mine3
  10.2 3.0 %collective-permute-done.2.mine2 = bf16[128,256]{1,0:T(8,128)(2,1)S(1)} collective-permute-done((bf16[128,256]{1,0:T(8,128)(2,1)S(1)}, bf16[128,256]{1,0:T(8,128)(2,1)S(1)}, u32[]{:S(2)}, u32[]{:S(2)}) %collective-permute-start.2) | collective-permute-done | bytes 65568 | tf_op jit(solution)/shard_map/ppermute | solution.py:278
  13.2 0.0 collective-permute-start.4
  13.2 0.0 collective-permute-done.1.mine1
  13.2 0.5 collective-permute-start.3
  13.7 0.0 collective-permute-start.5
  13.8 0.7 %collective-permute-done.4.twin2 = bf16[128,256]{1,0:T(8,128)(2,1)S(1)} collective-permute-done((bf16[128,256]{1,0:T(8,128)(2,1)S(1)}, bf16[128,256]{1,0:T(8,128)(2,1)S(1)}, u32[]{:S(2)}, u32[]{:S(2)}) %collective-permute-start.4) | collective-permute-done | bytes 65568 | tf_op jit(solution)/shard_map/ppermute | solution.py:278
  14.5 0.2 collective-permute-done.3.twin1
  14.6 0.4 collective-permute-done.5.twin3
  15.0 2.2 %shard_map.115 = (f32[128,1024]{1,0:T(8,128)S(1)}, bf16[128,1024]{1,0:T(8,128)(2,1)S(1)}) custom-call(bf16[128,1024]{1,0:T(8,128)(2,1)S(1)} %get-tuple-element.66.query_ref, bf16[128,1024]{1,0:T(8,128)(2,1)S(1)} %get-tuple-element.67.gate_ref, bf16[128,512]{1,0:T(8,128)(2,1)S(1)} %get-tuple-element.68.own_ref, ...), custom_call_target="tpu_custom_call" | custom-call | tf_op jit(solution)/shard_map/pallas_call | solution.py:264
  17.2 0.2 collective-permute-start.6
  17.4 1.4 %collective-permute-done.6.came_ref = bf16[128,1024]{1,0:T(8,128)(2,1)S(1)} collective-permute-done((bf16[128,1024]{1,0:T(8,128)(2,1)S(1)}, bf16[128,1024]{1,0:T(8,128)(2,1)S(1)}, u32[]{:S(2)}, u32[]{:S(2)}) %collective-permute-start.6) | collective-permute-done | bytes 262176 | tf_op jit(solution)/shard_map/ppermute | solution.py:278
  18.8 0.1 shard_map.116
  18.9 1.5 %collective-permute-start.7 = (bf16[128,1024]{1,0:T(8,128)(2,1)S(1)}, bf16[128,1024]{1,0:T(8,128)(2,1)S(1)}, u32[]{:S(2)}, u32[]{:S(2)}) collective-permute-start(bf16[128,1024]{1,0:T(8,128)(2,1)S(1)} %get-tuple-element.75), channel_id=1, source_target_pairs={{0,2},{2,0},{1,3},{3,1},{4,6},{6,4},{5,7},{7,5},{8,10},{10,8},{9,1... | collective-permute-start | bytes 786440 | tf_op jit(solution)/shard_map/ppermute | solution.py:278
  20.4 3.4 %shard_map.117 = (bf16[2048,2048]{1,0:T(8,128)(2,1)S(1)}, f32[1,2048]{1,0:T(1,128)S(1)}, bf16[8,2048]{1,0:T(8,128)(2,1)S(1)}, f32[8,128]{1,0:T(8,128)S(1)}) custom-call(bf16[2048,2048]{1,0:T(8,128)(2,1)} %refs_0_.1, f32[1,2048]{1,0:T(1,128)} %bitcast.6, bf16[8,2048]{1,0:T(8,128)(2,1)} %bitcast.5, f32[8,128]{1,0:T(8,128)} %bitcast.7), custom_call_target="tpu_custom_call" | custom-call | bytes 8433664 | tf_op jit(solution)/shard_map/pallas_call | solution.py:328
  23.9 3.5 %collective-permute-done.7.came_ref = bf16[128,1024]{1,0:T(8,128)(2,1)S(1)} collective-permute-done((bf16[128,1024]{1,0:T(8,128)(2,1)S(1)}, bf16[128,1024]{1,0:T(8,128)(2,1)S(1)}, u32[]{:S(2)}, u32[]{:S(2)}) %collective-permute-start.7) | collective-permute-done | bytes 262176 | tf_op jit(solution)/shard_map/ppermute | solution.py:278
  27.4 0.1 collective-permute-start.8
  27.5 1.5 %collective-permute-done.8.twin_ref = bf16[128,1024]{1,0:T(8,128)(2,1)S(1)} collective-permute-done((bf16[128,1024]{1,0:T(8,128)(2,1)S(1)}, bf16[128,1024]{1,0:T(8,128)(2,1)S(1)}, u32[]{:S(2)}, u32[]{:S(2)}) %collective-permute-start.8) | collective-permute-done | bytes 262176 | tf_op jit(solution)/shard_map/ppermute | solution.py:278
  29.0 0.5 shard_map.119
  29.5 0.6 %shard_map.122 = bf16[528,128]{1,0:T(8,128)(2,1)S(1)} custom-call(bf16[128,2048]{1,0:T(8,128)(2,1)S(1)} %get-tuple-element.89.normed_ref, bf16[2048,2048]{1,0:T(8,128)(2,1)S(1)} %get-tuple-element.90.weight_ref, f32[16,128]{1,0:T(8,128)S(1)} %get-tuple-element.91.extra_ref), custom_call_target="tpu_custom_call" | custom-call | tf_op jit(solution)/shard_map/pallas_call | solution.py:264
  30.1 0.1 collective-permute-start.11
  30.2 0.6 %shard_map.121 = bf16[528,128]{1,0:T(8,128)(2,1)S(1)} custom-call(bf16[128,2048]{1,0:T(8,128)(2,1)S(1)} %get-tuple-element.89.normed_ref, bf16[2048,2048]{1,0:T(8,128)(2,1)S(1)} %get-tuple-element.90.weight_ref, f32[16,128]{1,0:T(8,128)S(1)} %get-tuple-element.91.extra_ref), custom_call_target="tpu_custom_call" | custom-call | tf_op jit(solution)/shard_map/pallas_call | solution.py:264
  30.8 2.5 %collective-permute-start.10 = (bf16[528,128]{1,0:T(8,128)(2,1)S(1)}, bf16[528,128]{1,0:T(8,128)(2,1)S(1)}, u32[]{:S(2)}, u32[]{:S(2)}) collective-permute-start(bf16[528,128]{1,0:T(8,128)(2,1)S(1)} %shard_map.121), channel_id=1, source_target_pairs={{0,8},{4,12},{8,0},{12,4},{1,9},{5,13},{9,1},{13,5},{2,10},{6,14},... | collective-permute-start | bytes 405512 | tf_op jit(solution)/shard_map/ppermute | solution.py:278
  33.3 0.6 %shard_map.120 = bf16[528,128]{1,0:T(8,128)(2,1)S(1)} custom-call(bf16[128,2048]{1,0:T(8,128)(2,1)S(1)} %get-tuple-element.89.normed_ref, bf16[2048,2048]{1,0:T(8,128)(2,1)S(1)} %get-tuple-element.90.weight_ref, f32[16,128]{1,0:T(8,128)S(1)} %get-tuple-element.91.extra_ref), custom_call_target="tpu_custom_call" | custom-call | tf_op jit(solution)/shard_map/pallas_call | solution.py:264
  33.9 0.0 copy-start
  33.9 2.1 %collective-permute-start.9 = (bf16[528,128]{1,0:T(8,128)(2,1)S(1)}, bf16[528,128]{1,0:T(8,128)(2,1)S(1)}, u32[]{:S(2)}, u32[]{:S(2)}) collective-permute-start(bf16[528,128]{1,0:T(8,128)(2,1)S(1)} %shard_map.120), channel_id=1, source_target_pairs={{0,12},{4,0},{8,4},{12,8},{1,13},{5,1},{9,5},{13,9},{2,14},{6,2},{... | collective-permute-start | bytes 405512 | tf_op jit(solution)/shard_map/ppermute | solution.py:278
  36.0 0.6 shard_map.123.payload_ref
  36.6 2.1 %shard_map.124 = (f32[4,2,2,128,128]{4,3,2,1,0:T(8,128)S(1)}, bf16[4,2,2,192,128]{4,3,2,1,0:T(8,128)(2,1)S(1)}, f32[4,2,128,128]{3,2,1,0:T(8,128)S(1)}, f32[4,2,2,8,128]{4,3,2,1,0:T(8,128)S(1)}) custom-call(bf16[528,128]{1,0:T(8,128)(2,1)S(1)} %shard_map.123.payload_ref), custom_call_target="tpu_custom_call" | custom-call | tf_op jit(solution)/shard_map/pallas_call | solution.py:264
  38.7 0.0 collective-permute-done.11.payload_ref
  38.7 2.1 %shard_map.125 = (f32[4,2,2,128,128]{4,3,2,1,0:T(8,128)S(1)}, bf16[4,2,2,192,128]{4,3,2,1,0:T(8,128)(2,1)S(1)}, f32[4,2,128,128]{3,2,1,0:T(8,128)S(1)}, f32[4,2,2,8,128]{4,3,2,1,0:T(8,128)S(1)}) custom-call(bf16[528,128]{1,0:T(8,128)(2,1)S(1)} %collective-permute-done.11.payload_ref, ...), custom_call_target="tpu_custom_call", output_to_operand_aliasing={{0}: (1, {}), {1}: (2, {}), {2}: (3, {}), {3}: (4, {})} | custom-call | tf_op jit(solution)/shard_map/pallas_call | solution.py:264
  40.8 2.6 %collective-permute-done.10.payload_ref = bf16[528,128]{1,0:T(8,128)(2,1)S(1)} collective-permute-done((bf16[528,128]{1,0:T(8,128)(2,1)S(1)}, bf16[528,128]{1,0:T(8,128)(2,1)S(1)}, u32[]{:S(2)}, u32[]{:S(2)}) %collective-permute-start.10) | collective-permute-done | bytes 135200 | tf_op jit(solution)/shard_map/ppermute | solution.py:278
  43.5 2.1 %shard_map.126 = (f32[4,2,2,128,128]{4,3,2,1,0:T(8,128)S(1)}, bf16[4,2,2,192,128]{4,3,2,1,0:T(8,128)(2,1)S(1)}, f32[4,2,128,128]{3,2,1,0:T(8,128)S(1)}, f32[4,2,2,8,128]{4,3,2,1,0:T(8,128)S(1)}) custom-call(bf16[528,128]{1,0:T(8,128)(2,1)S(1)} %collective-permute-done.10.payload_ref, ...), custom_call_target="tpu_custom_call", output_to_operand_aliasing={{0}: (1, {}), {1}: (2, {}), {2}: (3, {}), {3}: (4, {})} | custom-call | tf_op jit(solution)/shard_map/pallas_call | solution.py:264
  45.6 0.0 collective-permute-done.9.payload_ref
  45.6 2.1 %shard_map.127 = (f32[4,2,2,128,128]{4,3,2,1,0:T(8,128)S(1)}, bf16[4,2,2,192,128]{4,3,2,1,0:T(8,128)(2,1)S(1)}, f32[4,2,128,128]{3,2,1,0:T(8,128)S(1)}, f32[4,2,2,8,128]{4,3,2,1,0:T(8,128)S(1)}) custom-call(bf16[528,128]{1,0:T(8,128)(2,1)S(1)} %collective-permute-done.9.payload_ref, ...), custom_call_target="tpu_custom_call", output_to_operand_aliasing={{0}: (1, {}), {1}: (2, {}), {2}: (3, {}), {3}: (4, {})} | custom-call | tf_op jit(solution)/shard_map/pallas_call | solution.py:264
  47.7 1.2 %shard_map.128 = (bf16[128,256]{1,0:T(8,128)(2,1)S(1)}, bf16[128,256]{1,0:T(8,128)(2,1)S(1)}, bf16[128,256]{1,0:T(8,128)(2,1)S(1)}, bf16[128,256]{1,0:T(8,128)(2,1)S(1)}) custom-call(f32[4,2,2,128,128]{4,3,2,1,0:T(8,128)S(1)} %get-tuple-element.104.offset_ref, bf16[4,2,2,192,128]{4,3,2,1,0:T(8,128)(2,1)S(1)} %get-tuple-element.105.linear_ref, ...), custom_call_target="tpu_custom_call" | custom-call | tf_op jit(solution)/shard_map/pallas_call | solution.py:264
  48.9 3.6 %collective-permute-start.12 = (bf16[128,256]{1,0:T(8,128)(2,1)S(1)}, bf16[128,256]{1,0:T(8,128)(2,1)S(1)}, u32[]{:S(2)}, u32[]{:S(2)}) collective-permute-start(bf16[128,256]{1,0:T(8,128)(2,1)S(1)} %get-tuple-element.109), channel_id=1, source_target_pairs={{0,12},{4,0},{8,4},{12,8},{1,13},{5,1},{9,5},{13,9},{2,14},{6,2},{... | collective-permute-start | bytes 196616 | tf_op jit(solution)/shard_map/ppermute | solution.py:278
  52.4 0.0 collective-permute-start.13
  52.4 0.8 %collective-permute-start.14 = (bf16[128,256]{1,0:T(8,128)(2,1)S(1)}, bf16[128,256]{1,0:T(8,128)(2,1)S(1)}, u32[]{:S(2)}, u32[]{:S(2)}) collective-permute-start(bf16[128,256]{1,0:T(8,128)(2,1)S(1)} %get-tuple-element.111), channel_id=1, source_target_pairs={{0,4},{4,8},{8,12},{12,0},{1,5},{5,9},{9,13},{13,1},{2,6},{6,10},{... | collective-permute-start | bytes 196616 | tf_op jit(solution)/shard_map/ppermute | solution.py:278
  53.2 0.7 %copy.36 = bf16[128,512]{1,0:T(8,128)(2,1)} copy(bf16[128,512]{1,0:T(8,128)(2,1)S(1)} %get-tuple-element.112) | data formatting | bytes 262144
  53.9 1.1 %collective-permute-done.12.back1 = bf16[128,256]{1,0:T(8,128)(2,1)S(1)} collective-permute-done((bf16[128,256]{1,0:T(8,128)(2,1)S(1)}, bf16[128,256]{1,0:T(8,128)(2,1)S(1)}, u32[]{:S(2)}, u32[]{:S(2)}) %collective-permute-start.12) | collective-permute-done | bytes 65568 | tf_op jit(solution)/shard_map/ppermute | solution.py:278
  54.9 2.9 %collective-permute-done.13.back2 = bf16[128,256]{1,0:T(8,128)(2,1)S(1)} collective-permute-done((bf16[128,256]{1,0:T(8,128)(2,1)S(1)}, bf16[128,256]{1,0:T(8,128)(2,1)S(1)}, u32[]{:S(2)}, u32[]{:S(2)}) %collective-permute-start.13) | collective-permute-done | bytes 65568 | tf_op jit(solution)/shard_map/ppermute | solution.py:278
  57.9 0.7 %collective-permute-done.14.back3 = bf16[128,256]{1,0:T(8,128)(2,1)S(1)} collective-permute-done((bf16[128,256]{1,0:T(8,128)(2,1)S(1)}, bf16[128,256]{1,0:T(8,128)(2,1)S(1)}, u32[]{:S(2)}, u32[]{:S(2)}) %collective-permute-start.14) | collective-permute-done | bytes 65568 | tf_op jit(solution)/shard_map/ppermute | solution.py:278
  58.6 0.7 %shard_map.129 = bf16[128,1024]{1,0:T(8,128)(2,1)} custom-call(bf16[128,256]{1,0:T(8,128)(2,1)S(1)} %get-tuple-element.108.own_ref, bf16[128,256]{1,0:T(8,128)(2,1)S(1)} %collective-permute-done.12.back1, bf16[128,256]{1,0:T(8,128)(2,1)S(1)} %collective-permute-done.13.back2, bf16[128,256]{1,0:T(8,128)(2,1)S(1)} %collective-permute-done.14.back3), custom_call_target="tpu_custom_call" | custom-call | tf_op jit(solution)/shard_map/pallas_call | solution.py:264
  (2 shorter events, 0.0 us)
Async XLA Ops:
  1.7 8.5 %collective-permute-start = (bf16[128,256]{1,0:T(8,128)(2,1)S(1)}, bf16[128,256]{1,0:T(8,128)(2,1)S(1)}, u32[]{:S(2)}, u32[]{:S(2)}) collective-permute-start(bf16[128,256]{1,0:T(8,128)(2,1)S(1)} %get-tuple-element.57), channel_id=1, source_target_pairs={{0,12},{4,0},{8,4},{12,8},{1,13},{5,1},{9,5},{13,9},{2,14},{6,2},{... | collective-permute-start | bytes 196616 | tf_op jit(solution)/shard_map/ppermute | solution.py:278
  6.8 6.5 %collective-permute-start.2 = (bf16[128,256]{1,0:T(8,128)(2,1)S(1)}, bf16[128,256]{1,0:T(8,128)(2,1)S(1)}, u32[]{:S(2)}, u32[]{:S(2)}) collective-permute-start(bf16[128,256]{1,0:T(8,128)(2,1)S(1)} %get-tuple-element.57), channel_id=1, source_target_pairs={{0,8},{4,12},{8,0},{12,4},{1,9},{5,13},{9,1},{13,5},{2,10},{6,14},... | collective-permute-start | bytes 196616 | tf_op jit(solution)/shard_map/ppermute | solution.py:278
  6.8 6.5 %collective-permute-start.1 = (bf16[128,256]{1,0:T(8,128)(2,1)S(1)}, bf16[128,256]{1,0:T(8,128)(2,1)S(1)}, u32[]{:S(2)}, u32[]{:S(2)}) collective-permute-start(bf16[128,256]{1,0:T(8,128)(2,1)S(1)} %get-tuple-element.57), channel_id=1, source_target_pairs={{0,4},{4,8},{8,12},{12,0},{1,5},{5,9},{9,13},{13,1},{2,6},{6,10},{... | collective-permute-start | bytes 196616 | tf_op jit(solution)/shard_map/ppermute | solution.py:278
  13.2 1.3 %collective-permute-start.4 = (bf16[128,256]{1,0:T(8,128)(2,1)S(1)}, bf16[128,256]{1,0:T(8,128)(2,1)S(1)}, u32[]{:S(2)}, u32[]{:S(2)}) collective-permute-start(bf16[128,256]{1,0:T(8,128)(2,1)S(1)} %collective-permute-done.2.mine2), channel_id=1, source_target_pairs={{0,1},{1,0},{2,3},{3,2},{4,5},{5,4},{6,7},{7,6},{8,9},{9,8},{10,11... | collective-permute-start | bytes 196616 | tf_op jit(solution)/shard_map/ppermute | solution.py:278
  13.2 1.4 %collective-permute-start.3 = (bf16[128,256]{1,0:T(8,128)(2,1)S(1)}, bf16[128,256]{1,0:T(8,128)(2,1)S(1)}, u32[]{:S(2)}, u32[]{:S(2)}) collective-permute-start(bf16[128,256]{1,0:T(8,128)(2,1)S(1)} %collective-permute-done.1.mine1), channel_id=1, source_target_pairs={{0,1},{1,0},{2,3},{3,2},{4,5},{5,4},{6,7},{7,6},{8,9},{9,8},{10,11... | collective-permute-start | bytes 196616 | tf_op jit(solution)/shard_map/ppermute | solution.py:278
  13.7 1.3 %collective-permute-start.5 = (bf16[128,256]{1,0:T(8,128)(2,1)S(1)}, bf16[128,256]{1,0:T(8,128)(2,1)S(1)}, u32[]{:S(2)}, u32[]{:S(2)}) collective-permute-start(bf16[128,256]{1,0:T(8,128)(2,1)S(1)} %collective-permute-done.mine3), channel_id=1, source_target_pairs={{0,1},{1,0},{2,3},{3,2},{4,5},{5,4},{6,7},{7,6},{8,9},{9,8},{10,11... | collective-permute-start | bytes 196616 | tf_op jit(solution)/shard_map/ppermute | solution.py:278
  17.2 1.6 %collective-permute-start.6 = (bf16[128,1024]{1,0:T(8,128)(2,1)S(1)}, bf16[128,1024]{1,0:T(8,128)(2,1)S(1)}, u32[]{:S(2)}, u32[]{:S(2)}) collective-permute-start(bf16[128,1024]{1,0:T(8,128)(2,1)S(1)} %get-tuple-element.73), channel_id=1, source_target_pairs={{0,1},{1,0},{2,3},{3,2},{4,5},{5,4},{6,7},{7,6},{8,9},{9,8},{10,11... | collective-permute-start | bytes 786440 | tf_op jit(solution)/shard_map/ppermute | solution.py:278
  18.9 8.4 %collective-permute-start.7 = (bf16[128,1024]{1,0:T(8,128)(2,1)S(1)}, bf16[128,1024]{1,0:T(8,128)(2,1)S(1)}, u32[]{:S(2)}, u32[]{:S(2)}) collective-permute-start(bf16[128,1024]{1,0:T(8,128)(2,1)S(1)} %get-tuple-element.75), channel_id=1, source_target_pairs={{0,2},{2,0},{1,3},{3,1},{4,6},{6,4},{5,7},{7,5},{8,10},{10,8},{9,1... | collective-permute-start | bytes 786440 | tf_op jit(solution)/shard_map/ppermute | solution.py:278
  27.4 1.6 %collective-permute-start.8 = (bf16[128,1024]{1,0:T(8,128)(2,1)S(1)}, bf16[128,1024]{1,0:T(8,128)(2,1)S(1)}, u32[]{:S(2)}, u32[]{:S(2)}) collective-permute-start(bf16[128,1024]{1,0:T(8,128)(2,1)S(1)} %shard_map.118.own_ref), channel_id=1, source_target_pairs={{0,1},{1,0},{2,3},{3,2},{4,5},{5,4},{6,7},{7,6},{8,9},{9,8},{10,11... | collective-permute-start | bytes 786440 | tf_op jit(solution)/shard_map/ppermute | solution.py:278
  30.1 8.6 %collective-permute-start.11 = (bf16[528,128]{1,0:T(8,128)(2,1)S(1)}, bf16[528,128]{1,0:T(8,128)(2,1)S(1)}, u32[]{:S(2)}, u32[]{:S(2)}) collective-permute-start(bf16[528,128]{1,0:T(8,128)(2,1)S(1)} %shard_map.122), channel_id=1, source_target_pairs={{0,4},{4,8},{8,12},{12,0},{1,5},{5,9},{9,13},{13,1},{2,6},{6,10},{... | collective-permute-start | bytes 405512 | tf_op jit(solution)/shard_map/ppermute | solution.py:278
  30.8 12.7 %collective-permute-start.10 = (bf16[528,128]{1,0:T(8,128)(2,1)S(1)}, bf16[528,128]{1,0:T(8,128)(2,1)S(1)}, u32[]{:S(2)}, u32[]{:S(2)}) collective-permute-start(bf16[528,128]{1,0:T(8,128)(2,1)S(1)} %shard_map.121), channel_id=1, source_target_pairs={{0,8},{4,12},{8,0},{12,4},{1,9},{5,13},{9,1},{13,5},{2,10},{6,14},... | collective-permute-start | bytes 405512 | tf_op jit(solution)/shard_map/ppermute | solution.py:278
  33.9 13.8 %copy-start = (f32[128]{0:T(128)S(1)}, f32[128]{0:T(128)}, u32[]{:S(2)}) copy-start(f32[128]{0:T(128)} %param.19) | copy-start | bytes 1540
  33.9 11.7 %collective-permute-start.9 = (bf16[528,128]{1,0:T(8,128)(2,1)S(1)}, bf16[528,128]{1,0:T(8,128)(2,1)S(1)}, u32[]{:S(2)}, u32[]{:S(2)}) collective-permute-start(bf16[528,128]{1,0:T(8,128)(2,1)S(1)} %shard_map.120), channel_id=1, source_target_pairs={{0,12},{4,0},{8,4},{12,8},{1,13},{5,1},{9,5},{13,9},{2,14},{6,2},{... | collective-permute-start | bytes 405512 | tf_op jit(solution)/shard_map/ppermute | solution.py:278
  48.9 6.1 %collective-permute-start.12 = (bf16[128,256]{1,0:T(8,128)(2,1)S(1)}, bf16[128,256]{1,0:T(8,128)(2,1)S(1)}, u32[]{:S(2)}, u32[]{:S(2)}) collective-permute-start(bf16[128,256]{1,0:T(8,128)(2,1)S(1)} %get-tuple-element.109), channel_id=1, source_target_pairs={{0,12},{4,0},{8,4},{12,8},{1,13},{5,1},{9,5},{13,9},{2,14},{6,2},{... | collective-permute-start | bytes 196616 | tf_op jit(solution)/shard_map/ppermute | solution.py:278
  52.4 5.4 %collective-permute-start.13 = (bf16[128,256]{1,0:T(8,128)(2,1)S(1)}, bf16[128,256]{1,0:T(8,128)(2,1)S(1)}, u32[]{:S(2)}, u32[]{:S(2)}) collective-permute-start(bf16[128,256]{1,0:T(8,128)(2,1)S(1)} %get-tuple-element.110), channel_id=1, source_target_pairs={{0,8},{4,12},{8,0},{12,4},{1,9},{5,13},{9,1},{13,5},{2,10},{6,14},... | collective-permute-start | bytes 196616 | tf_op jit(solution)/shard_map/ppermute | solution.py:278
  52.4 6.1 %collective-permute-start.14 = (bf16[128,256]{1,0:T(8,128)(2,1)S(1)}, bf16[128,256]{1,0:T(8,128)(2,1)S(1)}, u32[]{:S(2)}, u32[]{:S(2)}) collective-permute-start(bf16[128,256]{1,0:T(8,128)(2,1)S(1)} %get-tuple-element.111), channel_id=1, source_target_pairs={{0,4},{4,8},{8,12},{12,0},{1,5},{5,9},{9,13},{13,1},{2,6},{6,10},{... | collective-permute-start | bytes 196616 | tf_op jit(solution)/shard_map/ppermute | solution.py:278

commit v3 on v2

--- a/solution.py
+++ b/solution.py
@@ -273,9 +273,8 @@
     )(*[in_vmem(operand) for operand in operands])
 
 
-def rotated(value, axis, steps):
-    count = lax.axis_size(axis)
-    return lax.ppermute(value, axis, [(i, (i + steps) % count) for i in range(count)])
+def swapped(value, axis, mask=1):
+    return lax.ppermute(value, axis, [(i, i ^ mask) for i in range(lax.axis_size(axis))])
 
 
 def dot(left, right, dims=((1,), (0,))):
@@ -301,15 +300,11 @@
     return value / (1.0 + jnp.exp(-value))
 
 
-def piece_kernel(kv_ref, piece_ref, own_ref, sems):
-    start = pl.multiple_of(lax.axis_index("head") * 2 * HD, 2 * HD)
-    share = pl.multiple_of(start + lax.axis_index("sub") * HD, HD)
-    first = pltpu.make_async_copy(kv_ref.at[:, pl.ds(share, HD)], piece_ref, sems.at[0])
-    second = pltpu.make_async_copy(kv_ref.at[:, pl.ds(start, 2 * HD)], own_ref, sems.at[1])
-    first.start()
-    second.start()
-    first.wait()
-    second.wait()
+def piece_kernel(kv_ref, piece_ref, sem):
+    start = (lax.axis_index("head") * 2 + lax.axis_index("sub")) * HD
+    copy = pltpu.make_async_copy(kv_ref.at[:, pl.ds(pl.multiple_of(start, HD), HD)], piece_ref, sem)
+    copy.start()
+    copy.wait()
 
 
 def fetch_kernel(*refs):
@@ -337,36 +332,37 @@
 
 
 def attention_kernel(
-    query_ref, gate_ref, own_ref, mine1, mine2, mine3, twin1, twin2, twin3, weight_ref, residual_ref,
-    keep_ref, send_ref, keys, values, heads, partial,
+    query_ref, gate_ref, kv_ref, mine1, mine2, mine3, twin1, twin2, twin3, weight_ref, residual_ref,
+    heads_ref, send_ref, keys, values, sums,
 ):
     rows, head_columns = query_ref.shape
     half = rows // 2
     ctx_rank, head_rank, sub_rank = (lax.axis_index(name) for name in ("ctx", "head", "sub"))
     count = 4
-    keys[0:rows] = own_ref[:, 0:HD]
-    values[0:rows] = own_ref[:, HD : 2 * HD]
+    own_start = pl.multiple_of(head_rank * 2 * HD, 2 * HD)
+    keys[0:rows] = kv_ref[:, pl.ds(own_start, HD)]
+    values[0:rows] = kv_ref[:, pl.ds(own_start + HD, HD)]
 
     @pl.when(sub_rank == 0)
     def _():
-        for step, (mine, twin) in enumerate(((mine1, twin1), (mine2, twin2), (mine3, twin3)), 1):
-            keys[step * rows : (step + 1) * rows] = mine[...]
-            values[step * rows : (step + 1) * rows] = twin[...]
+        for mask, (mine, twin) in enumerate(((mine1, twin1), (mine2, twin2), (mine3, twin3)), 1):
+            keys[mask * rows : (mask + 1) * rows] = mine[...]
+            values[mask * rows : (mask + 1) * rows] = twin[...]
 
     @pl.when(sub_rank != 0)
     def _():
-        for step, (mine, twin) in enumerate(((mine1, twin1), (mine2, twin2), (mine3, twin3)), 1):
-            keys[step * rows : (step + 1) * rows] = twin[...]
-            values[step * rows : (step + 1) * rows] = mine[...]
+        for mask, (mine, twin) in enumerate(((mine1, twin1), (mine2, twin2), (mine3, twin3)), 1):
+            keys[mask * rows : (mask + 1) * rows] = twin[...]
+            values[mask * rows : (mask + 1) * rows] = mine[...]
 
     def places(row, device):
-        within = row % rows
+        within = row & (rows - 1)
         block = jnp.where(within < half, device, 2 * count - 1 - device)
-        return block * half + within % half
+        return block * half + (within & (half - 1))
 
     query_place = places(lax.broadcasted_iota(jnp.int32, (rows, 1), 0), ctx_rank)
     key_row = lax.broadcasted_iota(jnp.int32, (1, count * rows), 1)
-    key_place = places(key_row, (ctx_rank - key_row // rows + count) % count)
+    key_place = places(key_row, jnp.bitwise_xor(ctx_rank, key_row >> (rows.bit_length() - 1)))
     visible = query_place >= key_place
     for head in range(head_columns // HD):
         columns = slice(head * HD, (head + 1) * HD)
@@ -376,14 +372,27 @@
         total = jnp.sum(weights, axis=1, keepdims=True)
         gathered = dot(weights.astype(jnp.bfloat16), values[...])
         gate = sigmoid(gate_ref[:, columns].astype(jnp.float32))
-        heads[:, columns] = (gathered / total * gate).astype(jnp.bfloat16)
-    partial[...] = dot(heads[...], weight_ref[...])
+        heads_ref[:, columns] = (gathered / total * gate).astype(jnp.bfloat16)
+    mid = send_ref.shape[1]
     width = residual_ref.shape[1]
-    mid = partial.shape[1] // 2
-    own_columns = pl.ds(pl.multiple_of((head_rank * 2 + sub_rank) * width, width), width)
-    partial[:, own_columns] += residual_ref[...].astype(jnp.float32)
-    keep_ref[...] = partial[:, pl.ds(pl.multiple_of(sub_rank * mid, mid), mid)]
-    send_ref[...] = partial[:, pl.ds(pl.multiple_of((1 - sub_rank) * mid, mid), mid)].astype(jnp.bfloat16)
+    sums[...] = dot(heads_ref[...], weight_ref[:, pl.ds(pl.multiple_of((1 - sub_rank) * mid, mid), mid)])
+
+    @pl.when(sub_rank != head_rank)
+    def _():
+        sums[:, pl.ds(pl.multiple_of(sub_rank * width, width), width)] += residual_ref[...].astype(jnp.float32)
+
+    send_ref[...] = sums[...].astype(jnp.bfloat16)
+
+
+def keep_kernel(heads_ref, weight_ref, residual_ref, keep_ref):
+    head_rank, sub_rank = lax.axis_index("head"), lax.axis_index("sub")
+    mid = keep_ref.shape[1]
+    width = residual_ref.shape[1]
+    keep_ref[...] = dot(heads_ref[...], weight_ref[:, pl.ds(pl.multiple_of(sub_rank * mid, mid), mid)])
+
+    @pl.when(sub_rank == head_rank)
+    def _():
+        keep_ref[:, pl.ds(pl.multiple_of(sub_rank * width, width), width)] += residual_ref[...].astype(jnp.float32)
 
 
 def chip_sum_kernel(keep_ref, came_ref, sum_ref, send_ref):
@@ -396,9 +405,42 @@
     hidden_ref[...] = (keep_ref[...] + came_ref[...].astype(jnp.float32)).astype(jnp.bfloat16)
 
 
-def norm_kernel(own_ref, twin_ref, gain_ref, beta_ref, decay_ref, residual_ref, normed_ref, extra_ref):
+def half_of(ref, own):
+    sub_rank = lax.axis_index("sub")
+    mid = ref.shape[-1] // 2
+    return pl.ds(pl.multiple_of((sub_rank if own else 1 - sub_rank) * mid, mid), mid)
+
+
+def own_half_kernel(own_ref, gain_ref, weight_ref, beta_ref, mixed_ref, logit_ref, square_ref):
+    mid = own_ref.shape[1]
+    own = own_ref[...].astype(jnp.float32)
+    columns = half_of(gain_ref, True)
+    scaled = (own * gain_ref[:, columns]).astype(jnp.bfloat16)
+    square_ref[...] = jnp.broadcast_to(jnp.sum(own * own, axis=1, keepdims=True), square_ref.shape)
+    logit_ref[...] = dot(beta_ref[:, columns], scaled, ((1,), (1,)))
+    rows = pl.ds(pl.multiple_of(lax.axis_index("sub") * mid, mid), mid)
+    mixed_ref[...] = dot(scaled, weight_ref[rows, :])
+
+
+def twin_half_kernel(
+    twin_ref, gain_ref, beta_ref, decay_ref, logit_ref, square_ref, weight_ref, mixed_ref,
+    scaled_ref, scale_ref, extra_ref, payload_ref, small,
+):
+    twin = twin_ref[...].astype(jnp.float32)
+    columns = half_of(gain_ref, False)
+    scaled_ref[...] = (twin * gain_ref[:, columns]).astype(jnp.bfloat16)
+    squares = square_ref[...] + jnp.sum(twin * twin, axis=1, keepdims=True)
+    scale = lax.rsqrt(squares / gain_ref.shape[1] + EPSILON)
+    scale_ref[...] = scale
+    values = decay_ref.shape[0]
+    logits = logit_ref[...] + dot(beta_ref[:, columns], scaled_ref[...], ((1,), (1,)))
+    extra_ref[0:values] = decay_ref[...]
+    extra_ref[values : 2 * values] = sigmoid(logits * jnp.transpose(scale)[0:1])
+    payload_kernel(2, scaled_ref, scale_ref, weight_ref, mixed_ref, extra_ref, payload_ref, small)
+
+
+def residual_kernel(own_ref, twin_ref, residual_ref):
     head_rank, sub_rank = lax.axis_index("head"), lax.axis_index("sub")
-    mid = own_ref.shape[1]
     width = residual_ref.shape[1]
     columns = pl.ds(pl.multiple_of(sub_rank * width, width), width)
 
@@ -410,25 +452,15 @@
     def _():
         residual_ref[...] = twin_ref[:, columns]
 
-    own, twin = own_ref[...].astype(jnp.float32), twin_ref[...].astype(jnp.float32)
-    squares = jnp.sum(own * own, axis=1, keepdims=True) + jnp.sum(twin * twin, axis=1, keepdims=True)
-    scale = lax.rsqrt(squares / (2 * mid) + EPSILON)
-    own_half = pl.ds(pl.multiple_of(sub_rank * mid, mid), mid)
-    twin_half = pl.ds(pl.multiple_of((1 - sub_rank) * mid, mid), mid)
-    normed_ref[:, own_half] = (own * scale * gain_ref[:, own_half]).astype(jnp.bfloat16)
-    normed_ref[:, twin_half] = (twin * scale * gain_ref[:, twin_half]).astype(jnp.bfloat16)
-    values = decay_ref.shape[0]
-    extra_ref[0:values] = decay_ref[...]
-    extra_ref[values : 2 * values] = sigmoid(dot(beta_ref[...], normed_ref[...], ((1,), (1,))))
-
-
-def payload_kernel(step, normed_ref, weight_ref, extra_ref, payload_ref, small):
-    rows = normed_ref.shape[0]
+
+def payload_kernel(mask, scaled_ref, scale_ref, weight_ref, mixed_ref, extra_ref, payload_ref, small):
+    rows, mid = scaled_ref.shape
     group = 2 * DK + 2 * DV
-    count = 4
-    target = (lax.axis_index("ctx") + step) % count
+    target = jnp.bitwise_xor(lax.axis_index("ctx"), mask)
     columns = pl.ds(pl.multiple_of(target * group, group), group)
-    mixed = silu(dot(normed_ref[...], weight_ref[:, columns]))
+    weight_rows = pl.ds(pl.multiple_of((1 - lax.axis_index("sub")) * mid, mid), mid)
+    mixed = mixed_ref[:, columns] + dot(scaled_ref[...], weight_ref[weight_rows, columns])
+    mixed = silu(mixed * scale_ref[:, 0:1])
     query, key = mixed[:, :DK], mixed[:, DK : 2 * DK]
     payload_ref[0:rows] = (unit_rows(query) * DK ** (-0.5)).astype(jnp.bfloat16)
     payload_ref[rows : 2 * rows] = unit_rows(key).astype(jnp.bfloat16)
@@ -462,10 +494,9 @@
     return [result + dot3(quad, result) for result, quad in zip(results, quads)]
 
 
-def block_kernel(step, payload_ref, *refs):
+def block_kernel(mask, payload_ref, *refs):
     offset_ref, linear_ref, local_ref, growth_ref = refs[-4:]
-    count = 4
-    source = (lax.axis_index("ctx") + count - step) % count
+    source = jnp.bitwise_xor(lax.axis_index("ctx"), mask)
     rows = (payload_ref.shape[0] - 16) // 4
     half = rows // 2
     shift = half.bit_length() - 1
@@ -542,17 +573,20 @@
             scale = lax.rsqrt(jnp.mean(out * out, axis=1, keepdims=True) + EPSILON)
             outs[source, block_rows, head * DV : (head + 1) * DV] = (out * scale * gain_ref[...]).astype(jnp.bfloat16)
     own_ref[...] = outs[rank]
-    for step, back in enumerate((back1, back2, back3), 1):
-        back[...] = outs[(rank + count - step) % count]
-
-
-def place_kernel(own_ref, back1, back2, back3, out_ref):
-    count = 4
+    for mask, back in enumerate((back1, back2, back3), 1):
+        back[...] = outs[jnp.bitwise_xor(rank, mask)]
+
+
+def place_kernel(own_ref, back1, back2, back3, out_ref, sems):
     width = own_ref.shape[1]
     rank = lax.axis_index("ctx")
-    for step, back in enumerate((own_ref, back1, back2, back3)):
-        columns = pl.ds(pl.multiple_of((rank + step) % count * width, width), width)
-        out_ref[:, columns] = back[...]
+    copies = []
+    for mask, back in enumerate((own_ref, back1, back2, back3)):
+        columns = pl.ds(pl.multiple_of(jnp.bitwise_xor(rank, mask) * width, width), width)
+        copies.append(pltpu.make_async_copy(back, out_ref.at[:, columns], sems.at[mask]))
+        copies[-1].start()
+    for copy in copies:
+        copy.wait()
 
 
 def owner_local(
@@ -571,57 +605,67 @@
     rows, head_columns = att_query.shape
     model = out_weight.shape[1]
     half_model = model // 2
-    steps = (1, 2, 3)
-    piece, own_kv = pl.pallas_call(
+    value_here = log_decay.shape[1]
+    masks = (2, 3, 1)
+    piece = pl.pallas_call(
         piece_kernel,
-        out_shape=[pltpu.VMEM((rows, HD), bf16), pltpu.VMEM((rows, 2 * HD), bf16)],
+        out_shape=pltpu.VMEM((rows, HD), bf16),
         in_specs=[IN_HBM],
-        out_specs=[IN_VMEM] * 2,
-        scratch_shapes=[pltpu.SemaphoreType.DMA((2,))],
+        out_specs=IN_VMEM,
+        scratch_shapes=[pltpu.SemaphoreType.DMA],
         compiler_params=pltpu.CompilerParams(vmem_limit_bytes=4 * MIB),
     )(in_hbm(att_kv))
-    mine = [rotated(piece, "ctx", step) for step in steps]
-    piece, *late = lax.optimization_barrier((piece, att_query, att_gate, out_weight, residual))
+    mine = {mask: swapped(piece, "ctx", mask) for mask in masks[::-1]}
+    piece, *late = lax.optimization_barrier((piece, att_query, att_gate, att_kv, out_weight, residual))
     late = fetched(*late)
-    mine[2], (att_query, att_gate, out_weight, residual) = lax.optimization_barrier((mine[2], late))
-    twin = [rotated(part, "sub", 1) for part in mine]
-    keep, send = vmem_call(
+    mine[2], (att_query, att_gate, att_kv, out_weight, residual) = lax.optimization_barrier((mine[2], late))
+    twin = {mask: swapped(mine[mask], "sub") for mask in masks}
+    heads, send = vmem_call(
         attention_kernel,
-        [((rows, half_model), f32), ((rows, half_model), bf16)],
-        [att_query, att_gate, own_kv, *mine, *twin, out_weight, residual],
+        [((rows, head_columns), bf16), ((rows, half_model), bf16)],
+        [att_query, att_gate, att_kv, mine[1], mine[2], mine[3], twin[1], twin[2], twin[3], out_weight, residual],
         [
             pltpu.VMEM((4 * rows, HD), bf16),
             pltpu.VMEM((4 * rows, HD), bf16),
-            pltpu.VMEM((rows, head_columns), bf16),
-            pltpu.VMEM((rows, model), f32),
+            pltpu.VMEM((rows, half_model), f32),
         ],
     )
+    came = swapped(send, "sub")
+    keep = vmem_call(keep_kernel, [((rows, half_model), f32)], [heads, out_weight, residual])[0]
+    came, keep = lax.optimization_barrier((came, keep))
     chip_sum, send = vmem_call(
-        chip_sum_kernel,
-        [((rows, half_model), f32), ((rows, half_model), bf16)],
-        [keep, rotated(send, "sub", 1)],
-    )
-    other_sum = rotated(send, "head", 1)
+        chip_sum_kernel, [((rows, half_model), f32), ((rows, half_model), bf16)], [keep, came]
+    )
+    came = swapped(send, "head")
     send, *late = lax.optimization_barrier((send, in_weight, norm_gain[None, :], beta_weight.T, log_decay.T))
     late = fetched(*late)
-    other_sum, (in_weight, norm_gain, beta_weight, log_decay) = lax.optimization_barrier((other_sum, late))
-    hidden = vmem_call(hidden_kernel, [((rows, half_model), bf16)], [chip_sum, other_sum])[0]
-    value_here = log_decay.shape[0]
-    new_residual, normed, extra = vmem_call(
-        norm_kernel,
-        [(residual.shape, bf16), ((rows, model), bf16), ((2 * value_here, rows), f32)],
-        [hidden, rotated(hidden, "sub", 1), norm_gain, beta_weight, log_decay],
-    )
-    payloads = [
-        vmem_call(
-            functools.partial(payload_kernel, step),
-            [((4 * rows + 16, LANES), bf16)],
-            [normed, in_weight, extra],
+    came, (in_weight, norm_gain, beta_weight, log_decay) = lax.optimization_barrier((came, late))
+    hidden = vmem_call(hidden_kernel, [((rows, half_model), bf16)], [chip_sum, came])[0]
+    twin_hidden = swapped(hidden, "sub")
+    sums = vmem_call(
+        own_half_kernel,
+        [((rows, in_weight.shape[1]), f32), ((value_here, rows), f32), ((rows, LANES), f32)],
+        [hidden, norm_gain, in_weight, beta_weight],
+    )
+    twin_hidden, (mixed, logits, squares) = lax.optimization_barrier((twin_hidden, sums))
+    payload_shape = ((4 * rows + 16, LANES), bf16)
+    payloads = {}
+    scaled, scale, extra, payloads[2] = vmem_call(
+        twin_half_kernel,
+        [((rows, half_model), bf16), ((rows, LANES), f32), ((2 * value_here, rows), f32), payload_shape],
+        [twin_hidden, norm_gain, beta_weight, log_decay, logits, squares, in_weight, mixed],
+        [pltpu.VMEM((16, LANES), f32)],
+    )
+    for mask in (3, 1, 0):
+        payloads[mask] = vmem_call(
+            functools.partial(payload_kernel, mask),
+            [payload_shape],
+            [scaled, scale, in_weight, mixed, extra],
             [pltpu.VMEM((16, LANES), f32)],
         )[0]
-        for step in range(4)
-    ]
-    came = [payloads[0]] + [rotated(payloads[step], "ctx", step) for step in steps]
+    new_residual = vmem_call(residual_kernel, [(residual.shape, bf16)], [hidden, twin_hidden], last=True)[0]
+    came = {mask: swapped(payloads[mask], "ctx", mask) for mask in masks}
+    came[0] = payloads[0]
     half = rows // 2
     terms_shapes = [
         ((4, 2, 2, DK, DV), f32),
@@ -630,11 +674,11 @@
         ((4, 2, 2, 8, LANES), f32),
     ]
     terms = []
-    for step in range(4):
+    for mask in (0, 2, 1, 3):
         terms = vmem_call(
-            functools.partial(block_kernel, step),
+            functools.partial(block_kernel, mask),
             terms_shapes,
-            [came[step], *terms],
+            [came[mask], *terms],
             aliases={1 + i: i for i in range(4)} if terms else None,
         )
     own, *backs = vmem_call(
@@ -643,8 +687,15 @@
         [*terms, delta_gain[None, :]],
         [pltpu.VMEM((4, rows, 2 * DV), bf16)],
     )
-    backs = [rotated(back, "ctx", -step) for step, back in zip(steps, backs)]
-    delta_out = vmem_call(place_kernel, [((rows, value_here * DV), bf16)], [own, *backs], last=True)[0]
+    backs = {mask: swapped(backs[mask - 1], "ctx", mask) for mask in masks}
+    delta_out = pl.pallas_call(
+        place_kernel,
+        out_shape=jax.ShapeDtypeStruct((rows, value_here * DV), bf16),
+        in_specs=[IN_VMEM] * 4,
+        out_specs=IN_HBM,
+        scratch_shapes=[pltpu.SemaphoreType.DMA((4,))],
+        compiler_params=pltpu.CompilerParams(vmem_limit_bytes=4 * MIB),
+    )(*[in_vmem(back) for back in (own, backs[1], backs[2], backs[3])])
     return (new_residual, delta_out)
 
 

time: 59.4 us -> 57 us (0.960)
  waiting for transfers between devices: 18 us -> 16.1 us
  local copies, waits for them, and re-layouts: 0.66 us -> 0.01 us
    ppermute x15, waiting for transfers between devices: 18 us -> 16.1 us  [swapped(): lax.ppermute(value, axis, [(i, i ^ mask) for i in range(lax.axis_size(axi...]
    unnamed x3 -> x2, local copies, waits for them, and re-layouts: 0.66 us -> 0.01 us
    pallas_call x1 -> x2, Pallas kernels: 1.02 us -> 1.59 us  [the longest x1 0.86 us: owner_local(): pl.pallas_call(piece_kernel, out_shape=pltpu.VMEM((rows, HD), bf16), in_s...]
    pallas_call x14 -> x15, Pallas kernels: 15.5 us -> 15.4 us  [vmem_call(): pl.pallas_call(kernel, out_shape=[make(shape, dtype) for shape, dtype in...]
  transfers between devices with their start and end apart: 15 -> 15, of which waited for: 11 -> 12; matrix products, arithmetic and copies ran while one was open for 1% -> 0% of each run, Pallas kernels for 23% -> 27%
where the time goes in v3:
time: 57 us; the launch traced here: 56.8 us
  Pallas kernels  22.9 us (40%)
  starting transfers between devices  17.1 us (30%)
  waiting for transfers between devices  16.1 us (28%)
  between operations  0.8 us (1%)
    ppermute x15, starting transfers between devices, swapped(): lax.ppermute(value, axis, [(i, i ^ mask) for i in range(lax.axis_size(axi...  17.1 us
    ppermute x15, waiting for transfers between devices, swapped(): lax.ppermute(value, axis, [(i, i ^ mask) for i in range(lax.axis_size(axi...  16.1 us
    pallas_call x15, Pallas kernels, vmem_call(): pl.pallas_call(kernel, out_shape=[make(shape, dtype) for shape, dtype in...  15.4 us
    pallas_call x2, Pallas kernels, fetched(): pl.pallas_call(fetch_kernel, out_shape=[pltpu.VMEM(array.shape, array.dty...  5.9 us
  transfers between devices with their start and end apart: 15, of which 12 were waited for; matrix products, arithmetic and copies ran while one was open for 0% of the time, Pallas kernels for 27%

profile of v3, /device:TPU:0, one launch (start us, length us, event | category | flops | bytes accessed | tf_op | source)
XLA Modules:
  0.0 56.8 jit_solution(15428734834458019183)
XLA Ops:
  0.6 0.9 %shard_map.113 = bf16[128,256]{1,0:T(8,128)(2,1)S(1)} custom-call(bf16[128,1024]{1,0:T(8,128)(2,1)} %refs_2_), custom_call_target="tpu_custom_call" | custom-call | tf_op jit(solution)/shard_map/pallas_call | solution.py:610
  1.5 4.1 %collective-permute-start = (bf16[128,256]{1,0:T(8,128)(2,1)S(1)}, bf16[128,256]{1,0:T(8,128)(2,1)S(1)}, u32[]{:S(2)}, u32[]{:S(2)}) collective-permute-start(bf16[128,256]{1,0:T(8,128)(2,1)S(1)} %shard_map.113), channel_id=1, source_target_pairs={{0,8},{4,12},{8,0},{12,4},{1,9},{5,13},{9,1},{13,5},{2,10},{6,14},... | collective-permute-start | bytes 196616 | tf_op jit(solution)/shard_map/ppermute | solution.py:277
  5.6 1.3 %collective-permute-start.2 = (bf16[128,256]{1,0:T(8,128)(2,1)S(1)}, bf16[128,256]{1,0:T(8,128)(2,1)S(1)}, u32[]{:S(2)}, u32[]{:S(2)}) collective-permute-start(bf16[128,256]{1,0:T(8,128)(2,1)S(1)} %shard_map.113), channel_id=1, source_target_pairs={{0,12},{4,8},{8,4},{12,0},{1,13},{5,9},{9,5},{13,1},{2,14},{6,10},... | collective-permute-start | bytes 196616 | tf_op jit(solution)/shard_map/ppermute | solution.py:277
  6.9 0.2 collective-permute-start.1
  7.2 2.5 %shard_map.114 = (bf16[128,1024]{1,0:T(8,128)(2,1)S(1)}, bf16[128,1024]{1,0:T(8,128)(2,1)S(1)}, bf16[128,1024]{1,0:T(8,128)(2,1)S(1)}, bf16[1024,2048]{1,0:T(8,128)(2,1)S(1)}, bf16[128,512]{1,0:T(8,128)(2,1)S(1)}) custom-call(bf16[128,1024]{1,0:T(8,128)(2,1)} %refs_0_, bf16[128,1024]{1,0:T(8,128)(2,1)} %refs_1_, bf16[128,1024]{1,0:T(8,128)(2,1)} %refs_2_, ...), custom_call_target="tpu_custom_call" | custom-call | bytes 5111808 | tf_op jit(solution)/shard_map/pallas_call | solution.py:323
  9.7 0.0 collective-permute-done.mine2
  9.7 2.1 %collective-permute-done.2.mine3 = bf16[128,256]{1,0:T(8,128)(2,1)S(1)} collective-permute-done((bf16[128,256]{1,0:T(8,128)(2,1)S(1)}, bf16[128,256]{1,0:T(8,128)(2,1)S(1)}, u32[]{:S(2)}, u32[]{:S(2)}) %collective-permute-start.2) | collective-permute-done | bytes 65568 | tf_op jit(solution)/shard_map/ppermute | solution.py:277
  11.8 0.1 collective-permute-done.1.mine1
  11.9 0.4 collective-permute-start.3
  12.3 0.1 collective-permute-start.4
  12.4 0.7 %collective-permute-done.5.twin3 = bf16[128,256]{1,0:T(8,128)(2,1)S(1)} collective-permute-done((bf16[128,256]{1,0:T(8,128)(2,1)S(1)}, bf16[128,256]{1,0:T(8,128)(2,1)S(1)}, u32[]{:S(2)}, u32[]{:S(2)}) %collective-permute-start.5) | collective-permute-done | bytes 65568 | tf_op jit(solution)/shard_map/ppermute | solution.py:277
  13.1 0.2 collective-permute-done.3.twin1
  13.2 0.4 collective-permute-done.4.twin2
  13.6 1.8 %shard_map.115 = (bf16[128,1024]{1,0:T(8,128)(2,1)S(1)}, bf16[128,1024]{1,0:T(8,128)(2,1)S(1)}) custom-call(bf16[128,1024]{1,0:T(8,128)(2,1)S(1)} %get-tuple-element.78.query_ref, bf16[128,1024]{1,0:T(8,128)(2,1)S(1)} %get-tuple-element.79.gate_ref, bf16[128,1024]{1,0:T(8,128)(2,1)S(1)} %get-tuple-element.80.kv_ref, ...), custom_call_target="tpu_custom_call" | custom-call | tf_op jit(solution)/shard_map/pallas_call | solution.py:264
  15.4 0.2 collective-permute-start.6
  15.7 0.5 shard_map.116.keep_ref
  16.1 0.9 %collective-permute-done.6.came_ref = bf16[128,1024]{1,0:T(8,128)(2,1)S(1)} collective-permute-done((bf16[128,1024]{1,0:T(8,128)(2,1)S(1)}, bf16[128,1024]{1,0:T(8,128)(2,1)S(1)}, u32[]{:S(2)}, u32[]{:S(2)}) %collective-permute-start.6) | collective-permute-done | bytes 262176 | tf_op jit(solution)/shard_map/ppermute | solution.py:277
  17.0 0.1 shard_map.117
  17.1 1.6 %collective-permute-start.7 = (bf16[128,1024]{1,0:T(8,128)(2,1)S(1)}, bf16[128,1024]{1,0:T(8,128)(2,1)S(1)}, u32[]{:S(2)}, u32[]{:S(2)}) collective-permute-start(bf16[128,1024]{1,0:T(8,128)(2,1)S(1)} %get-tuple-element.89), channel_id=1, source_target_pairs={{0,2},{2,0},{1,3},{3,1},{4,6},{6,4},{5,7},{7,5},{8,10},{10,8},{9,1... | collective-permute-start | bytes 786440 | tf_op jit(solution)/shard_map/ppermute | solution.py:277
  18.7 3.4 %shard_map.118 = (bf16[2048,2048]{1,0:T(8,128)(2,1)S(1)}, f32[1,2048]{1,0:T(1,128)S(1)}, bf16[8,2048]{1,0:T(8,128)(2,1)S(1)}, f32[8,128]{1,0:T(8,128)S(1)}) custom-call(bf16[2048,2048]{1,0:T(8,128)(2,1)} %refs_0_.1, f32[1,2048]{1,0:T(1,128)} %bitcast.6, bf16[8,2048]{1,0:T(8,128)(2,1)} %bitcast.5, f32[8,128]{1,0:T(8,128)} %bitcast.7), custom_call_target="tpu_custom_call" | custom-call | bytes 8433664 | tf_op jit(solution)/shard_map/pallas_call | solution.py:323
  22.1 3.5 %collective-permute-done.7.came_ref = bf16[128,1024]{1,0:T(8,128)(2,1)S(1)} collective-permute-done((bf16[128,1024]{1,0:T(8,128)(2,1)S(1)}, bf16[128,1024]{1,0:T(8,128)(2,1)S(1)}, u32[]{:S(2)}, u32[]{:S(2)}) %collective-permute-start.7) | collective-permute-done | bytes 262176 | tf_op jit(solution)/shard_map/ppermute | solution.py:277
  25.6 0.1 collective-permute-start.8
  25.7 0.8 %shard_map.120 = (f32[128,2048]{1,0:T(8,128)S(1)}, f32[8,128]{1,0:T(8,128)S(1)}, f32[128,128]{1,0:T(8,128)S(1)}) custom-call(bf16[128,1024]{1,0:T(8,128)(2,1)S(1)} %shard_map.119.own_ref, f32[1,2048]{1,0:T(1,128)S(1)} %get-tuple-element.99.gain_ref, bf16[2048,2048]{1,0:T(8,128)(2,1)S(1)} %get-tuple-element.100.weight_ref, ...), custom_call_target="tpu_custom_call" | custom-call | tf_op jit(solution)/shard_map/pallas_call | solution.py:264
  26.5 0.7 %collective-permute-done.8.twin_ref = bf16[128,1024]{1,0:T(8,128)(2,1)S(1)} collective-permute-done((bf16[128,1024]{1,0:T(8,128)(2,1)S(1)}, bf16[128,1024]{1,0:T(8,128)(2,1)S(1)}, u32[]{:S(2)}, u32[]{:S(2)}) %collective-permute-start.8) | collective-permute-done | bytes 262176 | tf_op jit(solution)/shard_map/ppermute | solution.py:277
  27.2 0.6 shard_map.122
  27.8 2.8 %collective-permute-start.11 = (bf16[528,128]{1,0:T(8,128)(2,1)S(1)}, bf16[528,128]{1,0:T(8,128)(2,1)S(1)}, u32[]{:S(2)}, u32[]{:S(2)}) collective-permute-start(bf16[528,128]{1,0:T(8,128)(2,1)S(1)} %get-tuple-element.113), channel_id=1, source_target_pairs={{0,8},{4,12},{8,0},{12,4},{1,9},{5,13},{9,1},{13,5},{2,10},{6,14},... | collective-permute-start | bytes 405512 | tf_op jit(solution)/shard_map/ppermute | solution.py:277
  30.6 0.5 shard_map.124
  31.1 0.8 %collective-permute-start.10 = (bf16[528,128]{1,0:T(8,128)(2,1)S(1)}, bf16[528,128]{1,0:T(8,128)(2,1)S(1)}, u32[]{:S(2)}, u32[]{:S(2)}) collective-permute-start(bf16[528,128]{1,0:T(8,128)(2,1)S(1)} %shard_map.124), channel_id=1, source_target_pairs={{0,4},{4,0},{8,12},{12,8},{1,5},{5,1},{9,13},{13,9},{2,6},{6,2},{1... | collective-permute-start | bytes 405512 | tf_op jit(solution)/shard_map/ppermute | solution.py:277
  31.8 0.5 shard_map.123
  32.3 0.0 copy-start
  32.3 1.0 %collective-permute-start.9 = (bf16[528,128]{1,0:T(8,128)(2,1)S(1)}, bf16[528,128]{1,0:T(8,128)(2,1)S(1)}, u32[]{:S(2)}, u32[]{:S(2)}) collective-permute-start(bf16[528,128]{1,0:T(8,128)(2,1)S(1)} %shard_map.123), channel_id=1, source_target_pairs={{0,12},{4,8},{8,4},{12,0},{1,13},{5,9},{9,5},{13,1},{2,14},{6,10},... | collective-permute-start | bytes 405512 | tf_op jit(solution)/shard_map/ppermute | solution.py:277
  33.3 0.5 shard_map.125.payload_ref
  33.7 2.1 %shard_map.126 = (f32[4,2,2,128,128]{4,3,2,1,0:T(8,128)S(1)}, bf16[4,2,2,192,128]{4,3,2,1,0:T(8,128)(2,1)S(1)}, f32[4,2,128,128]{3,2,1,0:T(8,128)S(1)}, f32[4,2,2,8,128]{4,3,2,1,0:T(8,128)S(1)}) custom-call(bf16[528,128]{1,0:T(8,128)(2,1)S(1)} %shard_map.125.payload_ref), custom_call_target="tpu_custom_call" | custom-call | tf_op jit(solution)/shard_map/pallas_call | solution.py:264
  35.8 2.7 %collective-permute-done.11.payload_ref = bf16[528,128]{1,0:T(8,128)(2,1)S(1)} collective-permute-done((bf16[528,128]{1,0:T(8,128)(2,1)S(1)}, bf16[528,128]{1,0:T(8,128)(2,1)S(1)}, u32[]{:S(2)}, u32[]{:S(2)}) %collective-permute-start.11) | collective-permute-done | bytes 135200 | tf_op jit(solution)/shard_map/ppermute | solution.py:277
  38.5 2.1 %shard_map.127 = (f32[4,2,2,128,128]{4,3,2,1,0:T(8,128)S(1)}, bf16[4,2,2,192,128]{4,3,2,1,0:T(8,128)(2,1)S(1)}, f32[4,2,128,128]{3,2,1,0:T(8,128)S(1)}, f32[4,2,2,8,128]{4,3,2,1,0:T(8,128)S(1)}) custom-call(bf16[528,128]{1,0:T(8,128)(2,1)S(1)} %collective-permute-done.11.payload_ref, ...), custom_call_target="tpu_custom_call", output_to_operand_aliasing={{0}: (1, {}), {1}: (2, {}), {2}: (3, {}), {3}: (4, {})} | custom-call | tf_op jit(solution)/shard_map/pallas_call | solution.py:264
  40.6 1.4 %collective-permute-done.10.payload_ref = bf16[528,128]{1,0:T(8,128)(2,1)S(1)} collective-permute-done((bf16[528,128]{1,0:T(8,128)(2,1)S(1)}, bf16[528,128]{1,0:T(8,128)(2,1)S(1)}, u32[]{:S(2)}, u32[]{:S(2)}) %collective-permute-start.10) | collective-permute-done | bytes 135200 | tf_op jit(solution)/shard_map/ppermute | solution.py:277
  42.0 2.1 %shard_map.128 = (f32[4,2,2,128,128]{4,3,2,1,0:T(8,128)S(1)}, bf16[4,2,2,192,128]{4,3,2,1,0:T(8,128)(2,1)S(1)}, f32[4,2,128,128]{3,2,1,0:T(8,128)S(1)}, f32[4,2,2,8,128]{4,3,2,1,0:T(8,128)S(1)}) custom-call(bf16[528,128]{1,0:T(8,128)(2,1)S(1)} %collective-permute-done.10.payload_ref, ...), custom_call_target="tpu_custom_call", output_to_operand_aliasing={{0}: (1, {}), {1}: (2, {}), {2}: (3, {}), {3}: (4, {})} | custom-call | tf_op jit(solution)/shard_map/pallas_call | solution.py:264
  44.1 0.0 collective-permute-done.9.payload_ref
  44.1 2.1 %shard_map.129 = (f32[4,2,2,128,128]{4,3,2,1,0:T(8,128)S(1)}, bf16[4,2,2,192,128]{4,3,2,1,0:T(8,128)(2,1)S(1)}, f32[4,2,128,128]{3,2,1,0:T(8,128)S(1)}, f32[4,2,2,8,128]{4,3,2,1,0:T(8,128)S(1)}) custom-call(bf16[528,128]{1,0:T(8,128)(2,1)S(1)} %collective-permute-done.9.payload_ref, ...), custom_call_target="tpu_custom_call", output_to_operand_aliasing={{0}: (1, {}), {1}: (2, {}), {2}: (3, {}), {3}: (4, {})} | custom-call | tf_op jit(solution)/shard_map/pallas_call | solution.py:264
  46.2 1.2 %shard_map.130 = (bf16[128,256]{1,0:T(8,128)(2,1)S(1)}, bf16[128,256]{1,0:T(8,128)(2,1)S(1)}, bf16[128,256]{1,0:T(8,128)(2,1)S(1)}, bf16[128,256]{1,0:T(8,128)(2,1)S(1)}) custom-call(f32[4,2,2,128,128]{4,3,2,1,0:T(8,128)S(1)} %get-tuple-element.126.offset_ref, bf16[4,2,2,192,128]{4,3,2,1,0:T(8,128)(2,1)S(1)} %get-tuple-element.127.linear_ref, ...), custom_call_target="tpu_custom_call" | custom-call | tf_op jit(solution)/shard_map/pallas_call | solution.py:264
  47.4 0.1 collective-permute-start.12
  47.5 2.5 %collective-permute-start.13 = (bf16[128,256]{1,0:T(8,128)(2,1)S(1)}, bf16[128,256]{1,0:T(8,128)(2,1)S(1)}, u32[]{:S(2)}, u32[]{:S(2)}) collective-permute-start(bf16[128,256]{1,0:T(8,128)(2,1)S(1)} %get-tuple-element.132), channel_id=1, source_target_pairs={{0,8},{4,12},{8,0},{12,4},{1,9},{5,13},{9,1},{13,5},{2,10},{6,14},... | collective-permute-start | bytes 196616 | tf_op jit(solution)/shard_map/ppermute | solution.py:277
  49.9 1.9 %collective-permute-start.14 = (bf16[128,256]{1,0:T(8,128)(2,1)S(1)}, bf16[128,256]{1,0:T(8,128)(2,1)S(1)}, u32[]{:S(2)}, u32[]{:S(2)}) collective-permute-start(bf16[128,256]{1,0:T(8,128)(2,1)S(1)} %get-tuple-element.133), channel_id=1, source_target_pairs={{0,12},{4,8},{8,4},{12,0},{1,13},{5,9},{9,5},{13,1},{2,14},{6,10},... | collective-permute-start | bytes 196616 | tf_op jit(solution)/shard_map/ppermute | solution.py:277
  51.8 0.7 %shard_map.121 = bf16[128,512]{1,0:T(8,128)(2,1)} custom-call(bf16[128,1024]{1,0:T(8,128)(2,1)S(1)} %shard_map.119.own_ref, bf16[128,1024]{1,0:T(8,128)(2,1)S(1)} %collective-permute-done.8.twin_ref), custom_call_target="tpu_custom_call" | custom-call | tf_op jit(solution)/shard_map/pallas_call | solution.py:264
  52.5 0.0 collective-permute-done.12.back1
  52.5 2.2 %collective-permute-done.13.back2 = bf16[128,256]{1,0:T(8,128)(2,1)S(1)} collective-permute-done((bf16[128,256]{1,0:T(8,128)(2,1)S(1)}, bf16[128,256]{1,0:T(8,128)(2,1)S(1)}, u32[]{:S(2)}, u32[]{:S(2)}) %collective-permute-start.13) | collective-permute-done | bytes 65568 | tf_op jit(solution)/shard_map/ppermute | solution.py:277
  54.7 1.4 %collective-permute-done.14.back3 = bf16[128,256]{1,0:T(8,128)(2,1)S(1)} collective-permute-done((bf16[128,256]{1,0:T(8,128)(2,1)S(1)}, bf16[128,256]{1,0:T(8,128)(2,1)S(1)}, u32[]{:S(2)}, u32[]{:S(2)}) %collective-permute-start.14) | collective-permute-done | bytes 65568 | tf_op jit(solution)/shard_map/ppermute | solution.py:277
  56.1 0.7 %shard_map.131 = bf16[128,1024]{1,0:T(8,128)(2,1)} custom-call(bf16[128,256]{1,0:T(8,128)(2,1)S(1)} %get-tuple-element.130.own_ref, bf16[128,256]{1,0:T(8,128)(2,1)S(1)} %collective-permute-done.12.back1, bf16[128,256]{1,0:T(8,128)(2,1)S(1)} %collective-permute-done.13.back2, bf16[128,256]{1,0:T(8,128)(2,1)S(1)} %collective-permute-done.14.back3), custom_call_target="tpu_custom_call" | custom-call | tf_op jit(solution)/shard_map/pallas_call | solution.py:691
  (3 shorter events, 0.1 us)
Async XLA Ops:
  1.5 8.2 %collective-permute-start = (bf16[128,256]{1,0:T(8,128)(2,1)S(1)}, bf16[128,256]{1,0:T(8,128)(2,1)S(1)}, u32[]{:S(2)}, u32[]{:S(2)}) collective-permute-start(bf16[128,256]{1,0:T(8,128)(2,1)S(1)} %shard_map.113), channel_id=1, source_target_pairs={{0,8},{4,12},{8,0},{12,4},{1,9},{5,13},{9,1},{13,5},{2,10},{6,14},... | collective-permute-start | bytes 196616 | tf_op jit(solution)/shard_map/ppermute | solution.py:277
  5.6 6.2 %collective-permute-start.2 = (bf16[128,256]{1,0:T(8,128)(2,1)S(1)}, bf16[128,256]{1,0:T(8,128)(2,1)S(1)}, u32[]{:S(2)}, u32[]{:S(2)}) collective-permute-start(bf16[128,256]{1,0:T(8,128)(2,1)S(1)} %shard_map.113), channel_id=1, source_target_pairs={{0,12},{4,8},{8,4},{12,0},{1,13},{5,9},{9,5},{13,1},{2,14},{6,10},... | collective-permute-start | bytes 196616 | tf_op jit(solution)/shard_map/ppermute | solution.py:277
  6.9 5.0 %collective-permute-start.1 = (bf16[128,256]{1,0:T(8,128)(2,1)S(1)}, bf16[128,256]{1,0:T(8,128)(2,1)S(1)}, u32[]{:S(2)}, u32[]{:S(2)}) collective-permute-start(bf16[128,256]{1,0:T(8,128)(2,1)S(1)} %shard_map.113), channel_id=1, source_target_pairs={{0,4},{4,0},{8,12},{12,8},{1,5},{5,1},{9,13},{13,9},{2,6},{6,2},{1... | collective-permute-start | bytes 196616 | tf_op jit(solution)/shard_map/ppermute | solution.py:277
  11.8 1.3 %collective-permute-start.5 = (bf16[128,256]{1,0:T(8,128)(2,1)S(1)}, bf16[128,256]{1,0:T(8,128)(2,1)S(1)}, u32[]{:S(2)}, u32[]{:S(2)}) collective-permute-start(bf16[128,256]{1,0:T(8,128)(2,1)S(1)} %collective-permute-done.2.mine3), channel_id=1, source_target_pairs={{0,1},{1,0},{2,3},{3,2},{4,5},{5,4},{6,7},{7,6},{8,9},{9,8},{10,11... | collective-permute-start | bytes 196616 | tf_op jit(solution)/shard_map/ppermute | solution.py:277
  11.9 1.3 %collective-permute-start.3 = (bf16[128,256]{1,0:T(8,128)(2,1)S(1)}, bf16[128,256]{1,0:T(8,128)(2,1)S(1)}, u32[]{:S(2)}, u32[]{:S(2)}) collective-permute-start(bf16[128,256]{1,0:T(8,128)(2,1)S(1)} %collective-permute-done.1.mine1), channel_id=1, source_target_pairs={{0,1},{1,0},{2,3},{3,2},{4,5},{5,4},{6,7},{7,6},{8,9},{9,8},{10,11... | collective-permute-start | bytes 196616 | tf_op jit(solution)/shard_map/ppermute | solution.py:277
  12.3 1.3 %collective-permute-start.4 = (bf16[128,256]{1,0:T(8,128)(2,1)S(1)}, bf16[128,256]{1,0:T(8,128)(2,1)S(1)}, u32[]{:S(2)}, u32[]{:S(2)}) collective-permute-start(bf16[128,256]{1,0:T(8,128)(2,1)S(1)} %collective-permute-done.mine2), channel_id=1, source_target_pairs={{0,1},{1,0},{2,3},{3,2},{4,5},{5,4},{6,7},{7,6},{8,9},{9,8},{10,11... | collective-permute-start | bytes 196616 | tf_op jit(solution)/shard_map/ppermute | solution.py:277
  15.4 1.6 %collective-permute-start.6 = (bf16[128,1024]{1,0:T(8,128)(2,1)S(1)}, bf16[128,1024]{1,0:T(8,128)(2,1)S(1)}, u32[]{:S(2)}, u32[]{:S(2)}) collective-permute-start(bf16[128,1024]{1,0:T(8,128)(2,1)S(1)} %get-tuple-element.84), channel_id=1, source_target_pairs={{0,1},{1,0},{2,3},{3,2},{4,5},{5,4},{6,7},{7,6},{8,9},{9,8},{10,11... | collective-permute-start | bytes 786440 | tf_op jit(solution)/shard_map/ppermute | solution.py:277
  17.1 8.5 %collective-permute-start.7 = (bf16[128,1024]{1,0:T(8,128)(2,1)S(1)}, bf16[128,1024]{1,0:T(8,128)(2,1)S(1)}, u32[]{:S(2)}, u32[]{:S(2)}) collective-permute-start(bf16[128,1024]{1,0:T(8,128)(2,1)S(1)} %get-tuple-element.89), channel_id=1, source_target_pairs={{0,2},{2,0},{1,3},{3,1},{4,6},{6,4},{5,7},{7,5},{8,10},{10,8},{9,1... | collective-permute-start | bytes 786440 | tf_op jit(solution)/shard_map/ppermute | solution.py:277
  25.6 1.6 %collective-permute-start.8 = (bf16[128,1024]{1,0:T(8,128)(2,1)S(1)}, bf16[128,1024]{1,0:T(8,128)(2,1)S(1)}, u32[]{:S(2)}, u32[]{:S(2)}) collective-permute-start(bf16[128,1024]{1,0:T(8,128)(2,1)S(1)} %shard_map.119.own_ref), channel_id=1, source_target_pairs={{0,1},{1,0},{2,3},{3,2},{4,5},{5,4},{6,7},{7,6},{8,9},{9,8},{10,11... | collective-permute-start | bytes 786440 | tf_op jit(solution)/shard_map/ppermute | solution.py:277
  27.8 10.7 %collective-permute-start.11 = (bf16[528,128]{1,0:T(8,128)(2,1)S(1)}, bf16[528,128]{1,0:T(8,128)(2,1)S(1)}, u32[]{:S(2)}, u32[]{:S(2)}) collective-permute-start(bf16[528,128]{1,0:T(8,128)(2,1)S(1)} %get-tuple-element.113), channel_id=1, source_target_pairs={{0,8},{4,12},{8,0},{12,4},{1,9},{5,13},{9,1},{13,5},{2,10},{6,14},... | collective-permute-start | bytes 405512 | tf_op jit(solution)/shard_map/ppermute | solution.py:277
  31.1 10.9 %collective-permute-start.10 = (bf16[528,128]{1,0:T(8,128)(2,1)S(1)}, bf16[528,128]{1,0:T(8,128)(2,1)S(1)}, u32[]{:S(2)}, u32[]{:S(2)}) collective-permute-start(bf16[528,128]{1,0:T(8,128)(2,1)S(1)} %shard_map.124), channel_id=1, source_target_pairs={{0,4},{4,0},{8,12},{12,8},{1,5},{5,1},{9,13},{13,9},{2,6},{6,2},{1... | collective-permute-start | bytes 405512 | tf_op jit(solution)/shard_map/ppermute | solution.py:277
  32.3 13.9 %copy-start = (f32[128]{0:T(128)S(1)}, f32[128]{0:T(128)}, u32[]{:S(2)}) copy-start(f32[128]{0:T(128)} %param.19) | copy-start | bytes 1540
  32.3 11.8 %collective-permute-start.9 = (bf16[528,128]{1,0:T(8,128)(2,1)S(1)}, bf16[528,128]{1,0:T(8,128)(2,1)S(1)}, u32[]{:S(2)}, u32[]{:S(2)}) collective-permute-start(bf16[528,128]{1,0:T(8,128)(2,1)S(1)} %shard_map.123), channel_id=1, source_target_pairs={{0,12},{4,8},{8,4},{12,0},{1,13},{5,9},{9,5},{13,1},{2,14},{6,10},... | collective-permute-start | bytes 405512 | tf_op jit(solution)/shard_map/ppermute | solution.py:277
  47.4 5.1 %collective-permute-start.12 = (bf16[128,256]{1,0:T(8,128)(2,1)S(1)}, bf16[128,256]{1,0:T(8,128)(2,1)S(1)}, u32[]{:S(2)}, u32[]{:S(2)}) collective-permute-start(bf16[128,256]{1,0:T(8,128)(2,1)S(1)} %get-tuple-element.131), channel_id=1, source_target_pairs={{0,4},{4,0},{8,12},{12,8},{1,5},{5,1},{9,13},{13,9},{2,6},{6,2},{1... | collective-permute-start | bytes 196616 | tf_op jit(solution)/shard_map/ppermute | solution.py:277
  47.5 7.3 %collective-permute-start.13 = (bf16[128,256]{1,0:T(8,128)(2,1)S(1)}, bf16[128,256]{1,0:T(8,128)(2,1)S(1)}, u32[]{:S(2)}, u32[]{:S(2)}) collective-permute-start(bf16[128,256]{1,0:T(8,128)(2,1)S(1)} %get-tuple-element.132), channel_id=1, source_target_pairs={{0,8},{4,12},{8,0},{12,4},{1,9},{5,13},{9,1},{13,5},{2,10},{6,14},... | collective-permute-start | bytes 196616 | tf_op jit(solution)/shard_map/ppermute | solution.py:277
  49.9 6.2 %collective-permute-start.14 = (bf16[128,256]{1,0:T(8,128)(2,1)S(1)}, bf16[128,256]{1,0:T(8,128)(2,1)S(1)}, u32[]{:S(2)}, u32[]{:S(2)}) collective-permute-start(bf16[128,256]{1,0:T(8,128)(2,1)S(1)} %get-tuple-element.133), channel_id=1, source_target_pairs={{0,12},{4,8},{8,4},{12,0},{1,13},{5,9},{9,5},{13,1},{2,14},{6,10},... | collective-permute-start | bytes 196616 | tf_op jit(solution)/shard_map/ppermute | solution.py:277

commit v4 on v3

--- a/solution.py
+++ b/solution.py
@@ -286,12 +286,6 @@
     return high, (value - high.astype(jnp.float32)).astype(jnp.bfloat16)
 
 
-def dot3(left, right):
-    left_high, left_low = halves(left)
-    right_high, right_low = halves(right)
-    return dot(left_high, right_high) + (dot(left_high, right_low) + dot(left_low, right_high))
-
-
 def sigmoid(value):
     return 1.0 / (1.0 + jnp.exp(-value))
 
@@ -331,48 +325,60 @@
     )(*[in_hbm(array) for array in arrays])
 
 
+def attend(query_ref, gate_ref, keys, values, rows, key_total, visible):
+    count = query_ref.shape[1] // HD
+    columns = [slice(head * HD, (head + 1) * HD) for head in range(count)]
+    size = rows.stop - rows.start
+    queries = jnp.concatenate([query_ref[rows, part] for part in columns], axis=0)
+    gates = [sigmoid(gate_ref[rows, part].astype(jnp.float32)) for part in columns]
+    scores = dot(queries, keys[0:key_total], ((1,), (1,))) * HD ** (-0.5)
+    scores = jnp.where(jnp.concatenate([visible] * count, axis=0), scores, NEGATIVE)
+    weights = jnp.exp(scores - jnp.max(scores, axis=1, keepdims=True))
+    total = jnp.sum(weights, axis=1, keepdims=True)
+    gathered = dot(weights.astype(jnp.bfloat16), values[0:key_total]) / total
+    gated = [gathered[head * size : (head + 1) * size] * gates[head] for head in range(count)]
+    return jnp.concatenate(gated, axis=1).astype(jnp.bfloat16)
+
+
 def attention_kernel(
     query_ref, gate_ref, kv_ref, mine1, mine2, mine3, twin1, twin2, twin3, weight_ref, residual_ref,
     heads_ref, send_ref, keys, values, sums,
 ):
-    rows, head_columns = query_ref.shape
-    half = rows // 2
+    half = query_ref.shape[0] // 2
     ctx_rank, head_rank, sub_rank = (lax.axis_index(name) for name in ("ctx", "head", "sub"))
     count = 4
     own_start = pl.multiple_of(head_rank * 2 * HD, 2 * HD)
-    keys[0:rows] = kv_ref[:, pl.ds(own_start, HD)]
-    values[0:rows] = kv_ref[:, pl.ds(own_start + HD, HD)]
+
+    def put(target, mask, part):
+        target[mask * half : (mask + 1) * half] = part[0:half]
+        target[(count + mask) * half : (count + mask + 1) * half] = part[half : 2 * half]
+
+    put(keys, 0, kv_ref[:, pl.ds(own_start, HD)])
+    put(values, 0, kv_ref[:, pl.ds(own_start + HD, HD)])
 
     @pl.when(sub_rank == 0)
     def _():
         for mask, (mine, twin) in enumerate(((mine1, twin1), (mine2, twin2), (mine3, twin3)), 1):
-            keys[mask * rows : (mask + 1) * rows] = mine[...]
-            values[mask * rows : (mask + 1) * rows] = twin[...]
+            put(keys, mask, mine[...])
+            put(values, mask, twin[...])
 
     @pl.when(sub_rank != 0)
     def _():
         for mask, (mine, twin) in enumerate(((mine1, twin1), (mine2, twin2), (mine3, twin3)), 1):
-            keys[mask * rows : (mask + 1) * rows] = twin[...]
-            values[mask * rows : (mask + 1) * rows] = mine[...]
-
-    def places(row, device):
-        within = row & (rows - 1)
-        block = jnp.where(within < half, device, 2 * count - 1 - device)
-        return block * half + (within & (half - 1))
-
-    query_place = places(lax.broadcasted_iota(jnp.int32, (rows, 1), 0), ctx_rank)
-    key_row = lax.broadcasted_iota(jnp.int32, (1, count * rows), 1)
-    key_place = places(key_row, jnp.bitwise_xor(ctx_rank, key_row >> (rows.bit_length() - 1)))
-    visible = query_place >= key_place
-    for head in range(head_columns // HD):
-        columns = slice(head * HD, (head + 1) * HD)
-        scores = dot(query_ref[:, columns], keys[...], ((1,), (1,))) * HD ** (-0.5)
-        scores = jnp.where(visible, scores, NEGATIVE)
-        weights = jnp.exp(scores - jnp.max(scores, axis=1, keepdims=True))
-        total = jnp.sum(weights, axis=1, keepdims=True)
-        gathered = dot(weights.astype(jnp.bfloat16), values[...])
-        gate = sigmoid(gate_ref[:, columns].astype(jnp.float32))
-        heads_ref[:, columns] = (gathered / total * gate).astype(jnp.bfloat16)
+            put(keys, mask, twin[...])
+            put(values, mask, mine[...])
+
+    shift = half.bit_length() - 1
+    row = lax.broadcasted_iota(jnp.int32, (half, 1), 0)
+    column = lax.broadcasted_iota(jnp.int32, (1, 2 * count * half), 1)
+    device = jnp.bitwise_xor(ctx_rank, (column >> shift) & (count - 1))
+    block = jnp.where(column < count * half, device, 2 * count - 1 - device)
+    key_place = block * half + (column & (half - 1))
+    for part, block_here in enumerate((ctx_rank, 2 * count - 1 - ctx_rank)):
+        rows = slice(part * half, (part + 1) * half)
+        key_total = (part + 1) * count * half
+        visible = row + block_here * half >= key_place[:, :key_total]
+        heads_ref[rows] = attend(query_ref, gate_ref, keys, values, rows, key_total, visible)
     mid = send_ref.shape[1]
     width = residual_ref.shape[1]
     sums[...] = dot(heads_ref[...], weight_ref[:, pl.ds(pl.multiple_of((1 - sub_rank) * mid, mid), mid)])
@@ -476,22 +482,35 @@
     payload_ref[4 * rows : 4 * rows + 16] = small[...].astype(jnp.bfloat16)
 
 
+def joined(left, right):
+    (left_high, left_low), (right_high, right_low) = left, right
+    return dot(
+        jnp.concatenate([left_high, left_high, left_low], axis=1),
+        jnp.concatenate([right_high, right_low, right_high], axis=0),
+    )
+
+
 def unit_lower_inverses(stricts, row, column):
     inner = (row >> 3) == (column >> 3)
     identity = jnp.where(row == column, 1.0, 0.0)
+    number = range(len(stricts))
     smalls = [jnp.where(inner, strict, 0.0) for strict in stricts]
-    rests = [jnp.where(inner, 0.0, strict) for strict in stricts]
-    seconds = [dot3(small, small) for small in smalls]
-    inverses = [identity - small for small in smalls]
-    fourths = [dot3(second, second) for second in seconds]
-    inverses = [inverse + dot3(inverse, second) for inverse, second in zip(inverses, seconds)]
-    inverses = [inverse + dot3(inverse, fourth) for inverse, fourth in zip(inverses, fourths)]
-    steps = [dot3(inverse, rest) for inverse, rest in zip(inverses, rests)]
-    results = [inverse - dot3(step, inverse) for inverse, step in zip(inverses, steps)]
-    doubles = [dot3(step, step) for step in steps]
-    quads = [dot3(double, double) for double in doubles]
-    results = [result + dot3(double, result) for result, double in zip(results, doubles)]
-    return [result + dot3(quad, result) for result, quad in zip(results, quads)]
+    rests = [halves(jnp.where(inner, 0.0, strict)) for strict in stricts]
+    small = [halves(part) for part in smalls]
+    inverses = [identity - part for part in smalls]
+    split = [halves(inverse) for inverse in inverses]
+    seconds = [halves(joined(part, part)) for part in small]
+    fourths = [halves(joined(second, second)) for second in seconds]
+    inverses = [inverses[n] + joined(split[n], seconds[n]) for n in number]
+    split = [halves(inverse) for inverse in inverses]
+    inverses = [inverses[n] + joined(split[n], fourths[n]) for n in number]
+    split = [halves(inverse) for inverse in inverses]
+    steps = [halves(joined(split[n], rests[n])) for n in number]
+    doubles = [halves(joined(step, step)) for step in steps]
+    results = [inverses[n] - joined(steps[n], split[n]) for n in number]
+    quads = [halves(joined(double, double)) for double in doubles]
+    results = [results[n] + joined(doubles[n], halves(results[n])) for n in number]
+    return [results[n] + joined(quads[n], halves(results[n])) for n in number]
 
 
 def block_kernel(mask, payload_ref, *refs):

time: 57 us -> 56 us (0.982)
  Pallas kernels: 22.9 us -> 21.8 us
    pallas_call x15, Pallas kernels: 15.4 us -> 14.3 us  [vmem_call(): pl.pallas_call(kernel, out_shape=[make(shape, dtype) for shape, dtype in...]
where the time goes in v4:
time: 56 us; the launch traced here: 55.9 us
  Pallas kernels  21.8 us (39%)
  starting transfers between devices  17.1 us (31%)
  waiting for transfers between devices  16.1 us (29%)
  between operations  0.8 us (1%)
    ppermute x15, starting transfers between devices, swapped(): lax.ppermute(value, axis, [(i, i ^ mask) for i in range(lax.axis_size(axi...  17.1 us
    ppermute x15, waiting for transfers between devices, swapped(): lax.ppermute(value, axis, [(i, i ^ mask) for i in range(lax.axis_size(axi...  16.1 us
    pallas_call x15, Pallas kernels, vmem_call(): pl.pallas_call(kernel, out_shape=[make(shape, dtype) for shape, dtype in...  14.3 us
    pallas_call x2, Pallas kernels, fetched(): pl.pallas_call(fetch_kernel, out_shape=[pltpu.VMEM(array.shape, array.dty...  5.9 us
  transfers between devices with their start and end apart: 15, of which 12 were waited for; matrix products, arithmetic and copies ran while one was open for 0% of the time, Pallas kernels for 27%

profile of v4, /device:TPU:0, one launch (start us, length us, event | category | flops | bytes accessed | tf_op | source)
XLA Modules:
  0.0 55.9 jit_solution(8983394246049048669)
XLA Ops:
  0.6 0.9 %shard_map.113 = bf16[128,256]{1,0:T(8,128)(2,1)S(1)} custom-call(bf16[128,1024]{1,0:T(8,128)(2,1)} %refs_2_), custom_call_target="tpu_custom_call" | custom-call | tf_op jit(solution)/shard_map/pallas_call | solution.py:629
  1.5 4.1 %collective-permute-start = (bf16[128,256]{1,0:T(8,128)(2,1)S(1)}, bf16[128,256]{1,0:T(8,128)(2,1)S(1)}, u32[]{:S(2)}, u32[]{:S(2)}) collective-permute-start(bf16[128,256]{1,0:T(8,128)(2,1)S(1)} %shard_map.113), channel_id=1, source_target_pairs={{0,8},{4,12},{8,0},{12,4},{1,9},{5,13},{9,1},{13,5},{2,10},{6,14},... | collective-permute-start | bytes 196616 | tf_op jit(solution)/shard_map/ppermute | solution.py:277
  5.6 1.3 %collective-permute-start.2 = (bf16[128,256]{1,0:T(8,128)(2,1)S(1)}, bf16[128,256]{1,0:T(8,128)(2,1)S(1)}, u32[]{:S(2)}, u32[]{:S(2)}) collective-permute-start(bf16[128,256]{1,0:T(8,128)(2,1)S(1)} %shard_map.113), channel_id=1, source_target_pairs={{0,12},{4,8},{8,4},{12,0},{1,13},{5,9},{9,5},{13,1},{2,14},{6,10},... | collective-permute-start | bytes 196616 | tf_op jit(solution)/shard_map/ppermute | solution.py:277
  6.9 0.2 collective-permute-start.1
  7.2 2.5 %shard_map.114 = (bf16[128,1024]{1,0:T(8,128)(2,1)S(1)}, bf16[128,1024]{1,0:T(8,128)(2,1)S(1)}, bf16[128,1024]{1,0:T(8,128)(2,1)S(1)}, bf16[1024,2048]{1,0:T(8,128)(2,1)S(1)}, bf16[128,512]{1,0:T(8,128)(2,1)S(1)}) custom-call(bf16[128,1024]{1,0:T(8,128)(2,1)} %refs_0_, bf16[128,1024]{1,0:T(8,128)(2,1)} %refs_1_, bf16[128,1024]{1,0:T(8,128)(2,1)} %refs_2_, ...), custom_call_target="tpu_custom_call" | custom-call | bytes 5111808 | tf_op jit(solution)/shard_map/pallas_call | solution.py:317
  9.7 0.0 collective-permute-done.mine2
  9.7 2.1 %collective-permute-done.2.mine3 = bf16[128,256]{1,0:T(8,128)(2,1)S(1)} collective-permute-done((bf16[128,256]{1,0:T(8,128)(2,1)S(1)}, bf16[128,256]{1,0:T(8,128)(2,1)S(1)}, u32[]{:S(2)}, u32[]{:S(2)}) %collective-permute-start.2) | collective-permute-done | bytes 65568 | tf_op jit(solution)/shard_map/ppermute | solution.py:277
  11.8 0.0 collective-permute-start.5
  11.8 0.1 collective-permute-done.1.mine1
  11.9 0.4 collective-permute-start.3
  12.3 0.1 collective-permute-start.4
  12.4 0.7 %collective-permute-done.5.twin3 = bf16[128,256]{1,0:T(8,128)(2,1)S(1)} collective-permute-done((bf16[128,256]{1,0:T(8,128)(2,1)S(1)}, bf16[128,256]{1,0:T(8,128)(2,1)S(1)}, u32[]{:S(2)}, u32[]{:S(2)}) %collective-permute-start.5) | collective-permute-done | bytes 65568 | tf_op jit(solution)/shard_map/ppermute | solution.py:277
  13.1 0.2 collective-permute-done.3.twin1
  13.2 0.4 collective-permute-done.4.twin2
  13.6 1.2 %shard_map.115 = (bf16[128,1024]{1,0:T(8,128)(2,1)S(1)}, bf16[128,1024]{1,0:T(8,128)(2,1)S(1)}) custom-call(bf16[128,1024]{1,0:T(8,128)(2,1)S(1)} %get-tuple-element.78.query_ref, bf16[128,1024]{1,0:T(8,128)(2,1)S(1)} %get-tuple-element.79.gate_ref, bf16[128,1024]{1,0:T(8,128)(2,1)S(1)} %get-tuple-element.80.kv_ref, ...), custom_call_target="tpu_custom_call" | custom-call | tf_op jit(solution)/shard_map/pallas_call | solution.py:264
  14.8 0.2 collective-permute-start.6
  15.1 0.5 shard_map.116.keep_ref
  15.6 0.9 %collective-permute-done.6.came_ref = bf16[128,1024]{1,0:T(8,128)(2,1)S(1)} collective-permute-done((bf16[128,1024]{1,0:T(8,128)(2,1)S(1)}, bf16[128,1024]{1,0:T(8,128)(2,1)S(1)}, u32[]{:S(2)}, u32[]{:S(2)}) %collective-permute-start.6) | collective-permute-done | bytes 262176 | tf_op jit(solution)/shard_map/ppermute | solution.py:277
  16.4 0.1 shard_map.117
  16.5 1.6 %collective-permute-start.7 = (bf16[128,1024]{1,0:T(8,128)(2,1)S(1)}, bf16[128,1024]{1,0:T(8,128)(2,1)S(1)}, u32[]{:S(2)}, u32[]{:S(2)}) collective-permute-start(bf16[128,1024]{1,0:T(8,128)(2,1)S(1)} %get-tuple-element.89), channel_id=1, source_target_pairs={{0,2},{2,0},{1,3},{3,1},{4,6},{6,4},{5,7},{7,5},{8,10},{10,8},{9,1... | collective-permute-start | bytes 786440 | tf_op jit(solution)/shard_map/ppermute | solution.py:277
  18.1 3.4 %shard_map.118 = (bf16[2048,2048]{1,0:T(8,128)(2,1)S(1)}, f32[1,2048]{1,0:T(1,128)S(1)}, bf16[8,2048]{1,0:T(8,128)(2,1)S(1)}, f32[8,128]{1,0:T(8,128)S(1)}) custom-call(bf16[2048,2048]{1,0:T(8,128)(2,1)} %refs_0_.1, f32[1,2048]{1,0:T(1,128)} %bitcast.6, bf16[8,2048]{1,0:T(8,128)(2,1)} %bitcast.5, f32[8,128]{1,0:T(8,128)} %bitcast.7), custom_call_target="tpu_custom_call" | custom-call | bytes 8433664 | tf_op jit(solution)/shard_map/pallas_call | solution.py:317
  21.5 3.5 %collective-permute-done.7.came_ref = bf16[128,1024]{1,0:T(8,128)(2,1)S(1)} collective-permute-done((bf16[128,1024]{1,0:T(8,128)(2,1)S(1)}, bf16[128,1024]{1,0:T(8,128)(2,1)S(1)}, u32[]{:S(2)}, u32[]{:S(2)}) %collective-permute-start.7) | collective-permute-done | bytes 262176 | tf_op jit(solution)/shard_map/ppermute | solution.py:277
  25.0 0.1 collective-permute-start.8
  25.1 0.8 %shard_map.120 = (f32[128,2048]{1,0:T(8,128)S(1)}, f32[8,128]{1,0:T(8,128)S(1)}, f32[128,128]{1,0:T(8,128)S(1)}) custom-call(bf16[128,1024]{1,0:T(8,128)(2,1)S(1)} %shard_map.119.own_ref, f32[1,2048]{1,0:T(1,128)S(1)} %get-tuple-element.99.gain_ref, bf16[2048,2048]{1,0:T(8,128)(2,1)S(1)} %get-tuple-element.100.weight_ref, ...), custom_call_target="tpu_custom_call" | custom-call | tf_op jit(solution)/shard_map/pallas_call | solution.py:264
  25.9 0.7 %collective-permute-done.8.twin_ref = bf16[128,1024]{1,0:T(8,128)(2,1)S(1)} collective-permute-done((bf16[128,1024]{1,0:T(8,128)(2,1)S(1)}, bf16[128,1024]{1,0:T(8,128)(2,1)S(1)}, u32[]{:S(2)}, u32[]{:S(2)}) %collective-permute-start.8) | collective-permute-done | bytes 262176 | tf_op jit(solution)/shard_map/ppermute | solution.py:277
  26.6 0.6 %shard_map.122 = (bf16[128,1024]{1,0:T(8,128)(2,1)S(1)}, f32[128,128]{1,0:T(8,128)S(1)}, f32[16,128]{1,0:T(8,128)S(1)}, bf16[528,128]{1,0:T(8,128)(2,1)S(1)}) custom-call(bf16[128,1024]{1,0:T(8,128)(2,1)S(1)} %collective-permute-done.8.twin_ref, f32[1,2048]{1,0:T(1,128)S(1)} %get-tuple-element.99.gain_ref, bf16[8,2048]{1,0:T(8,128)(2,1)S(1)} %get-tuple-element.101.beta_ref, ...), custom_call_target="tpu_custom_call" | custom-call | tf_op jit(solution)/shard_map/pallas_call | solution.py:264
  27.2 2.8 %collective-permute-start.11 = (bf16[528,128]{1,0:T(8,128)(2,1)S(1)}, bf16[528,128]{1,0:T(8,128)(2,1)S(1)}, u32[]{:S(2)}, u32[]{:S(2)}) collective-permute-start(bf16[528,128]{1,0:T(8,128)(2,1)S(1)} %get-tuple-element.113), channel_id=1, source_target_pairs={{0,8},{4,12},{8,0},{12,4},{1,9},{5,13},{9,1},{13,5},{2,10},{6,14},... | collective-permute-start | bytes 405512 | tf_op jit(solution)/shard_map/ppermute | solution.py:277
  30.0 0.5 shard_map.124
  30.5 0.8 %collective-permute-start.10 = (bf16[528,128]{1,0:T(8,128)(2,1)S(1)}, bf16[528,128]{1,0:T(8,128)(2,1)S(1)}, u32[]{:S(2)}, u32[]{:S(2)}) collective-permute-start(bf16[528,128]{1,0:T(8,128)(2,1)S(1)} %shard_map.124), channel_id=1, source_target_pairs={{0,4},{4,0},{8,12},{12,8},{1,5},{5,1},{9,13},{13,9},{2,6},{6,2},{1... | collective-permute-start | bytes 405512 | tf_op jit(solution)/shard_map/ppermute | solution.py:277
  31.3 0.5 shard_map.123
  31.7 0.0 copy-start
  31.7 1.0 %collective-permute-start.9 = (bf16[528,128]{1,0:T(8,128)(2,1)S(1)}, bf16[528,128]{1,0:T(8,128)(2,1)S(1)}, u32[]{:S(2)}, u32[]{:S(2)}) collective-permute-start(bf16[528,128]{1,0:T(8,128)(2,1)S(1)} %shard_map.123), channel_id=1, source_target_pairs={{0,12},{4,8},{8,4},{12,0},{1,13},{5,9},{9,5},{13,1},{2,14},{6,10},... | collective-permute-start | bytes 405512 | tf_op jit(solution)/shard_map/ppermute | solution.py:277
  32.7 0.5 shard_map.125.payload_ref
  33.2 2.0 %shard_map.126 = (f32[4,2,2,128,128]{4,3,2,1,0:T(8,128)S(1)}, bf16[4,2,2,192,128]{4,3,2,1,0:T(8,128)(2,1)S(1)}, f32[4,2,128,128]{3,2,1,0:T(8,128)S(1)}, f32[4,2,2,8,128]{4,3,2,1,0:T(8,128)S(1)}) custom-call(bf16[528,128]{1,0:T(8,128)(2,1)S(1)} %shard_map.125.payload_ref), custom_call_target="tpu_custom_call" | custom-call | tf_op jit(solution)/shard_map/pallas_call | solution.py:264
  35.1 2.8 %collective-permute-done.11.payload_ref = bf16[528,128]{1,0:T(8,128)(2,1)S(1)} collective-permute-done((bf16[528,128]{1,0:T(8,128)(2,1)S(1)}, bf16[528,128]{1,0:T(8,128)(2,1)S(1)}, u32[]{:S(2)}, u32[]{:S(2)}) %collective-permute-start.11) | collective-permute-done | bytes 135200 | tf_op jit(solution)/shard_map/ppermute | solution.py:277
  37.9 2.0 %shard_map.127 = (f32[4,2,2,128,128]{4,3,2,1,0:T(8,128)S(1)}, bf16[4,2,2,192,128]{4,3,2,1,0:T(8,128)(2,1)S(1)}, f32[4,2,128,128]{3,2,1,0:T(8,128)S(1)}, f32[4,2,2,8,128]{4,3,2,1,0:T(8,128)S(1)}) custom-call(bf16[528,128]{1,0:T(8,128)(2,1)S(1)} %collective-permute-done.11.payload_ref, ...), custom_call_target="tpu_custom_call", output_to_operand_aliasing={{0}: (1, {}), {1}: (2, {}), {2}: (3, {}), {3}: (4, {})} | custom-call | tf_op jit(solution)/shard_map/pallas_call | solution.py:264
  39.9 1.5 %collective-permute-done.10.payload_ref = bf16[528,128]{1,0:T(8,128)(2,1)S(1)} collective-permute-done((bf16[528,128]{1,0:T(8,128)(2,1)S(1)}, bf16[528,128]{1,0:T(8,128)(2,1)S(1)}, u32[]{:S(2)}, u32[]{:S(2)}) %collective-permute-start.10) | collective-permute-done | bytes 135200 | tf_op jit(solution)/shard_map/ppermute | solution.py:277
  41.4 2.0 %shard_map.128 = (f32[4,2,2,128,128]{4,3,2,1,0:T(8,128)S(1)}, bf16[4,2,2,192,128]{4,3,2,1,0:T(8,128)(2,1)S(1)}, f32[4,2,128,128]{3,2,1,0:T(8,128)S(1)}, f32[4,2,2,8,128]{4,3,2,1,0:T(8,128)S(1)}) custom-call(bf16[528,128]{1,0:T(8,128)(2,1)S(1)} %collective-permute-done.10.payload_ref, ...), custom_call_target="tpu_custom_call", output_to_operand_aliasing={{0}: (1, {}), {1}: (2, {}), {2}: (3, {}), {3}: (4, {})} | custom-call | tf_op jit(solution)/shard_map/pallas_call | solution.py:264
  43.4 2.0 %shard_map.129 = (f32[4,2,2,128,128]{4,3,2,1,0:T(8,128)S(1)}, bf16[4,2,2,192,128]{4,3,2,1,0:T(8,128)(2,1)S(1)}, f32[4,2,128,128]{3,2,1,0:T(8,128)S(1)}, f32[4,2,2,8,128]{4,3,2,1,0:T(8,128)S(1)}) custom-call(bf16[528,128]{1,0:T(8,128)(2,1)S(1)} %collective-permute-done.9.payload_ref, ...), custom_call_target="tpu_custom_call", output_to_operand_aliasing={{0}: (1, {}), {1}: (2, {}), {2}: (3, {}), {3}: (4, {})} | custom-call | tf_op jit(solution)/shard_map/pallas_call | solution.py:264
  45.4 1.2 %shard_map.130 = (bf16[128,256]{1,0:T(8,128)(2,1)S(1)}, bf16[128,256]{1,0:T(8,128)(2,1)S(1)}, bf16[128,256]{1,0:T(8,128)(2,1)S(1)}, bf16[128,256]{1,0:T(8,128)(2,1)S(1)}) custom-call(f32[4,2,2,128,128]{4,3,2,1,0:T(8,128)S(1)} %get-tuple-element.126.offset_ref, bf16[4,2,2,192,128]{4,3,2,1,0:T(8,128)(2,1)S(1)} %get-tuple-element.127.linear_ref, ...), custom_call_target="tpu_custom_call" | custom-call | tf_op jit(solution)/shard_map/pallas_call | solution.py:264
  46.6 0.1 collective-permute-start.12
  46.7 2.3 %collective-permute-start.13 = (bf16[128,256]{1,0:T(8,128)(2,1)S(1)}, bf16[128,256]{1,0:T(8,128)(2,1)S(1)}, u32[]{:S(2)}, u32[]{:S(2)}) collective-permute-start(bf16[128,256]{1,0:T(8,128)(2,1)S(1)} %get-tuple-element.132), channel_id=1, source_target_pairs={{0,8},{4,12},{8,0},{12,4},{1,9},{5,13},{9,1},{13,5},{2,10},{6,14},... | collective-permute-start | bytes 196616 | tf_op jit(solution)/shard_map/ppermute | solution.py:277
  49.0 2.1 %collective-permute-start.14 = (bf16[128,256]{1,0:T(8,128)(2,1)S(1)}, bf16[128,256]{1,0:T(8,128)(2,1)S(1)}, u32[]{:S(2)}, u32[]{:S(2)}) collective-permute-start(bf16[128,256]{1,0:T(8,128)(2,1)S(1)} %get-tuple-element.133), channel_id=1, source_target_pairs={{0,12},{4,8},{8,4},{12,0},{1,13},{5,9},{9,5},{13,1},{2,14},{6,10},... | collective-permute-start | bytes 196616 | tf_op jit(solution)/shard_map/ppermute | solution.py:277
  51.0 0.7 %shard_map.121 = bf16[128,512]{1,0:T(8,128)(2,1)} custom-call(bf16[128,1024]{1,0:T(8,128)(2,1)S(1)} %shard_map.119.own_ref, bf16[128,1024]{1,0:T(8,128)(2,1)S(1)} %collective-permute-done.8.twin_ref), custom_call_target="tpu_custom_call" | custom-call | tf_op jit(solution)/shard_map/pallas_call | solution.py:264
  51.7 0.0 collective-permute-done.12.back1
  51.7 2.3 %collective-permute-done.13.back2 = bf16[128,256]{1,0:T(8,128)(2,1)S(1)} collective-permute-done((bf16[128,256]{1,0:T(8,128)(2,1)S(1)}, bf16[128,256]{1,0:T(8,128)(2,1)S(1)}, u32[]{:S(2)}, u32[]{:S(2)}) %collective-permute-start.13) | collective-permute-done | bytes 65568 | tf_op jit(solution)/shard_map/ppermute | solution.py:277
  54.0 1.1 %collective-permute-done.14.back3 = bf16[128,256]{1,0:T(8,128)(2,1)S(1)} collective-permute-done((bf16[128,256]{1,0:T(8,128)(2,1)S(1)}, bf16[128,256]{1,0:T(8,128)(2,1)S(1)}, u32[]{:S(2)}, u32[]{:S(2)}) %collective-permute-start.14) | collective-permute-done | bytes 65568 | tf_op jit(solution)/shard_map/ppermute | solution.py:277
  55.1 0.7 %shard_map.131 = bf16[128,1024]{1,0:T(8,128)(2,1)} custom-call(bf16[128,256]{1,0:T(8,128)(2,1)S(1)} %get-tuple-element.130.own_ref, bf16[128,256]{1,0:T(8,128)(2,1)S(1)} %collective-permute-done.12.back1, bf16[128,256]{1,0:T(8,128)(2,1)S(1)} %collective-permute-done.13.back2, bf16[128,256]{1,0:T(8,128)(2,1)S(1)} %collective-permute-done.14.back3), custom_call_target="tpu_custom_call" | custom-call | tf_op jit(solution)/shard_map/pallas_call | solution.py:710
  (3 shorter events, 0.1 us)
Async XLA Ops:
  1.5 8.2 %collective-permute-start = (bf16[128,256]{1,0:T(8,128)(2,1)S(1)}, bf16[128,256]{1,0:T(8,128)(2,1)S(1)}, u32[]{:S(2)}, u32[]{:S(2)}) collective-permute-start(bf16[128,256]{1,0:T(8,128)(2,1)S(1)} %shard_map.113), channel_id=1, source_target_pairs={{0,8},{4,12},{8,0},{12,4},{1,9},{5,13},{9,1},{13,5},{2,10},{6,14},... | collective-permute-start | bytes 196616 | tf_op jit(solution)/shard_map/ppermute | solution.py:277
  5.6 6.2 %collective-permute-start.2 = (bf16[128,256]{1,0:T(8,128)(2,1)S(1)}, bf16[128,256]{1,0:T(8,128)(2,1)S(1)}, u32[]{:S(2)}, u32[]{:S(2)}) collective-permute-start(bf16[128,256]{1,0:T(8,128)(2,1)S(1)} %shard_map.113), channel_id=1, source_target_pairs={{0,12},{4,8},{8,4},{12,0},{1,13},{5,9},{9,5},{13,1},{2,14},{6,10},... | collective-permute-start | bytes 196616 | tf_op jit(solution)/shard_map/ppermute | solution.py:277
  6.9 5.0 %collective-permute-start.1 = (bf16[128,256]{1,0:T(8,128)(2,1)S(1)}, bf16[128,256]{1,0:T(8,128)(2,1)S(1)}, u32[]{:S(2)}, u32[]{:S(2)}) collective-permute-start(bf16[128,256]{1,0:T(8,128)(2,1)S(1)} %shard_map.113), channel_id=1, source_target_pairs={{0,4},{4,0},{8,12},{12,8},{1,5},{5,1},{9,13},{13,9},{2,6},{6,2},{1... | collective-permute-start | bytes 196616 | tf_op jit(solution)/shard_map/ppermute | solution.py:277
  11.8 1.3 %collective-permute-start.5 = (bf16[128,256]{1,0:T(8,128)(2,1)S(1)}, bf16[128,256]{1,0:T(8,128)(2,1)S(1)}, u32[]{:S(2)}, u32[]{:S(2)}) collective-permute-start(bf16[128,256]{1,0:T(8,128)(2,1)S(1)} %collective-permute-done.2.mine3), channel_id=1, source_target_pairs={{0,1},{1,0},{2,3},{3,2},{4,5},{5,4},{6,7},{7,6},{8,9},{9,8},{10,11... | collective-permute-start | bytes 196616 | tf_op jit(solution)/shard_map/ppermute | solution.py:277
  11.9 1.3 %collective-permute-start.3 = (bf16[128,256]{1,0:T(8,128)(2,1)S(1)}, bf16[128,256]{1,0:T(8,128)(2,1)S(1)}, u32[]{:S(2)}, u32[]{:S(2)}) collective-permute-start(bf16[128,256]{1,0:T(8,128)(2,1)S(1)} %collective-permute-done.1.mine1), channel_id=1, source_target_pairs={{0,1},{1,0},{2,3},{3,2},{4,5},{5,4},{6,7},{7,6},{8,9},{9,8},{10,11... | collective-permute-start | bytes 196616 | tf_op jit(solution)/shard_map/ppermute | solution.py:277
  12.3 1.3 %collective-permute-start.4 = (bf16[128,256]{1,0:T(8,128)(2,1)S(1)}, bf16[128,256]{1,0:T(8,128)(2,1)S(1)}, u32[]{:S(2)}, u32[]{:S(2)}) collective-permute-start(bf16[128,256]{1,0:T(8,128)(2,1)S(1)} %collective-permute-done.mine2), channel_id=1, source_target_pairs={{0,1},{1,0},{2,3},{3,2},{4,5},{5,4},{6,7},{7,6},{8,9},{9,8},{10,11... | collective-permute-start | bytes 196616 | tf_op jit(solution)/shard_map/ppermute | solution.py:277
  14.8 1.6 %collective-permute-start.6 = (bf16[128,1024]{1,0:T(8,128)(2,1)S(1)}, bf16[128,1024]{1,0:T(8,128)(2,1)S(1)}, u32[]{:S(2)}, u32[]{:S(2)}) collective-permute-start(bf16[128,1024]{1,0:T(8,128)(2,1)S(1)} %get-tuple-element.84), channel_id=1, source_target_pairs={{0,1},{1,0},{2,3},{3,2},{4,5},{5,4},{6,7},{7,6},{8,9},{9,8},{10,11... | collective-permute-start | bytes 786440 | tf_op jit(solution)/shard_map/ppermute | solution.py:277
  16.5 8.5 %collective-permute-start.7 = (bf16[128,1024]{1,0:T(8,128)(2,1)S(1)}, bf16[128,1024]{1,0:T(8,128)(2,1)S(1)}, u32[]{:S(2)}, u32[]{:S(2)}) collective-permute-start(bf16[128,1024]{1,0:T(8,128)(2,1)S(1)} %get-tuple-element.89), channel_id=1, source_target_pairs={{0,2},{2,0},{1,3},{3,1},{4,6},{6,4},{5,7},{7,5},{8,10},{10,8},{9,1... | collective-permute-start | bytes 786440 | tf_op jit(solution)/shard_map/ppermute | solution.py:277
  25.0 1.6 %collective-permute-start.8 = (bf16[128,1024]{1,0:T(8,128)(2,1)S(1)}, bf16[128,1024]{1,0:T(8,128)(2,1)S(1)}, u32[]{:S(2)}, u32[]{:S(2)}) collective-permute-start(bf16[128,1024]{1,0:T(8,128)(2,1)S(1)} %shard_map.119.own_ref), channel_id=1, source_target_pairs={{0,1},{1,0},{2,3},{3,2},{4,5},{5,4},{6,7},{7,6},{8,9},{9,8},{10,11... | collective-permute-start | bytes 786440 | tf_op jit(solution)/shard_map/ppermute | solution.py:277
  27.2 10.7 %collective-permute-start.11 = (bf16[528,128]{1,0:T(8,128)(2,1)S(1)}, bf16[528,128]{1,0:T(8,128)(2,1)S(1)}, u32[]{:S(2)}, u32[]{:S(2)}) collective-permute-start(bf16[528,128]{1,0:T(8,128)(2,1)S(1)} %get-tuple-element.113), channel_id=1, source_target_pairs={{0,8},{4,12},{8,0},{12,4},{1,9},{5,13},{9,1},{13,5},{2,10},{6,14},... | collective-permute-start | bytes 405512 | tf_op jit(solution)/shard_map/ppermute | solution.py:277
  30.5 10.9 %collective-permute-start.10 = (bf16[528,128]{1,0:T(8,128)(2,1)S(1)}, bf16[528,128]{1,0:T(8,128)(2,1)S(1)}, u32[]{:S(2)}, u32[]{:S(2)}) collective-permute-start(bf16[528,128]{1,0:T(8,128)(2,1)S(1)} %shard_map.124), channel_id=1, source_target_pairs={{0,4},{4,0},{8,12},{12,8},{1,5},{5,1},{9,13},{13,9},{2,6},{6,2},{1... | collective-permute-start | bytes 405512 | tf_op jit(solution)/shard_map/ppermute | solution.py:277
  31.7 13.7 %copy-start = (f32[128]{0:T(128)S(1)}, f32[128]{0:T(128)}, u32[]{:S(2)}) copy-start(f32[128]{0:T(128)} %param.19) | copy-start | bytes 1540
  31.7 11.7 %collective-permute-start.9 = (bf16[528,128]{1,0:T(8,128)(2,1)S(1)}, bf16[528,128]{1,0:T(8,128)(2,1)S(1)}, u32[]{:S(2)}, u32[]{:S(2)}) collective-permute-start(bf16[528,128]{1,0:T(8,128)(2,1)S(1)} %shard_map.123), channel_id=1, source_target_pairs={{0,12},{4,8},{8,4},{12,0},{1,13},{5,9},{9,5},{13,1},{2,14},{6,10},... | collective-permute-start | bytes 405512 | tf_op jit(solution)/shard_map/ppermute | solution.py:277
  46.6 5.1 %collective-permute-start.12 = (bf16[128,256]{1,0:T(8,128)(2,1)S(1)}, bf16[128,256]{1,0:T(8,128)(2,1)S(1)}, u32[]{:S(2)}, u32[]{:S(2)}) collective-permute-start(bf16[128,256]{1,0:T(8,128)(2,1)S(1)} %get-tuple-element.131), channel_id=1, source_target_pairs={{0,4},{4,0},{8,12},{12,8},{1,5},{5,1},{9,13},{13,9},{2,6},{6,2},{1... | collective-permute-start | bytes 196616 | tf_op jit(solution)/shard_map/ppermute | solution.py:277
  46.7 7.4 %collective-permute-start.13 = (bf16[128,256]{1,0:T(8,128)(2,1)S(1)}, bf16[128,256]{1,0:T(8,128)(2,1)S(1)}, u32[]{:S(2)}, u32[]{:S(2)}) collective-permute-start(bf16[128,256]{1,0:T(8,128)(2,1)S(1)} %get-tuple-element.132), channel_id=1, source_target_pairs={{0,8},{4,12},{8,0},{12,4},{1,9},{5,13},{9,1},{13,5},{2,10},{6,14},... | collective-permute-start | bytes 196616 | tf_op jit(solution)/shard_map/ppermute | solution.py:277
  49.0 6.2 %collective-permute-start.14 = (bf16[128,256]{1,0:T(8,128)(2,1)S(1)}, bf16[128,256]{1,0:T(8,128)(2,1)S(1)}, u32[]{:S(2)}, u32[]{:S(2)}) collective-permute-start(bf16[128,256]{1,0:T(8,128)(2,1)S(1)} %get-tuple-element.133), channel_id=1, source_target_pairs={{0,12},{4,8},{8,4},{12,0},{1,13},{5,9},{9,5},{13,1},{2,14},{6,10},... | collective-permute-start | bytes 196616 | tf_op jit(solution)/shard_map/ppermute | solution.py:277

commit v5 on v4

--- a/solution.py
+++ b/solution.py
@@ -596,7 +596,7 @@
         back[...] = outs[jnp.bitwise_xor(rank, mask)]
 
 
-def place_kernel(own_ref, back1, back2, back3, out_ref, sems):
+def place_kernel(own_ref, back3, back1, back2, out_ref, sems):
     width = own_ref.shape[1]
     rank = lax.axis_index("ctx")
     copies = []
@@ -637,7 +637,7 @@
     mine = {mask: swapped(piece, "ctx", mask) for mask in masks[::-1]}
     piece, *late = lax.optimization_barrier((piece, att_query, att_gate, att_kv, out_weight, residual))
     late = fetched(*late)
-    mine[2], (att_query, att_gate, att_kv, out_weight, residual) = lax.optimization_barrier((mine[2], late))
+    mine[3], (att_query, att_gate, att_kv, out_weight, residual) = lax.optimization_barrier((mine[3], late))
     twin = {mask: swapped(mine[mask], "sub") for mask in masks}
     heads, send = vmem_call(
         attention_kernel,
@@ -714,7 +714,7 @@
         out_specs=IN_HBM,
         scratch_shapes=[pltpu.SemaphoreType.DMA((4,))],
         compiler_params=pltpu.CompilerParams(vmem_limit_bytes=4 * MIB),
-    )(*[in_vmem(back) for back in (own, backs[1], backs[2], backs[3])])
+    )(*[in_vmem(back) for back in (own, backs[3], backs[1], backs[2])])
     return (new_residual, delta_out)
 
 

time: 56 us -> 54.6 us (0.975)
  waiting for transfers between devices: 16.1 us -> 14.7 us
    ppermute x15, waiting for transfers between devices: 16.1 us -> 14.7 us  [swapped(): lax.ppermute(value, axis, [(i, i ^ mask) for i in range(lax.axis_size(axi...]
  transfers between devices with their start and end apart: 15 -> 15, of which waited for: 12 -> 11; matrix products, arithmetic and copies ran while one was open for 0% -> 0% of each run, Pallas kernels for 27% -> 28%
where the time goes in v5:
time: 54.6 us; the launch traced here: 54.5 us
  Pallas kernels  21.8 us (40%)
  starting transfers between devices  17.2 us (32%)
  waiting for transfers between devices  14.7 us (27%)
  between operations  0.8 us (1%)
    ppermute x15, starting transfers between devices, swapped(): lax.ppermute(value, axis, [(i, i ^ mask) for i in range(lax.axis_size(axi...  17.2 us
    ppermute x15, waiting for transfers between devices, swapped(): lax.ppermute(value, axis, [(i, i ^ mask) for i in range(lax.axis_size(axi...  14.7 us
    pallas_call x15, Pallas kernels, vmem_call(): pl.pallas_call(kernel, out_shape=[make(shape, dtype) for shape, dtype in...  14.3 us
    pallas_call x2, Pallas kernels, fetched(): pl.pallas_call(fetch_kernel, out_shape=[pltpu.VMEM(array.shape, array.dty...  5.9 us
  transfers between devices with their start and end apart: 15, of which 11 were waited for; matrix products, arithmetic and copies ran while one was open for 0% of the time, Pallas kernels for 28%

profile of v5, /device:TPU:0, one launch (start us, length us, event | category | flops | bytes accessed | tf_op | source)
XLA Modules:
  0.0 54.5 jit_solution(12289755761238357194)
XLA Ops:
  0.6 0.9 %shard_map.113 = bf16[128,256]{1,0:T(8,128)(2,1)S(1)} custom-call(bf16[128,1024]{1,0:T(8,128)(2,1)} %refs_2_), custom_call_target="tpu_custom_call" | custom-call | tf_op jit(solution)/shard_map/pallas_call | solution.py:629
  1.5 5.1 %collective-permute-start = (bf16[128,256]{1,0:T(8,128)(2,1)S(1)}, bf16[128,256]{1,0:T(8,128)(2,1)S(1)}, u32[]{:S(2)}, u32[]{:S(2)}) collective-permute-start(bf16[128,256]{1,0:T(8,128)(2,1)S(1)} %shard_map.113), channel_id=1, source_target_pairs={{0,12},{4,8},{8,4},{12,0},{1,13},{5,9},{9,5},{13,1},{2,14},{6,10},... | collective-permute-start | bytes 196616 | tf_op jit(solution)/shard_map/ppermute | solution.py:277
  6.6 0.6 %collective-permute-start.1 = (bf16[128,256]{1,0:T(8,128)(2,1)S(1)}, bf16[128,256]{1,0:T(8,128)(2,1)S(1)}, u32[]{:S(2)}, u32[]{:S(2)}) collective-permute-start(bf16[128,256]{1,0:T(8,128)(2,1)S(1)} %shard_map.113), channel_id=1, source_target_pairs={{0,4},{4,0},{8,12},{12,8},{1,5},{5,1},{9,13},{13,9},{2,6},{6,2},{1... | collective-permute-start | bytes 196616 | tf_op jit(solution)/shard_map/ppermute | solution.py:277
  7.3 2.5 %shard_map.114 = (bf16[128,1024]{1,0:T(8,128)(2,1)S(1)}, bf16[128,1024]{1,0:T(8,128)(2,1)S(1)}, bf16[128,1024]{1,0:T(8,128)(2,1)S(1)}, bf16[1024,2048]{1,0:T(8,128)(2,1)S(1)}, bf16[128,512]{1,0:T(8,128)(2,1)S(1)}) custom-call(bf16[128,1024]{1,0:T(8,128)(2,1)} %refs_0_, bf16[128,1024]{1,0:T(8,128)(2,1)} %refs_1_, bf16[128,1024]{1,0:T(8,128)(2,1)} %refs_2_, ...), custom_call_target="tpu_custom_call" | custom-call | bytes 5111808 | tf_op jit(solution)/shard_map/pallas_call | solution.py:317
  9.7 0.0 collective-permute-done.mine3
  9.8 2.5 %collective-permute-done.2.mine2 = bf16[128,256]{1,0:T(8,128)(2,1)S(1)} collective-permute-done((bf16[128,256]{1,0:T(8,128)(2,1)S(1)}, bf16[128,256]{1,0:T(8,128)(2,1)S(1)}, u32[]{:S(2)}, u32[]{:S(2)}) %collective-permute-start.2) | collective-permute-done | bytes 65568 | tf_op jit(solution)/shard_map/ppermute | solution.py:277
  12.2 0.0 collective-permute-start.4
  12.2 0.0 collective-permute-done.1.mine1
  12.2 0.5 collective-permute-start.3
  12.7 0.0 collective-permute-start.5
  12.7 0.7 %collective-permute-done.4.twin2 = bf16[128,256]{1,0:T(8,128)(2,1)S(1)} collective-permute-done((bf16[128,256]{1,0:T(8,128)(2,1)S(1)}, bf16[128,256]{1,0:T(8,128)(2,1)S(1)}, u32[]{:S(2)}, u32[]{:S(2)}) %collective-permute-start.4) | collective-permute-done | bytes 65568 | tf_op jit(solution)/shard_map/ppermute | solution.py:277
  13.5 0.2 collective-permute-done.3.twin1
  13.6 0.4 collective-permute-done.5.twin3
  14.0 1.2 %shard_map.115 = (bf16[128,1024]{1,0:T(8,128)(2,1)S(1)}, bf16[128,1024]{1,0:T(8,128)(2,1)S(1)}) custom-call(bf16[128,1024]{1,0:T(8,128)(2,1)S(1)} %get-tuple-element.78.query_ref, bf16[128,1024]{1,0:T(8,128)(2,1)S(1)} %get-tuple-element.79.gate_ref, bf16[128,1024]{1,0:T(8,128)(2,1)S(1)} %get-tuple-element.80.kv_ref, ...), custom_call_target="tpu_custom_call" | custom-call | tf_op jit(solution)/shard_map/pallas_call | solution.py:264
  15.2 0.2 collective-permute-start.6
  15.5 0.5 shard_map.116.keep_ref
  15.9 0.9 %collective-permute-done.6.came_ref = bf16[128,1024]{1,0:T(8,128)(2,1)S(1)} collective-permute-done((bf16[128,1024]{1,0:T(8,128)(2,1)S(1)}, bf16[128,1024]{1,0:T(8,128)(2,1)S(1)}, u32[]{:S(2)}, u32[]{:S(2)}) %collective-permute-start.6) | collective-permute-done | bytes 262176 | tf_op jit(solution)/shard_map/ppermute | solution.py:277
  16.8 0.1 shard_map.117
  16.9 1.6 %collective-permute-start.7 = (bf16[128,1024]{1,0:T(8,128)(2,1)S(1)}, bf16[128,1024]{1,0:T(8,128)(2,1)S(1)}, u32[]{:S(2)}, u32[]{:S(2)}) collective-permute-start(bf16[128,1024]{1,0:T(8,128)(2,1)S(1)} %get-tuple-element.89), channel_id=1, source_target_pairs={{0,2},{2,0},{1,3},{3,1},{4,6},{6,4},{5,7},{7,5},{8,10},{10,8},{9,1... | collective-permute-start | bytes 786440 | tf_op jit(solution)/shard_map/ppermute | solution.py:277
  18.5 3.4 %shard_map.118 = (bf16[2048,2048]{1,0:T(8,128)(2,1)S(1)}, f32[1,2048]{1,0:T(1,128)S(1)}, bf16[8,2048]{1,0:T(8,128)(2,1)S(1)}, f32[8,128]{1,0:T(8,128)S(1)}) custom-call(bf16[2048,2048]{1,0:T(8,128)(2,1)} %refs_0_.1, f32[1,2048]{1,0:T(1,128)} %bitcast.6, bf16[8,2048]{1,0:T(8,128)(2,1)} %bitcast.5, f32[8,128]{1,0:T(8,128)} %bitcast.7), custom_call_target="tpu_custom_call" | custom-call | bytes 8433664 | tf_op jit(solution)/shard_map/pallas_call | solution.py:317
  21.9 3.4 %collective-permute-done.7.came_ref = bf16[128,1024]{1,0:T(8,128)(2,1)S(1)} collective-permute-done((bf16[128,1024]{1,0:T(8,128)(2,1)S(1)}, bf16[128,1024]{1,0:T(8,128)(2,1)S(1)}, u32[]{:S(2)}, u32[]{:S(2)}) %collective-permute-start.7) | collective-permute-done | bytes 262176 | tf_op jit(solution)/shard_map/ppermute | solution.py:277
  25.4 0.1 collective-permute-start.8
  25.5 0.8 %shard_map.120 = (f32[128,2048]{1,0:T(8,128)S(1)}, f32[8,128]{1,0:T(8,128)S(1)}, f32[128,128]{1,0:T(8,128)S(1)}) custom-call(bf16[128,1024]{1,0:T(8,128)(2,1)S(1)} %shard_map.119.own_ref, f32[1,2048]{1,0:T(1,128)S(1)} %get-tuple-element.99.gain_ref, bf16[2048,2048]{1,0:T(8,128)(2,1)S(1)} %get-tuple-element.100.weight_ref, ...), custom_call_target="tpu_custom_call" | custom-call | tf_op jit(solution)/shard_map/pallas_call | solution.py:264
  26.3 0.7 %collective-permute-done.8.twin_ref = bf16[128,1024]{1,0:T(8,128)(2,1)S(1)} collective-permute-done((bf16[128,1024]{1,0:T(8,128)(2,1)S(1)}, bf16[128,1024]{1,0:T(8,128)(2,1)S(1)}, u32[]{:S(2)}, u32[]{:S(2)}) %collective-permute-start.8) | collective-permute-done | bytes 262176 | tf_op jit(solution)/shard_map/ppermute | solution.py:277
  27.0 0.6 %shard_map.122 = (bf16[128,1024]{1,0:T(8,128)(2,1)S(1)}, f32[128,128]{1,0:T(8,128)S(1)}, f32[16,128]{1,0:T(8,128)S(1)}, bf16[528,128]{1,0:T(8,128)(2,1)S(1)}) custom-call(bf16[128,1024]{1,0:T(8,128)(2,1)S(1)} %collective-permute-done.8.twin_ref, f32[1,2048]{1,0:T(1,128)S(1)} %get-tuple-element.99.gain_ref, bf16[8,2048]{1,0:T(8,128)(2,1)S(1)} %get-tuple-element.101.beta_ref, ...), custom_call_target="tpu_custom_call" | custom-call | tf_op jit(solution)/shard_map/pallas_call | solution.py:264
  27.6 1.5 %collective-permute-start.11 = (bf16[528,128]{1,0:T(8,128)(2,1)S(1)}, bf16[528,128]{1,0:T(8,128)(2,1)S(1)}, u32[]{:S(2)}, u32[]{:S(2)}) collective-permute-start(bf16[528,128]{1,0:T(8,128)(2,1)S(1)} %get-tuple-element.113), channel_id=1, source_target_pairs={{0,8},{4,12},{8,0},{12,4},{1,9},{5,13},{9,1},{13,5},{2,10},{6,14},... | collective-permute-start | bytes 405512 | tf_op jit(solution)/shard_map/ppermute | solution.py:277
  29.1 0.5 shard_map.124
  29.5 1.9 %collective-permute-start.10 = (bf16[528,128]{1,0:T(8,128)(2,1)S(1)}, bf16[528,128]{1,0:T(8,128)(2,1)S(1)}, u32[]{:S(2)}, u32[]{:S(2)}) collective-permute-start(bf16[528,128]{1,0:T(8,128)(2,1)S(1)} %shard_map.124), channel_id=1, source_target_pairs={{0,4},{4,0},{8,12},{12,8},{1,5},{5,1},{9,13},{13,9},{2,6},{6,2},{1... | collective-permute-start | bytes 405512 | tf_op jit(solution)/shard_map/ppermute | solution.py:277
  31.4 0.5 shard_map.123
  31.9 0.0 copy-start
  31.9 1.2 %collective-permute-start.9 = (bf16[528,128]{1,0:T(8,128)(2,1)S(1)}, bf16[528,128]{1,0:T(8,128)(2,1)S(1)}, u32[]{:S(2)}, u32[]{:S(2)}) collective-permute-start(bf16[528,128]{1,0:T(8,128)(2,1)S(1)} %shard_map.123), channel_id=1, source_target_pairs={{0,12},{4,8},{8,4},{12,0},{1,13},{5,9},{9,5},{13,1},{2,14},{6,10},... | collective-permute-start | bytes 405512 | tf_op jit(solution)/shard_map/ppermute | solution.py:277
  33.1 0.5 shard_map.125.payload_ref
  33.5 2.0 %shard_map.126 = (f32[4,2,2,128,128]{4,3,2,1,0:T(8,128)S(1)}, bf16[4,2,2,192,128]{4,3,2,1,0:T(8,128)(2,1)S(1)}, f32[4,2,128,128]{3,2,1,0:T(8,128)S(1)}, f32[4,2,2,8,128]{4,3,2,1,0:T(8,128)S(1)}) custom-call(bf16[528,128]{1,0:T(8,128)(2,1)S(1)} %shard_map.125.payload_ref), custom_call_target="tpu_custom_call" | custom-call | tf_op jit(solution)/shard_map/pallas_call | solution.py:264
  35.5 2.8 %collective-permute-done.11.payload_ref = bf16[528,128]{1,0:T(8,128)(2,1)S(1)} collective-permute-done((bf16[528,128]{1,0:T(8,128)(2,1)S(1)}, bf16[528,128]{1,0:T(8,128)(2,1)S(1)}, u32[]{:S(2)}, u32[]{:S(2)}) %collective-permute-start.11) | collective-permute-done | bytes 135200 | tf_op jit(solution)/shard_map/ppermute | solution.py:277
  38.3 2.0 %shard_map.127 = (f32[4,2,2,128,128]{4,3,2,1,0:T(8,128)S(1)}, bf16[4,2,2,192,128]{4,3,2,1,0:T(8,128)(2,1)S(1)}, f32[4,2,128,128]{3,2,1,0:T(8,128)S(1)}, f32[4,2,2,8,128]{4,3,2,1,0:T(8,128)S(1)}) custom-call(bf16[528,128]{1,0:T(8,128)(2,1)S(1)} %collective-permute-done.11.payload_ref, ...), custom_call_target="tpu_custom_call", output_to_operand_aliasing={{0}: (1, {}), {1}: (2, {}), {2}: (3, {}), {3}: (4, {})} | custom-call | tf_op jit(solution)/shard_map/pallas_call | solution.py:264
  40.3 0.0 collective-permute-done.10.payload_ref
  40.3 2.0 %shard_map.128 = (f32[4,2,2,128,128]{4,3,2,1,0:T(8,128)S(1)}, bf16[4,2,2,192,128]{4,3,2,1,0:T(8,128)(2,1)S(1)}, f32[4,2,128,128]{3,2,1,0:T(8,128)S(1)}, f32[4,2,2,8,128]{4,3,2,1,0:T(8,128)S(1)}) custom-call(bf16[528,128]{1,0:T(8,128)(2,1)S(1)} %collective-permute-done.10.payload_ref, ...), custom_call_target="tpu_custom_call", output_to_operand_aliasing={{0}: (1, {}), {1}: (2, {}), {2}: (3, {}), {3}: (4, {})} | custom-call | tf_op jit(solution)/shard_map/pallas_call | solution.py:264
  42.3 0.0 collective-permute-done.9.payload_ref
  42.3 2.0 %shard_map.129 = (f32[4,2,2,128,128]{4,3,2,1,0:T(8,128)S(1)}, bf16[4,2,2,192,128]{4,3,2,1,0:T(8,128)(2,1)S(1)}, f32[4,2,128,128]{3,2,1,0:T(8,128)S(1)}, f32[4,2,2,8,128]{4,3,2,1,0:T(8,128)S(1)}) custom-call(bf16[528,128]{1,0:T(8,128)(2,1)S(1)} %collective-permute-done.9.payload_ref, ...), custom_call_target="tpu_custom_call", output_to_operand_aliasing={{0}: (1, {}), {1}: (2, {}), {2}: (3, {}), {3}: (4, {})} | custom-call | tf_op jit(solution)/shard_map/pallas_call | solution.py:264
  44.3 1.2 %shard_map.130 = (bf16[128,256]{1,0:T(8,128)(2,1)S(1)}, bf16[128,256]{1,0:T(8,128)(2,1)S(1)}, bf16[128,256]{1,0:T(8,128)(2,1)S(1)}, bf16[128,256]{1,0:T(8,128)(2,1)S(1)}) custom-call(f32[4,2,2,128,128]{4,3,2,1,0:T(8,128)S(1)} %get-tuple-element.126.offset_ref, bf16[4,2,2,192,128]{4,3,2,1,0:T(8,128)(2,1)S(1)} %get-tuple-element.127.linear_ref, ...), custom_call_target="tpu_custom_call" | custom-call | tf_op jit(solution)/shard_map/pallas_call | solution.py:264
  45.5 2.3 %collective-permute-start.12 = (bf16[128,256]{1,0:T(8,128)(2,1)S(1)}, bf16[128,256]{1,0:T(8,128)(2,1)S(1)}, u32[]{:S(2)}, u32[]{:S(2)}) collective-permute-start(bf16[128,256]{1,0:T(8,128)(2,1)S(1)} %get-tuple-element.131), channel_id=1, source_target_pairs={{0,12},{4,8},{8,4},{12,0},{1,13},{5,9},{9,5},{13,1},{2,14},{6,10},... | collective-permute-start | bytes 196616 | tf_op jit(solution)/shard_map/ppermute | solution.py:277
  47.8 0.3 collective-permute-start.13
  48.1 1.8 %collective-permute-start.14 = (bf16[128,256]{1,0:T(8,128)(2,1)S(1)}, bf16[128,256]{1,0:T(8,128)(2,1)S(1)}, u32[]{:S(2)}, u32[]{:S(2)}) collective-permute-start(bf16[128,256]{1,0:T(8,128)(2,1)S(1)} %get-tuple-element.133), channel_id=1, source_target_pairs={{0,8},{4,12},{8,0},{12,4},{1,9},{5,13},{9,1},{13,5},{2,10},{6,14},... | collective-permute-start | bytes 196616 | tf_op jit(solution)/shard_map/ppermute | solution.py:277
  50.0 0.7 %shard_map.121 = bf16[128,512]{1,0:T(8,128)(2,1)} custom-call(bf16[128,1024]{1,0:T(8,128)(2,1)S(1)} %shard_map.119.own_ref, bf16[128,1024]{1,0:T(8,128)(2,1)S(1)} %collective-permute-done.8.twin_ref), custom_call_target="tpu_custom_call" | custom-call | tf_op jit(solution)/shard_map/pallas_call | solution.py:264
  50.6 1.1 %collective-permute-done.12.back3 = bf16[128,256]{1,0:T(8,128)(2,1)S(1)} collective-permute-done((bf16[128,256]{1,0:T(8,128)(2,1)S(1)}, bf16[128,256]{1,0:T(8,128)(2,1)S(1)}, u32[]{:S(2)}, u32[]{:S(2)}) %collective-permute-start.12) | collective-permute-done | bytes 65568 | tf_op jit(solution)/shard_map/ppermute | solution.py:277
  51.7 1.3 %collective-permute-done.13.back1 = bf16[128,256]{1,0:T(8,128)(2,1)S(1)} collective-permute-done((bf16[128,256]{1,0:T(8,128)(2,1)S(1)}, bf16[128,256]{1,0:T(8,128)(2,1)S(1)}, u32[]{:S(2)}, u32[]{:S(2)}) %collective-permute-start.13) | collective-permute-done | bytes 65568 | tf_op jit(solution)/shard_map/ppermute | solution.py:277
  53.0 0.7 %collective-permute-done.14.back2 = bf16[128,256]{1,0:T(8,128)(2,1)S(1)} collective-permute-done((bf16[128,256]{1,0:T(8,128)(2,1)S(1)}, bf16[128,256]{1,0:T(8,128)(2,1)S(1)}, u32[]{:S(2)}, u32[]{:S(2)}) %collective-permute-start.14) | collective-permute-done | bytes 65568 | tf_op jit(solution)/shard_map/ppermute | solution.py:277
  53.7 0.7 %shard_map.131 = bf16[128,1024]{1,0:T(8,128)(2,1)} custom-call(bf16[128,256]{1,0:T(8,128)(2,1)S(1)} %get-tuple-element.130.own_ref, bf16[128,256]{1,0:T(8,128)(2,1)S(1)} %collective-permute-done.12.back3, bf16[128,256]{1,0:T(8,128)(2,1)S(1)} %collective-permute-done.13.back1, bf16[128,256]{1,0:T(8,128)(2,1)S(1)} %collective-permute-done.14.back2), custom_call_target="tpu_custom_call" | custom-call | tf_op jit(solution)/shard_map/pallas_call | solution.py:710
  (3 shorter events, 0.1 us)
Async XLA Ops:
  1.5 8.3 %collective-permute-start = (bf16[128,256]{1,0:T(8,128)(2,1)S(1)}, bf16[128,256]{1,0:T(8,128)(2,1)S(1)}, u32[]{:S(2)}, u32[]{:S(2)}) collective-permute-start(bf16[128,256]{1,0:T(8,128)(2,1)S(1)} %shard_map.113), channel_id=1, source_target_pairs={{0,12},{4,8},{8,4},{12,0},{1,13},{5,9},{9,5},{13,1},{2,14},{6,10},... | collective-permute-start | bytes 196616 | tf_op jit(solution)/shard_map/ppermute | solution.py:277
  6.6 5.6 %collective-permute-start.2 = (bf16[128,256]{1,0:T(8,128)(2,1)S(1)}, bf16[128,256]{1,0:T(8,128)(2,1)S(1)}, u32[]{:S(2)}, u32[]{:S(2)}) collective-permute-start(bf16[128,256]{1,0:T(8,128)(2,1)S(1)} %shard_map.113), channel_id=1, source_target_pairs={{0,8},{4,12},{8,0},{12,4},{1,9},{5,13},{9,1},{13,5},{2,10},{6,14},... | collective-permute-start | bytes 196616 | tf_op jit(solution)/shard_map/ppermute | solution.py:277
  6.6 5.6 %collective-permute-start.1 = (bf16[128,256]{1,0:T(8,128)(2,1)S(1)}, bf16[128,256]{1,0:T(8,128)(2,1)S(1)}, u32[]{:S(2)}, u32[]{:S(2)}) collective-permute-start(bf16[128,256]{1,0:T(8,128)(2,1)S(1)} %shard_map.113), channel_id=1, source_target_pairs={{0,4},{4,0},{8,12},{12,8},{1,5},{5,1},{9,13},{13,9},{2,6},{6,2},{1... | collective-permute-start | bytes 196616 | tf_op jit(solution)/shard_map/ppermute | solution.py:277
  12.2 1.3 %collective-permute-start.4 = (bf16[128,256]{1,0:T(8,128)(2,1)S(1)}, bf16[128,256]{1,0:T(8,128)(2,1)S(1)}, u32[]{:S(2)}, u32[]{:S(2)}) collective-permute-start(bf16[128,256]{1,0:T(8,128)(2,1)S(1)} %collective-permute-done.2.mine2), channel_id=1, source_target_pairs={{0,1},{1,0},{2,3},{3,2},{4,5},{5,4},{6,7},{7,6},{8,9},{9,8},{10,11... | collective-permute-start | bytes 196616 | tf_op jit(solution)/shard_map/ppermute | solution.py:277
  12.2 1.4 %collective-permute-start.3 = (bf16[128,256]{1,0:T(8,128)(2,1)S(1)}, bf16[128,256]{1,0:T(8,128)(2,1)S(1)}, u32[]{:S(2)}, u32[]{:S(2)}) collective-permute-start(bf16[128,256]{1,0:T(8,128)(2,1)S(1)} %collective-permute-done.1.mine1), channel_id=1, source_target_pairs={{0,1},{1,0},{2,3},{3,2},{4,5},{5,4},{6,7},{7,6},{8,9},{9,8},{10,11... | collective-permute-start | bytes 196616 | tf_op jit(solution)/shard_map/ppermute | solution.py:277
  12.7 1.3 %collective-permute-start.5 = (bf16[128,256]{1,0:T(8,128)(2,1)S(1)}, bf16[128,256]{1,0:T(8,128)(2,1)S(1)}, u32[]{:S(2)}, u32[]{:S(2)}) collective-permute-start(bf16[128,256]{1,0:T(8,128)(2,1)S(1)} %collective-permute-done.mine3), channel_id=1, source_target_pairs={{0,1},{1,0},{2,3},{3,2},{4,5},{5,4},{6,7},{7,6},{8,9},{9,8},{10,11... | collective-permute-start | bytes 196616 | tf_op jit(solution)/shard_map/ppermute | solution.py:277
  15.2 1.6 %collective-permute-start.6 = (bf16[128,1024]{1,0:T(8,128)(2,1)S(1)}, bf16[128,1024]{1,0:T(8,128)(2,1)S(1)}, u32[]{:S(2)}, u32[]{:S(2)}) collective-permute-start(bf16[128,1024]{1,0:T(8,128)(2,1)S(1)} %get-tuple-element.84), channel_id=1, source_target_pairs={{0,1},{1,0},{2,3},{3,2},{4,5},{5,4},{6,7},{7,6},{8,9},{9,8},{10,11... | collective-permute-start | bytes 786440 | tf_op jit(solution)/shard_map/ppermute | solution.py:277
  16.9 8.5 %collective-permute-start.7 = (bf16[128,1024]{1,0:T(8,128)(2,1)S(1)}, bf16[128,1024]{1,0:T(8,128)(2,1)S(1)}, u32[]{:S(2)}, u32[]{:S(2)}) collective-permute-start(bf16[128,1024]{1,0:T(8,128)(2,1)S(1)} %get-tuple-element.89), channel_id=1, source_target_pairs={{0,2},{2,0},{1,3},{3,1},{4,6},{6,4},{5,7},{7,5},{8,10},{10,8},{9,1... | collective-permute-start | bytes 786440 | tf_op jit(solution)/shard_map/ppermute | solution.py:277
  25.4 1.6 %collective-permute-start.8 = (bf16[128,1024]{1,0:T(8,128)(2,1)S(1)}, bf16[128,1024]{1,0:T(8,128)(2,1)S(1)}, u32[]{:S(2)}, u32[]{:S(2)}) collective-permute-start(bf16[128,1024]{1,0:T(8,128)(2,1)S(1)} %shard_map.119.own_ref), channel_id=1, source_target_pairs={{0,1},{1,0},{2,3},{3,2},{4,5},{5,4},{6,7},{7,6},{8,9},{9,8},{10,11... | collective-permute-start | bytes 786440 | tf_op jit(solution)/shard_map/ppermute | solution.py:277
  27.6 10.8 %collective-permute-start.11 = (bf16[528,128]{1,0:T(8,128)(2,1)S(1)}, bf16[528,128]{1,0:T(8,128)(2,1)S(1)}, u32[]{:S(2)}, u32[]{:S(2)}) collective-permute-start(bf16[528,128]{1,0:T(8,128)(2,1)S(1)} %get-tuple-element.113), channel_id=1, source_target_pairs={{0,8},{4,12},{8,0},{12,4},{1,9},{5,13},{9,1},{13,5},{2,10},{6,14},... | collective-permute-start | bytes 405512 | tf_op jit(solution)/shard_map/ppermute | solution.py:277
  29.5 10.8 %collective-permute-start.10 = (bf16[528,128]{1,0:T(8,128)(2,1)S(1)}, bf16[528,128]{1,0:T(8,128)(2,1)S(1)}, u32[]{:S(2)}, u32[]{:S(2)}) collective-permute-start(bf16[528,128]{1,0:T(8,128)(2,1)S(1)} %shard_map.124), channel_id=1, source_target_pairs={{0,4},{4,0},{8,12},{12,8},{1,5},{5,1},{9,13},{13,9},{2,6},{6,2},{1... | collective-permute-start | bytes 405512 | tf_op jit(solution)/shard_map/ppermute | solution.py:277
  31.9 12.4 %copy-start = (f32[128]{0:T(128)S(1)}, f32[128]{0:T(128)}, u32[]{:S(2)}) copy-start(f32[128]{0:T(128)} %param.19) | copy-start | bytes 1540
  31.9 10.4 %collective-permute-start.9 = (bf16[528,128]{1,0:T(8,128)(2,1)S(1)}, bf16[528,128]{1,0:T(8,128)(2,1)S(1)}, u32[]{:S(2)}, u32[]{:S(2)}) collective-permute-start(bf16[528,128]{1,0:T(8,128)(2,1)S(1)} %shard_map.123), channel_id=1, source_target_pairs={{0,12},{4,8},{8,4},{12,0},{1,13},{5,9},{9,5},{13,1},{2,14},{6,10},... | collective-permute-start | bytes 405512 | tf_op jit(solution)/shard_map/ppermute | solution.py:277
  45.5 6.2 %collective-permute-start.12 = (bf16[128,256]{1,0:T(8,128)(2,1)S(1)}, bf16[128,256]{1,0:T(8,128)(2,1)S(1)}, u32[]{:S(2)}, u32[]{:S(2)}) collective-permute-start(bf16[128,256]{1,0:T(8,128)(2,1)S(1)} %get-tuple-element.131), channel_id=1, source_target_pairs={{0,12},{4,8},{8,4},{12,0},{1,13},{5,9},{9,5},{13,1},{2,14},{6,10},... | collective-permute-start | bytes 196616 | tf_op jit(solution)/shard_map/ppermute | solution.py:277
  47.8 5.2 %collective-permute-start.13 = (bf16[128,256]{1,0:T(8,128)(2,1)S(1)}, bf16[128,256]{1,0:T(8,128)(2,1)S(1)}, u32[]{:S(2)}, u32[]{:S(2)}) collective-permute-start(bf16[128,256]{1,0:T(8,128)(2,1)S(1)} %get-tuple-element.132), channel_id=1, source_target_pairs={{0,4},{4,0},{8,12},{12,8},{1,5},{5,1},{9,13},{13,9},{2,6},{6,2},{1... | collective-permute-start | bytes 196616 | tf_op jit(solution)/shard_map/ppermute | solution.py:277
  48.1 5.6 %collective-permute-start.14 = (bf16[128,256]{1,0:T(8,128)(2,1)S(1)}, bf16[128,256]{1,0:T(8,128)(2,1)S(1)}, u32[]{:S(2)}, u32[]{:S(2)}) collective-permute-start(bf16[128,256]{1,0:T(8,128)(2,1)S(1)} %get-tuple-element.133), channel_id=1, source_target_pairs={{0,8},{4,12},{8,0},{12,4},{1,9},{5,13},{9,1},{13,5},{2,10},{6,14},... | collective-permute-start | bytes 196616 | tf_op jit(solution)/shard_map/ppermute | solution.py:277

commit v6 on v5

--- a/solution.py
+++ b/solution.py
@@ -243,6 +243,7 @@
 IN_HBM = pl.BlockSpec(memory_space=pl.ANY)
 MIB = 2**20
 LANES = 128
+GROUPS = ((0,), (2,), (1,), (3,))
 
 
 def owners_fit(mesh):
@@ -468,10 +469,7 @@
     mixed = mixed_ref[:, columns] + dot(scaled_ref[...], weight_ref[weight_rows, columns])
     mixed = silu(mixed * scale_ref[:, 0:1])
     query, key = mixed[:, :DK], mixed[:, DK : 2 * DK]
-    payload_ref[0:rows] = (unit_rows(query) * DK ** (-0.5)).astype(jnp.bfloat16)
-    payload_ref[rows : 2 * rows] = unit_rows(key).astype(jnp.bfloat16)
-    payload_ref[2 * rows : 3 * rows] = mixed[:, 2 * DK : 2 * DK + DV].astype(jnp.bfloat16)
-    payload_ref[3 * rows : 4 * rows] = mixed[:, 2 * DK + DV :].astype(jnp.bfloat16)
+    payload_ref[0:rows] = unit_rows(key).astype(jnp.bfloat16)
     values = extra_ref.shape[0] // 2
     small[...] = jnp.zeros_like(small)
     for place, base in ((0, 0), (4, values)):
@@ -479,7 +477,10 @@
         high = full.astype(jnp.bfloat16).astype(jnp.float32)
         small[place : place + 2] = high
         small[place + 2 : place + 4] = full - high
-    payload_ref[4 * rows : 4 * rows + 16] = small[...].astype(jnp.bfloat16)
+    payload_ref[rows : rows + 16] = small[...].astype(jnp.bfloat16)
+    rest = (unit_rows(query) * DK ** (-0.5), mixed[:, 2 * DK : 2 * DK + DV], mixed[:, 2 * DK + DV :])
+    for number, part in enumerate(rest, 1):
+        payload_ref[number * rows + 16 : (number + 1) * rows + 16] = part.astype(jnp.bfloat16)
 
 
 def joined(left, right):
@@ -513,10 +514,8 @@
     return [results[n] + joined(quads[n], halves(results[n])) for n in number]
 
 
-def block_kernel(mask, payload_ref, *refs):
-    offset_ref, linear_ref, local_ref, growth_ref = refs[-4:]
-    source = jnp.bitwise_xor(lax.axis_index("ctx"), mask)
-    rows = (payload_ref.shape[0] - 16) // 4
+def key_terms(chunks):
+    rows = chunks[0][0].shape[0]
     half = rows // 2
     shift = half.bit_length() - 1
     row = lax.broadcasted_iota(jnp.int32, (rows, 1), 0)
@@ -527,50 +526,76 @@
     early = column < half
     below = jnp.where(inclusive, 1.0, 0.0).astype(jnp.bfloat16)
     diagonal = jnp.where(row == column, 1.0, 0.0).astype(jnp.bfloat16)
-    heads = range(2)
-    query, key = payload_ref[0:rows], payload_ref[rows : 2 * rows]
-    extra = payload_ref[4 * rows : 4 * rows + 16]
-    sums_row = dot(extra, below, ((1,), (1,)))
-    turned = dot(jnp.concatenate([below, diagonal], axis=0), extra, ((1,), (1,)))
-    key_gram = dot(key, key, ((1,), (1,)))
-    total_rows = [sums_row[h : h + 1] + sums_row[h + 2 : h + 3] for h in heads]
-    totals = [turned[:rows, h : h + 1] + turned[:rows, h + 2 : h + 3] for h in heads]
-    betas = [turned[rows:, h + 4 : h + 5] + turned[rows:, h + 6 : h + 7] for h in heads]
-    decays = [jnp.exp(jnp.where(inclusive, totals[h] - total_rows[h], NEGATIVE)) for h in heads]
-    stricts = [jnp.where(strictly, betas[h] * key_gram * decays[h], 0.0) for h in heads]
+    below, diagonal = (jnp.concatenate([left, left], axis=1) for left in (below, diagonal))
+    items = [(chunk, head) for chunk in range(len(chunks)) for head in range(2)]
+    keys = [key for key, _ in chunks]
+    extras = [extra.astype(jnp.float32) for _, extra in chunks]
+
+    def spread(left, chunk, place):
+        lanes = [
+            jnp.broadcast_to(extras[chunk][n : n + 1], (rows, rows)).astype(jnp.bfloat16) for n in (place, place + 2)
+        ]
+        return dot(left, jnp.concatenate(lanes, axis=1), ((1,), (1,)))
+
+    sums = [dot(extra, below[:, :rows], ((1,), (1,))) for _, extra in chunks]
+    key_grams = [dot(key, key, ((1,), (1,))) for key in keys]
+    totals = {item: spread(below, *item) for item in items}
+    betas = {(chunk, head): spread(diagonal, chunk, head + 4) for chunk, head in items}
+    total_rows = {(c, h): sums[c][h : h + 1] + sums[c][h + 2 : h + 3] for c, h in items}
+    decays = {item: jnp.exp(jnp.where(inclusive, totals[item] - total_rows[item], NEGATIVE)) for item in items}
+    stricts = [jnp.where(strictly, betas[item] * key_grams[item[0]] * decays[item], 0.0) for item in items]
+    wide = [key.astype(jnp.float32) for key in keys]
+    turned = [jnp.transpose(key) for key in wide]
+    growths = {item: jnp.exp(totals[item]) for item in items}
+    inverses = [halves(inverse) for inverse in unit_lower_inverses(stricts, row, column)]
+    terms = []
+    for item, (high, low) in zip(items, inverses):
+        total = total_rows[item]
+        end = jnp.where(early, total[:, half - 1 : half], total[:, rows - 1 : rows])
+        carried = turned[item[0]] * jnp.exp(end - total)
+        carried = [jnp.where(early, carried, 0.0), jnp.where(early, 0.0, carried)]
+        weighted = (betas[item] * growths[item] * wide[item[0]]).astype(jnp.bfloat16)
+        lefts = jnp.concatenate(carried, axis=0).astype(jnp.bfloat16)
+        terms.append((betas[item], decays[item], growths[item], weighted, lefts, high, low, jnp.exp(end)))
+    return terms
+
+
+def finish_terms(source, query, key, values, terms, offset_ref, linear_ref, local_ref, growth_ref):
+    rows = query.shape[0]
+    half = rows // 2
     query_gram = dot(query, key, ((1,), (1,)))
-    key_wide = key.astype(jnp.float32)
-    key_turned = jnp.transpose(key_wide)
-    growths = [jnp.exp(total) for total in totals]
-    values = [payload_ref[(2 + h) * rows : (3 + h) * rows].astype(jnp.float32) for h in heads]
-    rights = [
-        jnp.concatenate([betas[h] * values[h], (betas[h] * growths[h]) * key_wide], axis=1).astype(jnp.bfloat16)
-        for h in heads
-    ]
-    grams = [(query_gram * decays[h]).astype(jnp.bfloat16) for h in heads]
-    ends = [jnp.where(early, total[:, half - 1 : half], total[:, rows - 1 : rows]) for total in total_rows]
-    carried = [key_turned * jnp.exp(ends[h] - total_rows[h]) for h in heads]
-    lefts = [
-        jnp.concatenate([jnp.where(early, keys, 0.0), jnp.where(early, 0.0, keys)], axis=0).astype(jnp.bfloat16)
-        for keys in carried
-    ]
-    inverses = [halves(inverse) for inverse in unit_lower_inverses(stricts, row, column)]
-    solved = [
-        (dot(high, right) + dot(low, right)).astype(jnp.bfloat16) for (high, low), right in zip(inverses, rights)
-    ]
-    moved = [dot(jnp.concatenate([lefts[h], grams[h]], axis=0), solved[h]) for h in heads]
-    for h in heads:
-        attended = moved[h][2 * DK :]
-        local_ref[source, h] = attended[:, :DV]
-        reads = (growths[h] * query.astype(jnp.float32) - attended[:, DV:]).astype(jnp.bfloat16)
-        growth = jnp.exp(ends[h])
+    solved = []
+    for value, (beta, _, _, weighted, _, high, low, _) in zip(values, terms):
+        right = jnp.concatenate([(beta * value.astype(jnp.float32)).astype(jnp.bfloat16), weighted], axis=1)
+        solved.append((dot(high, right) + dot(low, right)).astype(jnp.bfloat16))
+    moved = []
+    for part, (_, decay, _, _, lefts, _, _, _) in zip(solved, terms):
+        moved.append(dot(jnp.concatenate([lefts, (query_gram * decay).astype(jnp.bfloat16)], axis=0), part))
+    for head, (part, (_, _, growth, _, _, _, _, ends)) in enumerate(zip(moved, terms)):
+        attended = part[2 * DK :]
+        local_ref[source, head] = attended[:, :DV]
+        reads = (growth * query.astype(jnp.float32) - attended[:, DV:]).astype(jnp.bfloat16)
         for block in range(2):
-            state = moved[h][block * DK : (block + 1) * DK]
-            offset_ref[source, h, block] = state[:, :DV]
-            linear_ref[source, h, block, 0:DK] = state[:, DV:].astype(jnp.bfloat16)
-            linear_ref[source, h, block, DK : DK + half] = reads[block * half : (block + 1) * half]
+            state = part[block * DK : (block + 1) * DK]
+            offset_ref[source, head, block] = state[:, :DV]
+            linear_ref[source, head, block, 0:DK] = state[:, DV:].astype(jnp.bfloat16)
+            linear_ref[source, head, block, DK : DK + half] = reads[block * half : (block + 1) * half]
             last = (block + 1) * half - 1
-            growth_ref[source, h, block] = jnp.broadcast_to(growth[:, last : last + 1], growth_ref.shape[3:])
+            growth_ref[source, head, block] = jnp.broadcast_to(ends[:, last : last + 1], growth_ref.shape[3:])
+
+
+def source_of(mask):
+    return jnp.bitwise_xor(lax.axis_index("ctx"), mask)
+
+
+def block_kernel(masks, *refs):
+    payload_refs, outs = refs[: len(masks)], refs[-4:]
+    rows = (payload_refs[0].shape[0] - 16) // 4
+    keys = [ref[0:rows] for ref in payload_refs]
+    terms = key_terms([(key, ref[rows : rows + 16]) for key, ref in zip(keys, payload_refs)])
+    for number, (mask, ref) in enumerate(zip(masks, payload_refs)):
+        query, *values = (ref[n * rows + 16 : (n + 1) * rows + 16] for n in (1, 2, 3))
+        finish_terms(source_of(mask), query, keys[number], values, terms[2 * number : 2 * number + 2], *outs)
 
 
 def scan_kernel(offset_ref, linear_ref, local_ref, growth_ref, gain_ref, own_ref, back1, back2, back3, outs):
@@ -638,7 +663,9 @@
     piece, *late = lax.optimization_barrier((piece, att_query, att_gate, att_kv, out_weight, residual))
     late = fetched(*late)
     mine[3], (att_query, att_gate, att_kv, out_weight, residual) = lax.optimization_barrier((mine[3], late))
-    twin = {mask: swapped(mine[mask], "sub") for mask in masks}
+    twin = {3: swapped(mine[3], "sub"), 1: swapped(mine[1], "sub")}
+    mine[2] = lax.optimization_barrier((mine[2], twin[3]))[0]
+    twin[2] = swapped(mine[2], "sub")
     heads, send = vmem_call(
         attention_kernel,
         [((rows, head_columns), bf16), ((rows, half_model), bf16)],
@@ -693,12 +720,12 @@
         ((4, 2, 2, 8, LANES), f32),
     ]
     terms = []
-    for mask in (0, 2, 1, 3):
+    for group in GROUPS:
         terms = vmem_call(
-            functools.partial(block_kernel, mask),
+            functools.partial(block_kernel, group),
             terms_shapes,
-            [came[mask], *terms],
-            aliases={1 + i: i for i in range(4)} if terms else None,
+            [*(came[mask] for mask in group), *terms],
+            aliases={len(group) + i: i for i in range(4)} if terms else None,
         )
     own, *backs = vmem_call(
         scan_kernel,

time: 54.6 us -> 54.2 us (level)
  transfers between devices with their start and end apart: 15 -> 15, of which waited for: 11 -> 10; matrix products, arithmetic and copies ran while one was open for 0% -> 0% of each run, Pallas kernels for 28% -> 28%
where the time goes in v6:
time: 54.2 us; the launch traced here: 54 us
  Pallas kernels  21.6 us (40%)
  starting transfers between devices  16.8 us (31%)
  waiting for transfers between devices  14.8 us (27%)
  between operations  0.81 us (1%)
    ppermute x15, starting transfers between devices, swapped(): lax.ppermute(value, axis, [(i, i ^ mask) for i in range(lax.axis_size(axi...  16.8 us
    ppermute x15, waiting for transfers between devices, swapped(): lax.ppermute(value, axis, [(i, i ^ mask) for i in range(lax.axis_size(axi...  14.8 us
    pallas_call x15, Pallas kernels, vmem_call(): pl.pallas_call(kernel, out_shape=[make(shape, dtype) for shape, dtype in...  14.1 us
    pallas_call x2, Pallas kernels, fetched(): pl.pallas_call(fetch_kernel, out_shape=[pltpu.VMEM(array.shape, array.dty...  5.9 us
  transfers between devices with their start and end apart: 15, of which 10 were waited for; matrix products, arithmetic and copies ran while one was open for 0% of the time, Pallas kernels for 28%

profile of v6, /device:TPU:0, one launch (start us, length us, event | category | flops | bytes accessed | tf_op | source)
XLA Modules:
  0.0 54.0 jit_solution(10705376484582057932)
XLA Ops:
  0.6 0.9 %shard_map.113 = bf16[128,256]{1,0:T(8,128)(2,1)S(1)} custom-call(bf16[128,1024]{1,0:T(8,128)(2,1)} %refs_2_), custom_call_target="tpu_custom_call" | custom-call | tf_op jit(solution)/shard_map/pallas_call | solution.py:654
  1.5 5.1 %collective-permute-start = (bf16[128,256]{1,0:T(8,128)(2,1)S(1)}, bf16[128,256]{1,0:T(8,128)(2,1)S(1)}, u32[]{:S(2)}, u32[]{:S(2)}) collective-permute-start(bf16[128,256]{1,0:T(8,128)(2,1)S(1)} %shard_map.113), channel_id=1, source_target_pairs={{0,12},{4,8},{8,4},{12,0},{1,13},{5,9},{9,5},{13,1},{2,14},{6,10},... | collective-permute-start | bytes 196616 | tf_op jit(solution)/shard_map/ppermute | solution.py:278
  6.6 0.0 collective-permute-start.2
  6.6 0.6 %collective-permute-start.1 = (bf16[128,256]{1,0:T(8,128)(2,1)S(1)}, bf16[128,256]{1,0:T(8,128)(2,1)S(1)}, u32[]{:S(2)}, u32[]{:S(2)}) collective-permute-start(bf16[128,256]{1,0:T(8,128)(2,1)S(1)} %shard_map.113), channel_id=1, source_target_pairs={{0,4},{4,0},{8,12},{12,8},{1,5},{5,1},{9,13},{13,9},{2,6},{6,2},{1... | collective-permute-start | bytes 196616 | tf_op jit(solution)/shard_map/ppermute | solution.py:278
  7.3 2.5 %shard_map.114 = (bf16[128,1024]{1,0:T(8,128)(2,1)S(1)}, bf16[128,1024]{1,0:T(8,128)(2,1)S(1)}, bf16[128,1024]{1,0:T(8,128)(2,1)S(1)}, bf16[1024,2048]{1,0:T(8,128)(2,1)S(1)}, bf16[128,512]{1,0:T(8,128)(2,1)S(1)}) custom-call(bf16[128,1024]{1,0:T(8,128)(2,1)} %refs_0_, bf16[128,1024]{1,0:T(8,128)(2,1)} %refs_1_, bf16[128,1024]{1,0:T(8,128)(2,1)} %refs_2_, ...), custom_call_target="tpu_custom_call" | custom-call | bytes 5111808 | tf_op jit(solution)/shard_map/pallas_call | solution.py:318
  9.7 0.0 collective-permute-done.mine3
  9.8 0.1 collective-permute-start.3
  9.8 1.0 %collective-permute-done.1.mine1 = bf16[128,256]{1,0:T(8,128)(2,1)S(1)} collective-permute-done((bf16[128,256]{1,0:T(8,128)(2,1)S(1)}, bf16[128,256]{1,0:T(8,128)(2,1)S(1)}, u32[]{:S(2)}, u32[]{:S(2)}) %collective-permute-start.1) | collective-permute-done | bytes 65568 | tf_op jit(solution)/shard_map/ppermute | solution.py:278
  10.9 0.0 collective-permute-start.4
  10.9 1.3 %collective-permute-done.2.mine2 = bf16[128,256]{1,0:T(8,128)(2,1)S(1)} collective-permute-done((bf16[128,256]{1,0:T(8,128)(2,1)S(1)}, bf16[128,256]{1,0:T(8,128)(2,1)S(1)}, u32[]{:S(2)}, u32[]{:S(2)}) %collective-permute-start.2) | collective-permute-done | bytes 65568 | tf_op jit(solution)/shard_map/ppermute | solution.py:278
  12.2 0.0 collective-permute-done.3.twin3
  12.2 0.0 collective-permute-start.5
  12.2 1.2 %collective-permute-done.5.twin2 = bf16[128,256]{1,0:T(8,128)(2,1)S(1)} collective-permute-done((bf16[128,256]{1,0:T(8,128)(2,1)S(1)}, bf16[128,256]{1,0:T(8,128)(2,1)S(1)}, u32[]{:S(2)}, u32[]{:S(2)}) %collective-permute-start.5) | collective-permute-done | bytes 65568 | tf_op jit(solution)/shard_map/ppermute | solution.py:278
  13.5 1.2 %shard_map.115 = (bf16[128,1024]{1,0:T(8,128)(2,1)S(1)}, bf16[128,1024]{1,0:T(8,128)(2,1)S(1)}) custom-call(bf16[128,1024]{1,0:T(8,128)(2,1)S(1)} %get-tuple-element.79.query_ref, bf16[128,1024]{1,0:T(8,128)(2,1)S(1)} %get-tuple-element.80.gate_ref, bf16[128,1024]{1,0:T(8,128)(2,1)S(1)} %get-tuple-element.81.kv_ref, ...), custom_call_target="tpu_custom_call" | custom-call | tf_op jit(solution)/shard_map/pallas_call | solution.py:265
  14.7 0.2 collective-permute-start.6
  14.9 0.5 shard_map.116.keep_ref
  15.4 0.9 %collective-permute-done.6.came_ref = bf16[128,1024]{1,0:T(8,128)(2,1)S(1)} collective-permute-done((bf16[128,1024]{1,0:T(8,128)(2,1)S(1)}, bf16[128,1024]{1,0:T(8,128)(2,1)S(1)}, u32[]{:S(2)}, u32[]{:S(2)}) %collective-permute-start.6) | collective-permute-done | bytes 262176 | tf_op jit(solution)/shard_map/ppermute | solution.py:278
  16.3 0.1 shard_map.117
  16.4 1.6 %collective-permute-start.7 = (bf16[128,1024]{1,0:T(8,128)(2,1)S(1)}, bf16[128,1024]{1,0:T(8,128)(2,1)S(1)}, u32[]{:S(2)}, u32[]{:S(2)}) collective-permute-start(bf16[128,1024]{1,0:T(8,128)(2,1)S(1)} %get-tuple-element.91), channel_id=1, source_target_pairs={{0,2},{2,0},{1,3},{3,1},{4,6},{6,4},{5,7},{7,5},{8,10},{10,8},{9,1... | collective-permute-start | bytes 786440 | tf_op jit(solution)/shard_map/ppermute | solution.py:278
  18.0 3.4 %shard_map.118 = (bf16[2048,2048]{1,0:T(8,128)(2,1)S(1)}, f32[1,2048]{1,0:T(1,128)S(1)}, bf16[8,2048]{1,0:T(8,128)(2,1)S(1)}, f32[8,128]{1,0:T(8,128)S(1)}) custom-call(bf16[2048,2048]{1,0:T(8,128)(2,1)} %refs_0_.1, f32[1,2048]{1,0:T(1,128)} %bitcast.6, bf16[8,2048]{1,0:T(8,128)(2,1)} %bitcast.5, f32[8,128]{1,0:T(8,128)} %bitcast.7), custom_call_target="tpu_custom_call" | custom-call | bytes 8433664 | tf_op jit(solution)/shard_map/pallas_call | solution.py:318
  21.4 3.5 %collective-permute-done.7.came_ref = bf16[128,1024]{1,0:T(8,128)(2,1)S(1)} collective-permute-done((bf16[128,1024]{1,0:T(8,128)(2,1)S(1)}, bf16[128,1024]{1,0:T(8,128)(2,1)S(1)}, u32[]{:S(2)}, u32[]{:S(2)}) %collective-permute-start.7) | collective-permute-done | bytes 262176 | tf_op jit(solution)/shard_map/ppermute | solution.py:278
  24.9 0.1 collective-permute-start.8
  25.0 0.8 %shard_map.120 = (f32[128,2048]{1,0:T(8,128)S(1)}, f32[8,128]{1,0:T(8,128)S(1)}, f32[128,128]{1,0:T(8,128)S(1)}) custom-call(bf16[128,1024]{1,0:T(8,128)(2,1)S(1)} %shard_map.119.own_ref, f32[1,2048]{1,0:T(1,128)S(1)} %get-tuple-element.101.gain_ref, bf16[2048,2048]{1,0:T(8,128)(2,1)S(1)} %get-tuple-element.102.weight_ref, ...), custom_call_target="tpu_custom_call" | custom-call | tf_op jit(solution)/shard_map/pallas_call | solution.py:265
  25.8 0.7 %collective-permute-done.8.twin_ref = bf16[128,1024]{1,0:T(8,128)(2,1)S(1)} collective-permute-done((bf16[128,1024]{1,0:T(8,128)(2,1)S(1)}, bf16[128,1024]{1,0:T(8,128)(2,1)S(1)}, u32[]{:S(2)}, u32[]{:S(2)}) %collective-permute-start.8) | collective-permute-done | bytes 262176 | tf_op jit(solution)/shard_map/ppermute | solution.py:278
  26.5 0.6 %shard_map.122 = (bf16[128,1024]{1,0:T(8,128)(2,1)S(1)}, f32[128,128]{1,0:T(8,128)S(1)}, f32[16,128]{1,0:T(8,128)S(1)}, bf16[528,128]{1,0:T(8,128)(2,1)S(1)}) custom-call(bf16[128,1024]{1,0:T(8,128)(2,1)S(1)} %collective-permute-done.8.twin_ref, f32[1,2048]{1,0:T(1,128)S(1)} %get-tuple-element.101.gain_ref, bf16[8,2048]{1,0:T(8,128)(2,1)S(1)} %get-tuple-element.103.beta_ref, ...), custom_call_target="tpu_custom_call" | custom-call | tf_op jit(solution)/shard_map/pallas_call | solution.py:265
  27.1 2.0 %collective-permute-start.11 = (bf16[528,128]{1,0:T(8,128)(2,1)S(1)}, bf16[528,128]{1,0:T(8,128)(2,1)S(1)}, u32[]{:S(2)}, u32[]{:S(2)}) collective-permute-start(bf16[528,128]{1,0:T(8,128)(2,1)S(1)} %get-tuple-element.115), channel_id=1, source_target_pairs={{0,8},{4,12},{8,0},{12,4},{1,9},{5,13},{9,1},{13,5},{2,10},{6,14},... | collective-permute-start | bytes 405512 | tf_op jit(solution)/shard_map/ppermute | solution.py:278
  29.1 0.5 shard_map.124
  29.5 1.4 %collective-permute-start.10 = (bf16[528,128]{1,0:T(8,128)(2,1)S(1)}, bf16[528,128]{1,0:T(8,128)(2,1)S(1)}, u32[]{:S(2)}, u32[]{:S(2)}) collective-permute-start(bf16[528,128]{1,0:T(8,128)(2,1)S(1)} %shard_map.124), channel_id=1, source_target_pairs={{0,4},{4,0},{8,12},{12,8},{1,5},{5,1},{9,13},{13,9},{2,6},{6,2},{1... | collective-permute-start | bytes 405512 | tf_op jit(solution)/shard_map/ppermute | solution.py:278
  30.9 0.5 shard_map.123
  31.4 0.0 copy-start
  31.4 1.2 %collective-permute-start.9 = (bf16[528,128]{1,0:T(8,128)(2,1)S(1)}, bf16[528,128]{1,0:T(8,128)(2,1)S(1)}, u32[]{:S(2)}, u32[]{:S(2)}) collective-permute-start(bf16[528,128]{1,0:T(8,128)(2,1)S(1)} %shard_map.123), channel_id=1, source_target_pairs={{0,12},{4,8},{8,4},{12,0},{1,13},{5,9},{9,5},{13,1},{2,14},{6,10},... | collective-permute-start | bytes 405512 | tf_op jit(solution)/shard_map/ppermute | solution.py:278
  32.6 0.5 shard_map.125.refs_0_
  33.0 1.9 %shard_map.126 = (f32[4,2,2,128,128]{4,3,2,1,0:T(8,128)S(1)}, bf16[4,2,2,192,128]{4,3,2,1,0:T(8,128)(2,1)S(1)}, f32[4,2,128,128]{3,2,1,0:T(8,128)S(1)}, f32[4,2,2,8,128]{4,3,2,1,0:T(8,128)S(1)}) custom-call(bf16[528,128]{1,0:T(8,128)(2,1)S(1)} %shard_map.125.refs_0_), custom_call_target="tpu_custom_call" | custom-call | tf_op jit(solution)/shard_map/pallas_call | solution.py:265
  35.0 3.1 %collective-permute-done.11.refs_0_ = bf16[528,128]{1,0:T(8,128)(2,1)S(1)} collective-permute-done((bf16[528,128]{1,0:T(8,128)(2,1)S(1)}, bf16[528,128]{1,0:T(8,128)(2,1)S(1)}, u32[]{:S(2)}, u32[]{:S(2)}) %collective-permute-start.11) | collective-permute-done | bytes 135200 | tf_op jit(solution)/shard_map/ppermute | solution.py:278
  38.0 1.9 %shard_map.127 = (f32[4,2,2,128,128]{4,3,2,1,0:T(8,128)S(1)}, bf16[4,2,2,192,128]{4,3,2,1,0:T(8,128)(2,1)S(1)}, f32[4,2,128,128]{3,2,1,0:T(8,128)S(1)}, f32[4,2,2,8,128]{4,3,2,1,0:T(8,128)S(1)}) custom-call(bf16[528,128]{1,0:T(8,128)(2,1)S(1)} %collective-permute-done.11.refs_0_, ...), custom_call_target="tpu_custom_call", output_to_operand_aliasing={{0}: (1, {}), {1}: (2, {}), {2}: (3, {}), {3}: (4, {})} | custom-call | tf_op jit(solution)/shard_map/pallas_call | solution.py:265
  40.0 0.0 collective-permute-done.10.refs_0_
  40.0 1.9 %shard_map.128 = (f32[4,2,2,128,128]{4,3,2,1,0:T(8,128)S(1)}, bf16[4,2,2,192,128]{4,3,2,1,0:T(8,128)(2,1)S(1)}, f32[4,2,128,128]{3,2,1,0:T(8,128)S(1)}, f32[4,2,2,8,128]{4,3,2,1,0:T(8,128)S(1)}) custom-call(bf16[528,128]{1,0:T(8,128)(2,1)S(1)} %collective-permute-done.10.refs_0_, ...), custom_call_target="tpu_custom_call", output_to_operand_aliasing={{0}: (1, {}), {1}: (2, {}), {2}: (3, {}), {3}: (4, {})} | custom-call | tf_op jit(solution)/shard_map/pallas_call | solution.py:265
  41.9 0.0 collective-permute-done.9.refs_0_
  41.9 1.9 %shard_map.129 = (f32[4,2,2,128,128]{4,3,2,1,0:T(8,128)S(1)}, bf16[4,2,2,192,128]{4,3,2,1,0:T(8,128)(2,1)S(1)}, f32[4,2,128,128]{3,2,1,0:T(8,128)S(1)}, f32[4,2,2,8,128]{4,3,2,1,0:T(8,128)S(1)}) custom-call(bf16[528,128]{1,0:T(8,128)(2,1)S(1)} %collective-permute-done.9.refs_0_, ...), custom_call_target="tpu_custom_call", output_to_operand_aliasing={{0}: (1, {}), {1}: (2, {}), {2}: (3, {}), {3}: (4, {})} | custom-call | tf_op jit(solution)/shard_map/pallas_call | solution.py:265
  43.9 1.2 %shard_map.130 = (bf16[128,256]{1,0:T(8,128)(2,1)S(1)}, bf16[128,256]{1,0:T(8,128)(2,1)S(1)}, bf16[128,256]{1,0:T(8,128)(2,1)S(1)}, bf16[128,256]{1,0:T(8,128)(2,1)S(1)}) custom-call(f32[4,2,2,128,128]{4,3,2,1,0:T(8,128)S(1)} %get-tuple-element.128.offset_ref, bf16[4,2,2,192,128]{4,3,2,1,0:T(8,128)(2,1)S(1)} %get-tuple-element.129.linear_ref, ...), custom_call_target="tpu_custom_call" | custom-call | tf_op jit(solution)/shard_map/pallas_call | solution.py:265
  45.0 2.4 %collective-permute-start.12 = (bf16[128,256]{1,0:T(8,128)(2,1)S(1)}, bf16[128,256]{1,0:T(8,128)(2,1)S(1)}, u32[]{:S(2)}, u32[]{:S(2)}) collective-permute-start(bf16[128,256]{1,0:T(8,128)(2,1)S(1)} %get-tuple-element.133), channel_id=1, source_target_pairs={{0,12},{4,8},{8,4},{12,0},{1,13},{5,9},{9,5},{13,1},{2,14},{6,10},... | collective-permute-start | bytes 196616 | tf_op jit(solution)/shard_map/ppermute | solution.py:278
  47.4 0.5 collective-permute-start.13
  48.0 1.5 %collective-permute-start.14 = (bf16[128,256]{1,0:T(8,128)(2,1)S(1)}, bf16[128,256]{1,0:T(8,128)(2,1)S(1)}, u32[]{:S(2)}, u32[]{:S(2)}) collective-permute-start(bf16[128,256]{1,0:T(8,128)(2,1)S(1)} %get-tuple-element.135), channel_id=1, source_target_pairs={{0,8},{4,12},{8,0},{12,4},{1,9},{5,13},{9,1},{13,5},{2,10},{6,14},... | collective-permute-start | bytes 196616 | tf_op jit(solution)/shard_map/ppermute | solution.py:278
  49.5 0.7 %shard_map.121 = bf16[128,512]{1,0:T(8,128)(2,1)} custom-call(bf16[128,1024]{1,0:T(8,128)(2,1)S(1)} %shard_map.119.own_ref, bf16[128,1024]{1,0:T(8,128)(2,1)S(1)} %collective-permute-done.8.twin_ref), custom_call_target="tpu_custom_call" | custom-call | tf_op jit(solution)/shard_map/pallas_call | solution.py:265
  50.2 1.2 %collective-permute-done.12.back3 = bf16[128,256]{1,0:T(8,128)(2,1)S(1)} collective-permute-done((bf16[128,256]{1,0:T(8,128)(2,1)S(1)}, bf16[128,256]{1,0:T(8,128)(2,1)S(1)}, u32[]{:S(2)}, u32[]{:S(2)}) %collective-permute-start.12) | collective-permute-done | bytes 65568 | tf_op jit(solution)/shard_map/ppermute | solution.py:278
  51.3 1.2 %collective-permute-done.13.back1 = bf16[128,256]{1,0:T(8,128)(2,1)S(1)} collective-permute-done((bf16[128,256]{1,0:T(8,128)(2,1)S(1)}, bf16[128,256]{1,0:T(8,128)(2,1)S(1)}, u32[]{:S(2)}, u32[]{:S(2)}) %collective-permute-start.13) | collective-permute-done | bytes 65568 | tf_op jit(solution)/shard_map/ppermute | solution.py:278
  52.5 0.8 %collective-permute-done.14.back2 = bf16[128,256]{1,0:T(8,128)(2,1)S(1)} collective-permute-done((bf16[128,256]{1,0:T(8,128)(2,1)S(1)}, bf16[128,256]{1,0:T(8,128)(2,1)S(1)}, u32[]{:S(2)}, u32[]{:S(2)}) %collective-permute-start.14) | collective-permute-done | bytes 65568 | tf_op jit(solution)/shard_map/ppermute | solution.py:278
  53.3 0.7 %shard_map.131 = bf16[128,1024]{1,0:T(8,128)(2,1)} custom-call(bf16[128,256]{1,0:T(8,128)(2,1)S(1)} %get-tuple-element.132.own_ref, bf16[128,256]{1,0:T(8,128)(2,1)S(1)} %collective-permute-done.12.back3, bf16[128,256]{1,0:T(8,128)(2,1)S(1)} %collective-permute-done.13.back1, bf16[128,256]{1,0:T(8,128)(2,1)S(1)} %collective-permute-done.14.back2), custom_call_target="tpu_custom_call" | custom-call | tf_op jit(solution)/shard_map/pallas_call | solution.py:737
  (3 shorter events, 0.1 us)
Async XLA Ops:
  1.5 8.3 %collective-permute-start = (bf16[128,256]{1,0:T(8,128)(2,1)S(1)}, bf16[128,256]{1,0:T(8,128)(2,1)S(1)}, u32[]{:S(2)}, u32[]{:S(2)}) collective-permute-start(bf16[128,256]{1,0:T(8,128)(2,1)S(1)} %shard_map.113), channel_id=1, source_target_pairs={{0,12},{4,8},{8,4},{12,0},{1,13},{5,9},{9,5},{13,1},{2,14},{6,10},... | collective-permute-start | bytes 196616 | tf_op jit(solution)/shard_map/ppermute | solution.py:278
  6.6 5.6 %collective-permute-start.2 = (bf16[128,256]{1,0:T(8,128)(2,1)S(1)}, bf16[128,256]{1,0:T(8,128)(2,1)S(1)}, u32[]{:S(2)}, u32[]{:S(2)}) collective-permute-start(bf16[128,256]{1,0:T(8,128)(2,1)S(1)} %shard_map.113), channel_id=1, source_target_pairs={{0,8},{4,12},{8,0},{12,4},{1,9},{5,13},{9,1},{13,5},{2,10},{6,14},... | collective-permute-start | bytes 196616 | tf_op jit(solution)/shard_map/ppermute | solution.py:278
  6.6 4.3 %collective-permute-start.1 = (bf16[128,256]{1,0:T(8,128)(2,1)S(1)}, bf16[128,256]{1,0:T(8,128)(2,1)S(1)}, u32[]{:S(2)}, u32[]{:S(2)}) collective-permute-start(bf16[128,256]{1,0:T(8,128)(2,1)S(1)} %shard_map.113), channel_id=1, source_target_pairs={{0,4},{4,0},{8,12},{12,8},{1,5},{5,1},{9,13},{13,9},{2,6},{6,2},{1... | collective-permute-start | bytes 196616 | tf_op jit(solution)/shard_map/ppermute | solution.py:278
  9.8 2.5 %collective-permute-start.3 = (bf16[128,256]{1,0:T(8,128)(2,1)S(1)}, bf16[128,256]{1,0:T(8,128)(2,1)S(1)}, u32[]{:S(2)}, u32[]{:S(2)}) collective-permute-start(bf16[128,256]{1,0:T(8,128)(2,1)S(1)} %collective-permute-done.mine3), channel_id=1, source_target_pairs={{0,1},{1,0},{2,3},{3,2},{4,5},{5,4},{6,7},{7,6},{8,9},{9,8},{10,11... | collective-permute-start | bytes 196616 | tf_op jit(solution)/shard_map/ppermute | solution.py:278
  10.9 1.3 %collective-permute-start.4 = (bf16[128,256]{1,0:T(8,128)(2,1)S(1)}, bf16[128,256]{1,0:T(8,128)(2,1)S(1)}, u32[]{:S(2)}, u32[]{:S(2)}) collective-permute-start(bf16[128,256]{1,0:T(8,128)(2,1)S(1)} %collective-permute-done.1.mine1), channel_id=1, source_target_pairs={{0,1},{1,0},{2,3},{3,2},{4,5},{5,4},{6,7},{7,6},{8,9},{9,8},{10,11... | collective-permute-start | bytes 196616 | tf_op jit(solution)/shard_map/ppermute | solution.py:278
  12.2 1.3 %collective-permute-start.5 = (bf16[128,256]{1,0:T(8,128)(2,1)S(1)}, bf16[128,256]{1,0:T(8,128)(2,1)S(1)}, u32[]{:S(2)}, u32[]{:S(2)}) collective-permute-start(bf16[128,256]{1,0:T(8,128)(2,1)S(1)} %collective-permute-done.2.mine2), channel_id=1, source_target_pairs={{0,1},{1,0},{2,3},{3,2},{4,5},{5,4},{6,7},{7,6},{8,9},{9,8},{10,11... | collective-permute-start | bytes 196616 | tf_op jit(solution)/shard_map/ppermute | solution.py:278
  14.7 1.6 %collective-permute-start.6 = (bf16[128,1024]{1,0:T(8,128)(2,1)S(1)}, bf16[128,1024]{1,0:T(8,128)(2,1)S(1)}, u32[]{:S(2)}, u32[]{:S(2)}) collective-permute-start(bf16[128,1024]{1,0:T(8,128)(2,1)S(1)} %get-tuple-element.86), channel_id=1, source_target_pairs={{0,1},{1,0},{2,3},{3,2},{4,5},{5,4},{6,7},{7,6},{8,9},{9,8},{10,11... | collective-permute-start | bytes 786440 | tf_op jit(solution)/shard_map/ppermute | solution.py:278
  16.4 8.5 %collective-permute-start.7 = (bf16[128,1024]{1,0:T(8,128)(2,1)S(1)}, bf16[128,1024]{1,0:T(8,128)(2,1)S(1)}, u32[]{:S(2)}, u32[]{:S(2)}) collective-permute-start(bf16[128,1024]{1,0:T(8,128)(2,1)S(1)} %get-tuple-element.91), channel_id=1, source_target_pairs={{0,2},{2,0},{1,3},{3,1},{4,6},{6,4},{5,7},{7,5},{8,10},{10,8},{9,1... | collective-permute-start | bytes 786440 | tf_op jit(solution)/shard_map/ppermute | solution.py:278
  24.9 1.6 %collective-permute-start.8 = (bf16[128,1024]{1,0:T(8,128)(2,1)S(1)}, bf16[128,1024]{1,0:T(8,128)(2,1)S(1)}, u32[]{:S(2)}, u32[]{:S(2)}) collective-permute-start(bf16[128,1024]{1,0:T(8,128)(2,1)S(1)} %shard_map.119.own_ref), channel_id=1, source_target_pairs={{0,1},{1,0},{2,3},{3,2},{4,5},{5,4},{6,7},{7,6},{8,9},{9,8},{10,11... | collective-permute-start | bytes 786440 | tf_op jit(solution)/shard_map/ppermute | solution.py:278
  27.1 11.0 %collective-permute-start.11 = (bf16[528,128]{1,0:T(8,128)(2,1)S(1)}, bf16[528,128]{1,0:T(8,128)(2,1)S(1)}, u32[]{:S(2)}, u32[]{:S(2)}) collective-permute-start(bf16[528,128]{1,0:T(8,128)(2,1)S(1)} %get-tuple-element.115), channel_id=1, source_target_pairs={{0,8},{4,12},{8,0},{12,4},{1,9},{5,13},{9,1},{13,5},{2,10},{6,14},... | collective-permute-start | bytes 405512 | tf_op jit(solution)/shard_map/ppermute | solution.py:278
  29.5 10.4 %collective-permute-start.10 = (bf16[528,128]{1,0:T(8,128)(2,1)S(1)}, bf16[528,128]{1,0:T(8,128)(2,1)S(1)}, u32[]{:S(2)}, u32[]{:S(2)}) collective-permute-start(bf16[528,128]{1,0:T(8,128)(2,1)S(1)} %shard_map.124), channel_id=1, source_target_pairs={{0,4},{4,0},{8,12},{12,8},{1,5},{5,1},{9,13},{13,9},{2,6},{6,2},{1... | collective-permute-start | bytes 405512 | tf_op jit(solution)/shard_map/ppermute | solution.py:278
  31.4 12.5 %copy-start = (f32[128]{0:T(128)S(1)}, f32[128]{0:T(128)}, u32[]{:S(2)}) copy-start(f32[128]{0:T(128)} %param.19) | copy-start | bytes 1540
  31.4 10.5 %collective-permute-start.9 = (bf16[528,128]{1,0:T(8,128)(2,1)S(1)}, bf16[528,128]{1,0:T(8,128)(2,1)S(1)}, u32[]{:S(2)}, u32[]{:S(2)}) collective-permute-start(bf16[528,128]{1,0:T(8,128)(2,1)S(1)} %shard_map.123), channel_id=1, source_target_pairs={{0,12},{4,8},{8,4},{12,0},{1,13},{5,9},{9,5},{13,1},{2,14},{6,10},... | collective-permute-start | bytes 405512 | tf_op jit(solution)/shard_map/ppermute | solution.py:278
  45.0 6.3 %collective-permute-start.12 = (bf16[128,256]{1,0:T(8,128)(2,1)S(1)}, bf16[128,256]{1,0:T(8,128)(2,1)S(1)}, u32[]{:S(2)}, u32[]{:S(2)}) collective-permute-start(bf16[128,256]{1,0:T(8,128)(2,1)S(1)} %get-tuple-element.133), channel_id=1, source_target_pairs={{0,12},{4,8},{8,4},{12,0},{1,13},{5,9},{9,5},{13,1},{2,14},{6,10},... | collective-permute-start | bytes 196616 | tf_op jit(solution)/shard_map/ppermute | solution.py:278
  47.4 5.1 %collective-permute-start.13 = (bf16[128,256]{1,0:T(8,128)(2,1)S(1)}, bf16[128,256]{1,0:T(8,128)(2,1)S(1)}, u32[]{:S(2)}, u32[]{:S(2)}) collective-permute-start(bf16[128,256]{1,0:T(8,128)(2,1)S(1)} %get-tuple-element.134), channel_id=1, source_target_pairs={{0,4},{4,0},{8,12},{12,8},{1,5},{5,1},{9,13},{13,9},{2,6},{6,2},{1... | collective-permute-start | bytes 196616 | tf_op jit(solution)/shard_map/ppermute | solution.py:278
  48.0 5.3 %collective-permute-start.14 = (bf16[128,256]{1,0:T(8,128)(2,1)S(1)}, bf16[128,256]{1,0:T(8,128)(2,1)S(1)}, u32[]{:S(2)}, u32[]{:S(2)}) collective-permute-start(bf16[128,256]{1,0:T(8,128)(2,1)S(1)} %get-tuple-element.135), channel_id=1, source_target_pairs={{0,8},{4,12},{8,0},{12,4},{1,9},{5,13},{9,1},{13,5},{2,10},{6,14},... | collective-permute-start | bytes 196616 | tf_op jit(solution)/shard_map/ppermute | solution.py:278

commit v7 on v6

--- a/solution.py
+++ b/solution.py
@@ -485,13 +485,23 @@
 
 def joined(left, right):
     (left_high, left_low), (right_high, right_low) = left, right
+    right_high, right_low = apart(right_high), apart(right_low)
     return dot(
         jnp.concatenate([left_high, left_high, left_low], axis=1),
         jnp.concatenate([right_high, right_low, right_high], axis=0),
     )
 
 
-def unit_lower_inverses(stricts, row, column):
+def apart(pair):
+    first = lax.broadcasted_iota(jnp.int32, pair.shape, 1) < pair.shape[1] // 2
+    zero = jnp.zeros_like(pair)
+    return jnp.concatenate([jnp.where(first, pair, zero), jnp.where(first, zero, pair)], axis=0)
+
+
+def unit_lower_inverses(stricts):
+    half = stricts[0].shape[0]
+    row = lax.broadcasted_iota(jnp.int32, (half, 1), 0)
+    column = lax.broadcasted_iota(jnp.int32, (1, 2 * half), 1) & (half - 1)
     inner = (row >> 3) == (column >> 3)
     identity = jnp.where(row == column, 1.0, 0.0)
     number = range(len(stricts))
@@ -547,7 +557,8 @@
     wide = [key.astype(jnp.float32) for key in keys]
     turned = [jnp.transpose(key) for key in wide]
     growths = {item: jnp.exp(totals[item]) for item in items}
-    inverses = [halves(inverse) for inverse in unit_lower_inverses(stricts, row, column)]
+    pairs = [strict[:half] + strict[half:] for strict in stricts]
+    inverses = [[apart(part) for part in halves(inverse)] for inverse in unit_lower_inverses(pairs)]
     terms = []
     for item, (high, low) in zip(items, inverses):
         total = total_rows[item]

time: 54.2 us -> 53.9 us (level)
  transfers between devices with their start and end apart: 15 -> 15, of which waited for: 10 -> 10; matrix products, arithmetic and copies ran while one was open for 0% -> 0% of each run, Pallas kernels for 28% -> 27%
where the time goes in v7:
time: 53.9 us; the launch traced here: 53.7 us
  Pallas kernels  21.2 us (39%)
  starting transfers between devices  16.8 us (31%)
  waiting for transfers between devices  15 us (28%)
  between operations  0.81 us (2%)
    ppermute x15, starting transfers between devices, swapped(): lax.ppermute(value, axis, [(i, i ^ mask) for i in range(lax.axis_size(axi...  16.8 us
    ppermute x15, waiting for transfers between devices, swapped(): lax.ppermute(value, axis, [(i, i ^ mask) for i in range(lax.axis_size(axi...  15 us
    pallas_call x15, Pallas kernels, vmem_call(): pl.pallas_call(kernel, out_shape=[make(shape, dtype) for shape, dtype in...  13.7 us
    pallas_call x2, Pallas kernels, fetched(): pl.pallas_call(fetch_kernel, out_shape=[pltpu.VMEM(array.shape, array.dty...  5.9 us
  transfers between devices with their start and end apart: 15, of which 10 were waited for; matrix products, arithmetic and copies ran while one was open for 0% of the time, Pallas kernels for 27%

profile of v7, /device:TPU:0, one launch (start us, length us, event | category | flops | bytes accessed | tf_op | source)
XLA Modules:
  0.0 53.7 jit_solution(9339006918119270452)
XLA Ops:
  0.6 0.9 %shard_map.113 = bf16[128,256]{1,0:T(8,128)(2,1)S(1)} custom-call(bf16[128,1024]{1,0:T(8,128)(2,1)} %refs_2_), custom_call_target="tpu_custom_call" | custom-call | tf_op jit(solution)/shard_map/pallas_call | solution.py:665
  1.5 5.1 %collective-permute-start = (bf16[128,256]{1,0:T(8,128)(2,1)S(1)}, bf16[128,256]{1,0:T(8,128)(2,1)S(1)}, u32[]{:S(2)}, u32[]{:S(2)}) collective-permute-start(bf16[128,256]{1,0:T(8,128)(2,1)S(1)} %shard_map.113), channel_id=1, source_target_pairs={{0,12},{4,8},{8,4},{12,0},{1,13},{5,9},{9,5},{13,1},{2,14},{6,10},... | collective-permute-start | bytes 196616 | tf_op jit(solution)/shard_map/ppermute | solution.py:278
  6.6 0.0 collective-permute-start.2
  6.6 0.6 %collective-permute-start.1 = (bf16[128,256]{1,0:T(8,128)(2,1)S(1)}, bf16[128,256]{1,0:T(8,128)(2,1)S(1)}, u32[]{:S(2)}, u32[]{:S(2)}) collective-permute-start(bf16[128,256]{1,0:T(8,128)(2,1)S(1)} %shard_map.113), channel_id=1, source_target_pairs={{0,4},{4,0},{8,12},{12,8},{1,5},{5,1},{9,13},{13,9},{2,6},{6,2},{1... | collective-permute-start | bytes 196616 | tf_op jit(solution)/shard_map/ppermute | solution.py:278
  7.3 2.5 %shard_map.114 = (bf16[128,1024]{1,0:T(8,128)(2,1)S(1)}, bf16[128,1024]{1,0:T(8,128)(2,1)S(1)}, bf16[128,1024]{1,0:T(8,128)(2,1)S(1)}, bf16[1024,2048]{1,0:T(8,128)(2,1)S(1)}, bf16[128,512]{1,0:T(8,128)(2,1)S(1)}) custom-call(bf16[128,1024]{1,0:T(8,128)(2,1)} %refs_0_, bf16[128,1024]{1,0:T(8,128)(2,1)} %refs_1_, bf16[128,1024]{1,0:T(8,128)(2,1)} %refs_2_, ...), custom_call_target="tpu_custom_call" | custom-call | bytes 5111808 | tf_op jit(solution)/shard_map/pallas_call | solution.py:318
  9.7 0.0 collective-permute-done.mine3
  9.8 0.1 collective-permute-start.3
  9.8 1.0 %collective-permute-done.1.mine1 = bf16[128,256]{1,0:T(8,128)(2,1)S(1)} collective-permute-done((bf16[128,256]{1,0:T(8,128)(2,1)S(1)}, bf16[128,256]{1,0:T(8,128)(2,1)S(1)}, u32[]{:S(2)}, u32[]{:S(2)}) %collective-permute-start.1) | collective-permute-done | bytes 65568 | tf_op jit(solution)/shard_map/ppermute | solution.py:278
  10.9 0.0 collective-permute-start.4
  10.9 1.3 %collective-permute-done.2.mine2 = bf16[128,256]{1,0:T(8,128)(2,1)S(1)} collective-permute-done((bf16[128,256]{1,0:T(8,128)(2,1)S(1)}, bf16[128,256]{1,0:T(8,128)(2,1)S(1)}, u32[]{:S(2)}, u32[]{:S(2)}) %collective-permute-start.2) | collective-permute-done | bytes 65568 | tf_op jit(solution)/shard_map/ppermute | solution.py:278
  12.2 0.0 collective-permute-done.3.twin3
  12.2 0.0 collective-permute-start.5
  12.2 0.0 collective-permute-done.4.twin1
  12.2 1.2 %collective-permute-done.5.twin2 = bf16[128,256]{1,0:T(8,128)(2,1)S(1)} collective-permute-done((bf16[128,256]{1,0:T(8,128)(2,1)S(1)}, bf16[128,256]{1,0:T(8,128)(2,1)S(1)}, u32[]{:S(2)}, u32[]{:S(2)}) %collective-permute-start.5) | collective-permute-done | bytes 65568 | tf_op jit(solution)/shard_map/ppermute | solution.py:278
  13.5 1.2 %shard_map.115 = (bf16[128,1024]{1,0:T(8,128)(2,1)S(1)}, bf16[128,1024]{1,0:T(8,128)(2,1)S(1)}) custom-call(bf16[128,1024]{1,0:T(8,128)(2,1)S(1)} %get-tuple-element.79.query_ref, bf16[128,1024]{1,0:T(8,128)(2,1)S(1)} %get-tuple-element.80.gate_ref, bf16[128,1024]{1,0:T(8,128)(2,1)S(1)} %get-tuple-element.81.kv_ref, ...), custom_call_target="tpu_custom_call" | custom-call | tf_op jit(solution)/shard_map/pallas_call | solution.py:265
  14.7 0.2 collective-permute-start.6
  14.9 0.5 shard_map.116.keep_ref
  15.4 0.9 %collective-permute-done.6.came_ref = bf16[128,1024]{1,0:T(8,128)(2,1)S(1)} collective-permute-done((bf16[128,1024]{1,0:T(8,128)(2,1)S(1)}, bf16[128,1024]{1,0:T(8,128)(2,1)S(1)}, u32[]{:S(2)}, u32[]{:S(2)}) %collective-permute-start.6) | collective-permute-done | bytes 262176 | tf_op jit(solution)/shard_map/ppermute | solution.py:278
  16.3 0.1 shard_map.117
  16.4 1.6 %collective-permute-start.7 = (bf16[128,1024]{1,0:T(8,128)(2,1)S(1)}, bf16[128,1024]{1,0:T(8,128)(2,1)S(1)}, u32[]{:S(2)}, u32[]{:S(2)}) collective-permute-start(bf16[128,1024]{1,0:T(8,128)(2,1)S(1)} %get-tuple-element.91), channel_id=1, source_target_pairs={{0,2},{2,0},{1,3},{3,1},{4,6},{6,4},{5,7},{7,5},{8,10},{10,8},{9,1... | collective-permute-start | bytes 786440 | tf_op jit(solution)/shard_map/ppermute | solution.py:278
  18.0 3.4 %shard_map.118 = (bf16[2048,2048]{1,0:T(8,128)(2,1)S(1)}, f32[1,2048]{1,0:T(1,128)S(1)}, bf16[8,2048]{1,0:T(8,128)(2,1)S(1)}, f32[8,128]{1,0:T(8,128)S(1)}) custom-call(bf16[2048,2048]{1,0:T(8,128)(2,1)} %refs_0_.1, f32[1,2048]{1,0:T(1,128)} %bitcast.6, bf16[8,2048]{1,0:T(8,128)(2,1)} %bitcast.5, f32[8,128]{1,0:T(8,128)} %bitcast.7), custom_call_target="tpu_custom_call" | custom-call | bytes 8433664 | tf_op jit(solution)/shard_map/pallas_call | solution.py:318
  21.4 3.5 %collective-permute-done.7.came_ref = bf16[128,1024]{1,0:T(8,128)(2,1)S(1)} collective-permute-done((bf16[128,1024]{1,0:T(8,128)(2,1)S(1)}, bf16[128,1024]{1,0:T(8,128)(2,1)S(1)}, u32[]{:S(2)}, u32[]{:S(2)}) %collective-permute-start.7) | collective-permute-done | bytes 262176 | tf_op jit(solution)/shard_map/ppermute | solution.py:278
  24.9 0.1 collective-permute-start.8
  25.0 0.8 %shard_map.120 = (f32[128,2048]{1,0:T(8,128)S(1)}, f32[8,128]{1,0:T(8,128)S(1)}, f32[128,128]{1,0:T(8,128)S(1)}) custom-call(bf16[128,1024]{1,0:T(8,128)(2,1)S(1)} %shard_map.119.own_ref, f32[1,2048]{1,0:T(1,128)S(1)} %get-tuple-element.101.gain_ref, bf16[2048,2048]{1,0:T(8,128)(2,1)S(1)} %get-tuple-element.102.weight_ref, ...), custom_call_target="tpu_custom_call" | custom-call | tf_op jit(solution)/shard_map/pallas_call | solution.py:265
  25.8 0.7 %collective-permute-done.8.twin_ref = bf16[128,1024]{1,0:T(8,128)(2,1)S(1)} collective-permute-done((bf16[128,1024]{1,0:T(8,128)(2,1)S(1)}, bf16[128,1024]{1,0:T(8,128)(2,1)S(1)}, u32[]{:S(2)}, u32[]{:S(2)}) %collective-permute-start.8) | collective-permute-done | bytes 262176 | tf_op jit(solution)/shard_map/ppermute | solution.py:278
  26.5 0.6 %shard_map.122 = (bf16[128,1024]{1,0:T(8,128)(2,1)S(1)}, f32[128,128]{1,0:T(8,128)S(1)}, f32[16,128]{1,0:T(8,128)S(1)}, bf16[528,128]{1,0:T(8,128)(2,1)S(1)}) custom-call(bf16[128,1024]{1,0:T(8,128)(2,1)S(1)} %collective-permute-done.8.twin_ref, f32[1,2048]{1,0:T(1,128)S(1)} %get-tuple-element.101.gain_ref, bf16[8,2048]{1,0:T(8,128)(2,1)S(1)} %get-tuple-element.103.beta_ref, ...), custom_call_target="tpu_custom_call" | custom-call | tf_op jit(solution)/shard_map/pallas_call | solution.py:265
  27.1 2.0 %collective-permute-start.11 = (bf16[528,128]{1,0:T(8,128)(2,1)S(1)}, bf16[528,128]{1,0:T(8,128)(2,1)S(1)}, u32[]{:S(2)}, u32[]{:S(2)}) collective-permute-start(bf16[528,128]{1,0:T(8,128)(2,1)S(1)} %get-tuple-element.115), channel_id=1, source_target_pairs={{0,8},{4,12},{8,0},{12,4},{1,9},{5,13},{9,1},{13,5},{2,10},{6,14},... | collective-permute-start | bytes 405512 | tf_op jit(solution)/shard_map/ppermute | solution.py:278
  29.1 0.5 shard_map.124
  29.5 1.4 %collective-permute-start.10 = (bf16[528,128]{1,0:T(8,128)(2,1)S(1)}, bf16[528,128]{1,0:T(8,128)(2,1)S(1)}, u32[]{:S(2)}, u32[]{:S(2)}) collective-permute-start(bf16[528,128]{1,0:T(8,128)(2,1)S(1)} %shard_map.124), channel_id=1, source_target_pairs={{0,4},{4,0},{8,12},{12,8},{1,5},{5,1},{9,13},{13,9},{2,6},{6,2},{1... | collective-permute-start | bytes 405512 | tf_op jit(solution)/shard_map/ppermute | solution.py:278
  30.9 0.5 shard_map.123
  31.4 0.0 copy-start
  31.4 1.2 %collective-permute-start.9 = (bf16[528,128]{1,0:T(8,128)(2,1)S(1)}, bf16[528,128]{1,0:T(8,128)(2,1)S(1)}, u32[]{:S(2)}, u32[]{:S(2)}) collective-permute-start(bf16[528,128]{1,0:T(8,128)(2,1)S(1)} %shard_map.123), channel_id=1, source_target_pairs={{0,12},{4,8},{8,4},{12,0},{1,13},{5,9},{9,5},{13,1},{2,14},{6,10},... | collective-permute-start | bytes 405512 | tf_op jit(solution)/shard_map/ppermute | solution.py:278
  32.6 0.5 shard_map.125.refs_0_
  33.0 1.8 %shard_map.126 = (f32[4,2,2,128,128]{4,3,2,1,0:T(8,128)S(1)}, bf16[4,2,2,192,128]{4,3,2,1,0:T(8,128)(2,1)S(1)}, f32[4,2,128,128]{3,2,1,0:T(8,128)S(1)}, f32[4,2,2,8,128]{4,3,2,1,0:T(8,128)S(1)}) custom-call(bf16[528,128]{1,0:T(8,128)(2,1)S(1)} %shard_map.125.refs_0_), custom_call_target="tpu_custom_call" | custom-call | tf_op jit(solution)/shard_map/pallas_call | solution.py:265
  34.9 3.2 %collective-permute-done.11.refs_0_ = bf16[528,128]{1,0:T(8,128)(2,1)S(1)} collective-permute-done((bf16[528,128]{1,0:T(8,128)(2,1)S(1)}, bf16[528,128]{1,0:T(8,128)(2,1)S(1)}, u32[]{:S(2)}, u32[]{:S(2)}) %collective-permute-start.11) | collective-permute-done | bytes 135200 | tf_op jit(solution)/shard_map/ppermute | solution.py:278
  38.0 1.8 %shard_map.127 = (f32[4,2,2,128,128]{4,3,2,1,0:T(8,128)S(1)}, bf16[4,2,2,192,128]{4,3,2,1,0:T(8,128)(2,1)S(1)}, f32[4,2,128,128]{3,2,1,0:T(8,128)S(1)}, f32[4,2,2,8,128]{4,3,2,1,0:T(8,128)S(1)}) custom-call(bf16[528,128]{1,0:T(8,128)(2,1)S(1)} %collective-permute-done.11.refs_0_, ...), custom_call_target="tpu_custom_call", output_to_operand_aliasing={{0}: (1, {}), {1}: (2, {}), {2}: (3, {}), {3}: (4, {})} | custom-call | tf_op jit(solution)/shard_map/pallas_call | solution.py:265
  39.9 0.0 collective-permute-done.10.refs_0_
  39.9 1.8 %shard_map.128 = (f32[4,2,2,128,128]{4,3,2,1,0:T(8,128)S(1)}, bf16[4,2,2,192,128]{4,3,2,1,0:T(8,128)(2,1)S(1)}, f32[4,2,128,128]{3,2,1,0:T(8,128)S(1)}, f32[4,2,2,8,128]{4,3,2,1,0:T(8,128)S(1)}) custom-call(bf16[528,128]{1,0:T(8,128)(2,1)S(1)} %collective-permute-done.10.refs_0_, ...), custom_call_target="tpu_custom_call", output_to_operand_aliasing={{0}: (1, {}), {1}: (2, {}), {2}: (3, {}), {3}: (4, {})} | custom-call | tf_op jit(solution)/shard_map/pallas_call | solution.py:265
  41.7 1.8 %shard_map.129 = (f32[4,2,2,128,128]{4,3,2,1,0:T(8,128)S(1)}, bf16[4,2,2,192,128]{4,3,2,1,0:T(8,128)(2,1)S(1)}, f32[4,2,128,128]{3,2,1,0:T(8,128)S(1)}, f32[4,2,2,8,128]{4,3,2,1,0:T(8,128)S(1)}) custom-call(bf16[528,128]{1,0:T(8,128)(2,1)S(1)} %collective-permute-done.9.refs_0_, ...), custom_call_target="tpu_custom_call", output_to_operand_aliasing={{0}: (1, {}), {1}: (2, {}), {2}: (3, {}), {3}: (4, {})} | custom-call | tf_op jit(solution)/shard_map/pallas_call | solution.py:265
  43.6 1.2 %shard_map.130 = (bf16[128,256]{1,0:T(8,128)(2,1)S(1)}, bf16[128,256]{1,0:T(8,128)(2,1)S(1)}, bf16[128,256]{1,0:T(8,128)(2,1)S(1)}, bf16[128,256]{1,0:T(8,128)(2,1)S(1)}) custom-call(f32[4,2,2,128,128]{4,3,2,1,0:T(8,128)S(1)} %get-tuple-element.128.offset_ref, bf16[4,2,2,192,128]{4,3,2,1,0:T(8,128)(2,1)S(1)} %get-tuple-element.129.linear_ref, ...), custom_call_target="tpu_custom_call" | custom-call | tf_op jit(solution)/shard_map/pallas_call | solution.py:265
  44.7 2.4 %collective-permute-start.12 = (bf16[128,256]{1,0:T(8,128)(2,1)S(1)}, bf16[128,256]{1,0:T(8,128)(2,1)S(1)}, u32[]{:S(2)}, u32[]{:S(2)}) collective-permute-start(bf16[128,256]{1,0:T(8,128)(2,1)S(1)} %get-tuple-element.133), channel_id=1, source_target_pairs={{0,12},{4,8},{8,4},{12,0},{1,13},{5,9},{9,5},{13,1},{2,14},{6,10},... | collective-permute-start | bytes 196616 | tf_op jit(solution)/shard_map/ppermute | solution.py:278
  47.1 0.7 %collective-permute-start.13 = (bf16[128,256]{1,0:T(8,128)(2,1)S(1)}, bf16[128,256]{1,0:T(8,128)(2,1)S(1)}, u32[]{:S(2)}, u32[]{:S(2)}) collective-permute-start(bf16[128,256]{1,0:T(8,128)(2,1)S(1)} %get-tuple-element.134), channel_id=1, source_target_pairs={{0,4},{4,0},{8,12},{12,8},{1,5},{5,1},{9,13},{13,9},{2,6},{6,2},{1... | collective-permute-start | bytes 196616 | tf_op jit(solution)/shard_map/ppermute | solution.py:278
  47.8 1.3 %collective-permute-start.14 = (bf16[128,256]{1,0:T(8,128)(2,1)S(1)}, bf16[128,256]{1,0:T(8,128)(2,1)S(1)}, u32[]{:S(2)}, u32[]{:S(2)}) collective-permute-start(bf16[128,256]{1,0:T(8,128)(2,1)S(1)} %get-tuple-element.135), channel_id=1, source_target_pairs={{0,8},{4,12},{8,0},{12,4},{1,9},{5,13},{9,1},{13,5},{2,10},{6,14},... | collective-permute-start | bytes 196616 | tf_op jit(solution)/shard_map/ppermute | solution.py:278
  49.2 0.7 %shard_map.121 = bf16[128,512]{1,0:T(8,128)(2,1)} custom-call(bf16[128,1024]{1,0:T(8,128)(2,1)S(1)} %shard_map.119.own_ref, bf16[128,1024]{1,0:T(8,128)(2,1)S(1)} %collective-permute-done.8.twin_ref), custom_call_target="tpu_custom_call" | custom-call | tf_op jit(solution)/shard_map/pallas_call | solution.py:265
  49.9 1.1 %collective-permute-done.12.back3 = bf16[128,256]{1,0:T(8,128)(2,1)S(1)} collective-permute-done((bf16[128,256]{1,0:T(8,128)(2,1)S(1)}, bf16[128,256]{1,0:T(8,128)(2,1)S(1)}, u32[]{:S(2)}, u32[]{:S(2)}) %collective-permute-start.12) | collective-permute-done | bytes 65568 | tf_op jit(solution)/shard_map/ppermute | solution.py:278
  51.0 1.2 %collective-permute-done.13.back1 = bf16[128,256]{1,0:T(8,128)(2,1)S(1)} collective-permute-done((bf16[128,256]{1,0:T(8,128)(2,1)S(1)}, bf16[128,256]{1,0:T(8,128)(2,1)S(1)}, u32[]{:S(2)}, u32[]{:S(2)}) %collective-permute-start.13) | collective-permute-done | bytes 65568 | tf_op jit(solution)/shard_map/ppermute | solution.py:278
  52.2 0.8 %collective-permute-done.14.back2 = bf16[128,256]{1,0:T(8,128)(2,1)S(1)} collective-permute-done((bf16[128,256]{1,0:T(8,128)(2,1)S(1)}, bf16[128,256]{1,0:T(8,128)(2,1)S(1)}, u32[]{:S(2)}, u32[]{:S(2)}) %collective-permute-start.14) | collective-permute-done | bytes 65568 | tf_op jit(solution)/shard_map/ppermute | solution.py:278
  53.0 0.7 %shard_map.131 = bf16[128,1024]{1,0:T(8,128)(2,1)} custom-call(bf16[128,256]{1,0:T(8,128)(2,1)S(1)} %get-tuple-element.132.own_ref, bf16[128,256]{1,0:T(8,128)(2,1)S(1)} %collective-permute-done.12.back3, bf16[128,256]{1,0:T(8,128)(2,1)S(1)} %collective-permute-done.13.back1, bf16[128,256]{1,0:T(8,128)(2,1)S(1)} %collective-permute-done.14.back2), custom_call_target="tpu_custom_call" | custom-call | tf_op jit(solution)/shard_map/pallas_call | solution.py:748
  (3 shorter events, 0.1 us)
Async XLA Ops:
  1.5 8.3 %collective-permute-start = (bf16[128,256]{1,0:T(8,128)(2,1)S(1)}, bf16[128,256]{1,0:T(8,128)(2,1)S(1)}, u32[]{:S(2)}, u32[]{:S(2)}) collective-permute-start(bf16[128,256]{1,0:T(8,128)(2,1)S(1)} %shard_map.113), channel_id=1, source_target_pairs={{0,12},{4,8},{8,4},{12,0},{1,13},{5,9},{9,5},{13,1},{2,14},{6,10},... | collective-permute-start | bytes 196616 | tf_op jit(solution)/shard_map/ppermute | solution.py:278
  6.6 5.6 %collective-permute-start.2 = (bf16[128,256]{1,0:T(8,128)(2,1)S(1)}, bf16[128,256]{1,0:T(8,128)(2,1)S(1)}, u32[]{:S(2)}, u32[]{:S(2)}) collective-permute-start(bf16[128,256]{1,0:T(8,128)(2,1)S(1)} %shard_map.113), channel_id=1, source_target_pairs={{0,8},{4,12},{8,0},{12,4},{1,9},{5,13},{9,1},{13,5},{2,10},{6,14},... | collective-permute-start | bytes 196616 | tf_op jit(solution)/shard_map/ppermute | solution.py:278
  6.6 4.3 %collective-permute-start.1 = (bf16[128,256]{1,0:T(8,128)(2,1)S(1)}, bf16[128,256]{1,0:T(8,128)(2,1)S(1)}, u32[]{:S(2)}, u32[]{:S(2)}) collective-permute-start(bf16[128,256]{1,0:T(8,128)(2,1)S(1)} %shard_map.113), channel_id=1, source_target_pairs={{0,4},{4,0},{8,12},{12,8},{1,5},{5,1},{9,13},{13,9},{2,6},{6,2},{1... | collective-permute-start | bytes 196616 | tf_op jit(solution)/shard_map/ppermute | solution.py:278
  9.8 2.5 %collective-permute-start.3 = (bf16[128,256]{1,0:T(8,128)(2,1)S(1)}, bf16[128,256]{1,0:T(8,128)(2,1)S(1)}, u32[]{:S(2)}, u32[]{:S(2)}) collective-permute-start(bf16[128,256]{1,0:T(8,128)(2,1)S(1)} %collective-permute-done.mine3), channel_id=1, source_target_pairs={{0,1},{1,0},{2,3},{3,2},{4,5},{5,4},{6,7},{7,6},{8,9},{9,8},{10,11... | collective-permute-start | bytes 196616 | tf_op jit(solution)/shard_map/ppermute | solution.py:278
  10.9 1.3 %collective-permute-start.4 = (bf16[128,256]{1,0:T(8,128)(2,1)S(1)}, bf16[128,256]{1,0:T(8,128)(2,1)S(1)}, u32[]{:S(2)}, u32[]{:S(2)}) collective-permute-start(bf16[128,256]{1,0:T(8,128)(2,1)S(1)} %collective-permute-done.1.mine1), channel_id=1, source_target_pairs={{0,1},{1,0},{2,3},{3,2},{4,5},{5,4},{6,7},{7,6},{8,9},{9,8},{10,11... | collective-permute-start | bytes 196616 | tf_op jit(solution)/shard_map/ppermute | solution.py:278
  12.2 1.3 %collective-permute-start.5 = (bf16[128,256]{1,0:T(8,128)(2,1)S(1)}, bf16[128,256]{1,0:T(8,128)(2,1)S(1)}, u32[]{:S(2)}, u32[]{:S(2)}) collective-permute-start(bf16[128,256]{1,0:T(8,128)(2,1)S(1)} %collective-permute-done.2.mine2), channel_id=1, source_target_pairs={{0,1},{1,0},{2,3},{3,2},{4,5},{5,4},{6,7},{7,6},{8,9},{9,8},{10,11... | collective-permute-start | bytes 196616 | tf_op jit(solution)/shard_map/ppermute | solution.py:278
  14.7 1.6 %collective-permute-start.6 = (bf16[128,1024]{1,0:T(8,128)(2,1)S(1)}, bf16[128,1024]{1,0:T(8,128)(2,1)S(1)}, u32[]{:S(2)}, u32[]{:S(2)}) collective-permute-start(bf16[128,1024]{1,0:T(8,128)(2,1)S(1)} %get-tuple-element.86), channel_id=1, source_target_pairs={{0,1},{1,0},{2,3},{3,2},{4,5},{5,4},{6,7},{7,6},{8,9},{9,8},{10,11... | collective-permute-start | bytes 786440 | tf_op jit(solution)/shard_map/ppermute | solution.py:278
  16.4 8.5 %collective-permute-start.7 = (bf16[128,1024]{1,0:T(8,128)(2,1)S(1)}, bf16[128,1024]{1,0:T(8,128)(2,1)S(1)}, u32[]{:S(2)}, u32[]{:S(2)}) collective-permute-start(bf16[128,1024]{1,0:T(8,128)(2,1)S(1)} %get-tuple-element.91), channel_id=1, source_target_pairs={{0,2},{2,0},{1,3},{3,1},{4,6},{6,4},{5,7},{7,5},{8,10},{10,8},{9,1... | collective-permute-start | bytes 786440 | tf_op jit(solution)/shard_map/ppermute | solution.py:278
  24.9 1.6 %collective-permute-start.8 = (bf16[128,1024]{1,0:T(8,128)(2,1)S(1)}, bf16[128,1024]{1,0:T(8,128)(2,1)S(1)}, u32[]{:S(2)}, u32[]{:S(2)}) collective-permute-start(bf16[128,1024]{1,0:T(8,128)(2,1)S(1)} %shard_map.119.own_ref), channel_id=1, source_target_pairs={{0,1},{1,0},{2,3},{3,2},{4,5},{5,4},{6,7},{7,6},{8,9},{9,8},{10,11... | collective-permute-start | bytes 786440 | tf_op jit(solution)/shard_map/ppermute | solution.py:278
  27.1 11.0 %collective-permute-start.11 = (bf16[528,128]{1,0:T(8,128)(2,1)S(1)}, bf16[528,128]{1,0:T(8,128)(2,1)S(1)}, u32[]{:S(2)}, u32[]{:S(2)}) collective-permute-start(bf16[528,128]{1,0:T(8,128)(2,1)S(1)} %get-tuple-element.115), channel_id=1, source_target_pairs={{0,8},{4,12},{8,0},{12,4},{1,9},{5,13},{9,1},{13,5},{2,10},{6,14},... | collective-permute-start | bytes 405512 | tf_op jit(solution)/shard_map/ppermute | solution.py:278
  29.5 10.3 %collective-permute-start.10 = (bf16[528,128]{1,0:T(8,128)(2,1)S(1)}, bf16[528,128]{1,0:T(8,128)(2,1)S(1)}, u32[]{:S(2)}, u32[]{:S(2)}) collective-permute-start(bf16[528,128]{1,0:T(8,128)(2,1)S(1)} %shard_map.124), channel_id=1, source_target_pairs={{0,4},{4,0},{8,12},{12,8},{1,5},{5,1},{9,13},{13,9},{2,6},{6,2},{1... | collective-permute-start | bytes 405512 | tf_op jit(solution)/shard_map/ppermute | solution.py:278
  31.4 12.2 %copy-start = (f32[128]{0:T(128)S(1)}, f32[128]{0:T(128)}, u32[]{:S(2)}) copy-start(f32[128]{0:T(128)} %param.19) | copy-start | bytes 1540
  31.4 10.3 %collective-permute-start.9 = (bf16[528,128]{1,0:T(8,128)(2,1)S(1)}, bf16[528,128]{1,0:T(8,128)(2,1)S(1)}, u32[]{:S(2)}, u32[]{:S(2)}) collective-permute-start(bf16[528,128]{1,0:T(8,128)(2,1)S(1)} %shard_map.123), channel_id=1, source_target_pairs={{0,12},{4,8},{8,4},{12,0},{1,13},{5,9},{9,5},{13,1},{2,14},{6,10},... | collective-permute-start | bytes 405512 | tf_op jit(solution)/shard_map/ppermute | solution.py:278
  44.7 6.3 %collective-permute-start.12 = (bf16[128,256]{1,0:T(8,128)(2,1)S(1)}, bf16[128,256]{1,0:T(8,128)(2,1)S(1)}, u32[]{:S(2)}, u32[]{:S(2)}) collective-permute-start(bf16[128,256]{1,0:T(8,128)(2,1)S(1)} %get-tuple-element.133), channel_id=1, source_target_pairs={{0,12},{4,8},{8,4},{12,0},{1,13},{5,9},{9,5},{13,1},{2,14},{6,10},... | collective-permute-start | bytes 196616 | tf_op jit(solution)/shard_map/ppermute | solution.py:278
  47.1 5.1 %collective-permute-start.13 = (bf16[128,256]{1,0:T(8,128)(2,1)S(1)}, bf16[128,256]{1,0:T(8,128)(2,1)S(1)}, u32[]{:S(2)}, u32[]{:S(2)}) collective-permute-start(bf16[128,256]{1,0:T(8,128)(2,1)S(1)} %get-tuple-element.134), channel_id=1, source_target_pairs={{0,4},{4,0},{8,12},{12,8},{1,5},{5,1},{9,13},{13,9},{2,6},{6,2},{1... | collective-permute-start | bytes 196616 | tf_op jit(solution)/shard_map/ppermute | solution.py:278
  47.8 5.2 %collective-permute-start.14 = (bf16[128,256]{1,0:T(8,128)(2,1)S(1)}, bf16[128,256]{1,0:T(8,128)(2,1)S(1)}, u32[]{:S(2)}, u32[]{:S(2)}) collective-permute-start(bf16[128,256]{1,0:T(8,128)(2,1)S(1)} %get-tuple-element.135), channel_id=1, source_target_pairs={{0,8},{4,12},{8,0},{12,4},{1,9},{5,13},{9,1},{13,5},{2,10},{6,14},... | collective-permute-start | bytes 196616 | tf_op jit(solution)/shard_map/ppermute | solution.py:278

commit v8 on v7

--- a/solution.py
+++ b/solution.py
@@ -578,7 +578,8 @@
     solved = []
     for value, (beta, _, _, weighted, _, high, low, _) in zip(values, terms):
         right = jnp.concatenate([(beta * value.astype(jnp.float32)).astype(jnp.bfloat16), weighted], axis=1)
-        solved.append((dot(high, right) + dot(low, right)).astype(jnp.bfloat16))
+        both = dot(jnp.concatenate([high, low], axis=1), jnp.concatenate([right, right], axis=0))
+        solved.append(both.astype(jnp.bfloat16))
     moved = []
     for part, (_, decay, _, _, lefts, _, _, _) in zip(solved, terms):
         moved.append(dot(jnp.concatenate([lefts, (query_gram * decay).astype(jnp.bfloat16)], axis=0), part))

time: 53.9 us -> 53.9 us (level)
  no operation moved by 1% of the time
where the time goes in v8:
time: 53.9 us; the launch traced here: 53.7 us
  Pallas kernels  21 us (39%)
  starting transfers between devices  16.8 us (31%)
  waiting for transfers between devices  15.1 us (28%)
  between operations  0.81 us (2%)
    ppermute x15, starting transfers between devices, swapped(): lax.ppermute(value, axis, [(i, i ^ mask) for i in range(lax.axis_size(axi...  16.8 us
    ppermute x15, waiting for transfers between devices, swapped(): lax.ppermute(value, axis, [(i, i ^ mask) for i in range(lax.axis_size(axi...  15.1 us
    pallas_call x15, Pallas kernels, vmem_call(): pl.pallas_call(kernel, out_shape=[make(shape, dtype) for shape, dtype in...  13.5 us
    pallas_call x2, Pallas kernels, fetched(): pl.pallas_call(fetch_kernel, out_shape=[pltpu.VMEM(array.shape, array.dty...  5.9 us
  transfers between devices with their start and end apart: 15, of which 10 were waited for; matrix products, arithmetic and copies ran while one was open for 0% of the time, Pallas kernels for 27%

profile of v8, /device:TPU:0, one launch (start us, length us, event | category | flops | bytes accessed | tf_op | source)
XLA Modules:
  0.0 53.7 jit_solution(8737486104047177345)
XLA Ops:
  0.6 0.9 %shard_map.113 = bf16[128,256]{1,0:T(8,128)(2,1)S(1)} custom-call(bf16[128,1024]{1,0:T(8,128)(2,1)} %refs_2_), custom_call_target="tpu_custom_call" | custom-call | tf_op jit(solution)/shard_map/pallas_call | solution.py:666
  1.5 5.1 %collective-permute-start = (bf16[128,256]{1,0:T(8,128)(2,1)S(1)}, bf16[128,256]{1,0:T(8,128)(2,1)S(1)}, u32[]{:S(2)}, u32[]{:S(2)}) collective-permute-start(bf16[128,256]{1,0:T(8,128)(2,1)S(1)} %shard_map.113), channel_id=1, source_target_pairs={{0,12},{4,8},{8,4},{12,0},{1,13},{5,9},{9,5},{13,1},{2,14},{6,10},... | collective-permute-start | bytes 196616 | tf_op jit(solution)/shard_map/ppermute | solution.py:278
  6.6 0.0 collective-permute-start.2
  6.6 0.6 %collective-permute-start.1 = (bf16[128,256]{1,0:T(8,128)(2,1)S(1)}, bf16[128,256]{1,0:T(8,128)(2,1)S(1)}, u32[]{:S(2)}, u32[]{:S(2)}) collective-permute-start(bf16[128,256]{1,0:T(8,128)(2,1)S(1)} %shard_map.113), channel_id=1, source_target_pairs={{0,4},{4,0},{8,12},{12,8},{1,5},{5,1},{9,13},{13,9},{2,6},{6,2},{1... | collective-permute-start | bytes 196616 | tf_op jit(solution)/shard_map/ppermute | solution.py:278
  7.3 2.5 %shard_map.114 = (bf16[128,1024]{1,0:T(8,128)(2,1)S(1)}, bf16[128,1024]{1,0:T(8,128)(2,1)S(1)}, bf16[128,1024]{1,0:T(8,128)(2,1)S(1)}, bf16[1024,2048]{1,0:T(8,128)(2,1)S(1)}, bf16[128,512]{1,0:T(8,128)(2,1)S(1)}) custom-call(bf16[128,1024]{1,0:T(8,128)(2,1)} %refs_0_, bf16[128,1024]{1,0:T(8,128)(2,1)} %refs_1_, bf16[128,1024]{1,0:T(8,128)(2,1)} %refs_2_, ...), custom_call_target="tpu_custom_call" | custom-call | bytes 5111808 | tf_op jit(solution)/shard_map/pallas_call | solution.py:318
  9.7 0.0 collective-permute-done.mine3
  9.8 0.1 collective-permute-start.3
  9.8 1.0 %collective-permute-done.1.mine1 = bf16[128,256]{1,0:T(8,128)(2,1)S(1)} collective-permute-done((bf16[128,256]{1,0:T(8,128)(2,1)S(1)}, bf16[128,256]{1,0:T(8,128)(2,1)S(1)}, u32[]{:S(2)}, u32[]{:S(2)}) %collective-permute-start.1) | collective-permute-done | bytes 65568 | tf_op jit(solution)/shard_map/ppermute | solution.py:278
  10.9 0.0 collective-permute-start.4
  10.9 1.3 %collective-permute-done.2.mine2 = bf16[128,256]{1,0:T(8,128)(2,1)S(1)} collective-permute-done((bf16[128,256]{1,0:T(8,128)(2,1)S(1)}, bf16[128,256]{1,0:T(8,128)(2,1)S(1)}, u32[]{:S(2)}, u32[]{:S(2)}) %collective-permute-start.2) | collective-permute-done | bytes 65568 | tf_op jit(solution)/shard_map/ppermute | solution.py:278
  12.2 0.0 collective-permute-done.3.twin3
  12.2 0.0 collective-permute-start.5
  12.2 0.0 collective-permute-done.4.twin1
  12.2 1.2 %collective-permute-done.5.twin2 = bf16[128,256]{1,0:T(8,128)(2,1)S(1)} collective-permute-done((bf16[128,256]{1,0:T(8,128)(2,1)S(1)}, bf16[128,256]{1,0:T(8,128)(2,1)S(1)}, u32[]{:S(2)}, u32[]{:S(2)}) %collective-permute-start.5) | collective-permute-done | bytes 65568 | tf_op jit(solution)/shard_map/ppermute | solution.py:278
  13.5 1.2 %shard_map.115 = (bf16[128,1024]{1,0:T(8,128)(2,1)S(1)}, bf16[128,1024]{1,0:T(8,128)(2,1)S(1)}) custom-call(bf16[128,1024]{1,0:T(8,128)(2,1)S(1)} %get-tuple-element.79.query_ref, bf16[128,1024]{1,0:T(8,128)(2,1)S(1)} %get-tuple-element.80.gate_ref, bf16[128,1024]{1,0:T(8,128)(2,1)S(1)} %get-tuple-element.81.kv_ref, ...), custom_call_target="tpu_custom_call" | custom-call | tf_op jit(solution)/shard_map/pallas_call | solution.py:265
  14.7 0.2 collective-permute-start.6
  14.9 0.5 shard_map.116.keep_ref
  15.4 0.9 %collective-permute-done.6.came_ref = bf16[128,1024]{1,0:T(8,128)(2,1)S(1)} collective-permute-done((bf16[128,1024]{1,0:T(8,128)(2,1)S(1)}, bf16[128,1024]{1,0:T(8,128)(2,1)S(1)}, u32[]{:S(2)}, u32[]{:S(2)}) %collective-permute-start.6) | collective-permute-done | bytes 262176 | tf_op jit(solution)/shard_map/ppermute | solution.py:278
  16.3 0.1 shard_map.117
  16.4 1.6 %collective-permute-start.7 = (bf16[128,1024]{1,0:T(8,128)(2,1)S(1)}, bf16[128,1024]{1,0:T(8,128)(2,1)S(1)}, u32[]{:S(2)}, u32[]{:S(2)}) collective-permute-start(bf16[128,1024]{1,0:T(8,128)(2,1)S(1)} %get-tuple-element.91), channel_id=1, source_target_pairs={{0,2},{2,0},{1,3},{3,1},{4,6},{6,4},{5,7},{7,5},{8,10},{10,8},{9,1... | collective-permute-start | bytes 786440 | tf_op jit(solution)/shard_map/ppermute | solution.py:278
  18.0 3.4 %shard_map.118 = (bf16[2048,2048]{1,0:T(8,128)(2,1)S(1)}, f32[1,2048]{1,0:T(1,128)S(1)}, bf16[8,2048]{1,0:T(8,128)(2,1)S(1)}, f32[8,128]{1,0:T(8,128)S(1)}) custom-call(bf16[2048,2048]{1,0:T(8,128)(2,1)} %refs_0_.1, f32[1,2048]{1,0:T(1,128)} %bitcast.6, bf16[8,2048]{1,0:T(8,128)(2,1)} %bitcast.5, f32[8,128]{1,0:T(8,128)} %bitcast.7), custom_call_target="tpu_custom_call" | custom-call | bytes 8433664 | tf_op jit(solution)/shard_map/pallas_call | solution.py:318
  21.4 3.5 %collective-permute-done.7.came_ref = bf16[128,1024]{1,0:T(8,128)(2,1)S(1)} collective-permute-done((bf16[128,1024]{1,0:T(8,128)(2,1)S(1)}, bf16[128,1024]{1,0:T(8,128)(2,1)S(1)}, u32[]{:S(2)}, u32[]{:S(2)}) %collective-permute-start.7) | collective-permute-done | bytes 262176 | tf_op jit(solution)/shard_map/ppermute | solution.py:278
  24.9 0.1 collective-permute-start.8
  25.0 0.8 %shard_map.120 = (f32[128,2048]{1,0:T(8,128)S(1)}, f32[8,128]{1,0:T(8,128)S(1)}, f32[128,128]{1,0:T(8,128)S(1)}) custom-call(bf16[128,1024]{1,0:T(8,128)(2,1)S(1)} %shard_map.119.own_ref, f32[1,2048]{1,0:T(1,128)S(1)} %get-tuple-element.101.gain_ref, bf16[2048,2048]{1,0:T(8,128)(2,1)S(1)} %get-tuple-element.102.weight_ref, ...), custom_call_target="tpu_custom_call" | custom-call | tf_op jit(solution)/shard_map/pallas_call | solution.py:265
  25.8 0.7 %collective-permute-done.8.twin_ref = bf16[128,1024]{1,0:T(8,128)(2,1)S(1)} collective-permute-done((bf16[128,1024]{1,0:T(8,128)(2,1)S(1)}, bf16[128,1024]{1,0:T(8,128)(2,1)S(1)}, u32[]{:S(2)}, u32[]{:S(2)}) %collective-permute-start.8) | collective-permute-done | bytes 262176 | tf_op jit(solution)/shard_map/ppermute | solution.py:278
  26.5 0.6 %shard_map.122 = (bf16[128,1024]{1,0:T(8,128)(2,1)S(1)}, f32[128,128]{1,0:T(8,128)S(1)}, f32[16,128]{1,0:T(8,128)S(1)}, bf16[528,128]{1,0:T(8,128)(2,1)S(1)}) custom-call(bf16[128,1024]{1,0:T(8,128)(2,1)S(1)} %collective-permute-done.8.twin_ref, f32[1,2048]{1,0:T(1,128)S(1)} %get-tuple-element.101.gain_ref, bf16[8,2048]{1,0:T(8,128)(2,1)S(1)} %get-tuple-element.103.beta_ref, ...), custom_call_target="tpu_custom_call" | custom-call | tf_op jit(solution)/shard_map/pallas_call | solution.py:265
  27.1 2.0 %collective-permute-start.11 = (bf16[528,128]{1,0:T(8,128)(2,1)S(1)}, bf16[528,128]{1,0:T(8,128)(2,1)S(1)}, u32[]{:S(2)}, u32[]{:S(2)}) collective-permute-start(bf16[528,128]{1,0:T(8,128)(2,1)S(1)} %get-tuple-element.115), channel_id=1, source_target_pairs={{0,8},{4,12},{8,0},{12,4},{1,9},{5,13},{9,1},{13,5},{2,10},{6,14},... | collective-permute-start | bytes 405512 | tf_op jit(solution)/shard_map/ppermute | solution.py:278
  29.1 0.5 shard_map.124
  29.5 1.4 %collective-permute-start.10 = (bf16[528,128]{1,0:T(8,128)(2,1)S(1)}, bf16[528,128]{1,0:T(8,128)(2,1)S(1)}, u32[]{:S(2)}, u32[]{:S(2)}) collective-permute-start(bf16[528,128]{1,0:T(8,128)(2,1)S(1)} %shard_map.124), channel_id=1, source_target_pairs={{0,4},{4,0},{8,12},{12,8},{1,5},{5,1},{9,13},{13,9},{2,6},{6,2},{1... | collective-permute-start | bytes 405512 | tf_op jit(solution)/shard_map/ppermute | solution.py:278
  30.9 0.5 shard_map.123
  31.4 0.0 copy-start
  31.4 1.2 %collective-permute-start.9 = (bf16[528,128]{1,0:T(8,128)(2,1)S(1)}, bf16[528,128]{1,0:T(8,128)(2,1)S(1)}, u32[]{:S(2)}, u32[]{:S(2)}) collective-permute-start(bf16[528,128]{1,0:T(8,128)(2,1)S(1)} %shard_map.123), channel_id=1, source_target_pairs={{0,12},{4,8},{8,4},{12,0},{1,13},{5,9},{9,5},{13,1},{2,14},{6,10},... | collective-permute-start | bytes 405512 | tf_op jit(solution)/shard_map/ppermute | solution.py:278
  32.6 0.5 shard_map.125.refs_0_
  33.0 1.8 %shard_map.126 = (f32[4,2,2,128,128]{4,3,2,1,0:T(8,128)S(1)}, bf16[4,2,2,192,128]{4,3,2,1,0:T(8,128)(2,1)S(1)}, f32[4,2,128,128]{3,2,1,0:T(8,128)S(1)}, f32[4,2,2,8,128]{4,3,2,1,0:T(8,128)S(1)}) custom-call(bf16[528,128]{1,0:T(8,128)(2,1)S(1)} %shard_map.125.refs_0_), custom_call_target="tpu_custom_call" | custom-call | tf_op jit(solution)/shard_map/pallas_call | solution.py:265
  34.8 3.2 %collective-permute-done.11.refs_0_ = bf16[528,128]{1,0:T(8,128)(2,1)S(1)} collective-permute-done((bf16[528,128]{1,0:T(8,128)(2,1)S(1)}, bf16[528,128]{1,0:T(8,128)(2,1)S(1)}, u32[]{:S(2)}, u32[]{:S(2)}) %collective-permute-start.11) | collective-permute-done | bytes 135200 | tf_op jit(solution)/shard_map/ppermute | solution.py:278
  38.0 1.8 %shard_map.127 = (f32[4,2,2,128,128]{4,3,2,1,0:T(8,128)S(1)}, bf16[4,2,2,192,128]{4,3,2,1,0:T(8,128)(2,1)S(1)}, f32[4,2,128,128]{3,2,1,0:T(8,128)S(1)}, f32[4,2,2,8,128]{4,3,2,1,0:T(8,128)S(1)}) custom-call(bf16[528,128]{1,0:T(8,128)(2,1)S(1)} %collective-permute-done.11.refs_0_, ...), custom_call_target="tpu_custom_call", output_to_operand_aliasing={{0}: (1, {}), {1}: (2, {}), {2}: (3, {}), {3}: (4, {})} | custom-call | tf_op jit(solution)/shard_map/pallas_call | solution.py:265
  39.8 1.8 %shard_map.128 = (f32[4,2,2,128,128]{4,3,2,1,0:T(8,128)S(1)}, bf16[4,2,2,192,128]{4,3,2,1,0:T(8,128)(2,1)S(1)}, f32[4,2,128,128]{3,2,1,0:T(8,128)S(1)}, f32[4,2,2,8,128]{4,3,2,1,0:T(8,128)S(1)}) custom-call(bf16[528,128]{1,0:T(8,128)(2,1)S(1)} %collective-permute-done.10.refs_0_, ...), custom_call_target="tpu_custom_call", output_to_operand_aliasing={{0}: (1, {}), {1}: (2, {}), {2}: (3, {}), {3}: (4, {})} | custom-call | tf_op jit(solution)/shard_map/pallas_call | solution.py:265
  41.6 0.0 collective-permute-done.9.refs_0_
  41.6 1.8 %shard_map.129 = (f32[4,2,2,128,128]{4,3,2,1,0:T(8,128)S(1)}, bf16[4,2,2,192,128]{4,3,2,1,0:T(8,128)(2,1)S(1)}, f32[4,2,128,128]{3,2,1,0:T(8,128)S(1)}, f32[4,2,2,8,128]{4,3,2,1,0:T(8,128)S(1)}) custom-call(bf16[528,128]{1,0:T(8,128)(2,1)S(1)} %collective-permute-done.9.refs_0_, ...), custom_call_target="tpu_custom_call", output_to_operand_aliasing={{0}: (1, {}), {1}: (2, {}), {2}: (3, {}), {3}: (4, {})} | custom-call | tf_op jit(solution)/shard_map/pallas_call | solution.py:265
  43.4 1.2 %shard_map.130 = (bf16[128,256]{1,0:T(8,128)(2,1)S(1)}, bf16[128,256]{1,0:T(8,128)(2,1)S(1)}, bf16[128,256]{1,0:T(8,128)(2,1)S(1)}, bf16[128,256]{1,0:T(8,128)(2,1)S(1)}) custom-call(f32[4,2,2,128,128]{4,3,2,1,0:T(8,128)S(1)} %get-tuple-element.128.offset_ref, bf16[4,2,2,192,128]{4,3,2,1,0:T(8,128)(2,1)S(1)} %get-tuple-element.129.linear_ref, ...), custom_call_target="tpu_custom_call" | custom-call | tf_op jit(solution)/shard_map/pallas_call | solution.py:265
  44.6 2.4 %collective-permute-start.12 = (bf16[128,256]{1,0:T(8,128)(2,1)S(1)}, bf16[128,256]{1,0:T(8,128)(2,1)S(1)}, u32[]{:S(2)}, u32[]{:S(2)}) collective-permute-start(bf16[128,256]{1,0:T(8,128)(2,1)S(1)} %get-tuple-element.133), channel_id=1, source_target_pairs={{0,12},{4,8},{8,4},{12,0},{1,13},{5,9},{9,5},{13,1},{2,14},{6,10},... | collective-permute-start | bytes 196616 | tf_op jit(solution)/shard_map/ppermute | solution.py:278
  47.0 0.8 %collective-permute-start.13 = (bf16[128,256]{1,0:T(8,128)(2,1)S(1)}, bf16[128,256]{1,0:T(8,128)(2,1)S(1)}, u32[]{:S(2)}, u32[]{:S(2)}) collective-permute-start(bf16[128,256]{1,0:T(8,128)(2,1)S(1)} %get-tuple-element.134), channel_id=1, source_target_pairs={{0,4},{4,0},{8,12},{12,8},{1,5},{5,1},{9,13},{13,9},{2,6},{6,2},{1... | collective-permute-start | bytes 196616 | tf_op jit(solution)/shard_map/ppermute | solution.py:278
  47.8 1.3 %collective-permute-start.14 = (bf16[128,256]{1,0:T(8,128)(2,1)S(1)}, bf16[128,256]{1,0:T(8,128)(2,1)S(1)}, u32[]{:S(2)}, u32[]{:S(2)}) collective-permute-start(bf16[128,256]{1,0:T(8,128)(2,1)S(1)} %get-tuple-element.135), channel_id=1, source_target_pairs={{0,8},{4,12},{8,0},{12,4},{1,9},{5,13},{9,1},{13,5},{2,10},{6,14},... | collective-permute-start | bytes 196616 | tf_op jit(solution)/shard_map/ppermute | solution.py:278
  49.1 0.7 %shard_map.121 = bf16[128,512]{1,0:T(8,128)(2,1)} custom-call(bf16[128,1024]{1,0:T(8,128)(2,1)S(1)} %shard_map.119.own_ref, bf16[128,1024]{1,0:T(8,128)(2,1)S(1)} %collective-permute-done.8.twin_ref), custom_call_target="tpu_custom_call" | custom-call | tf_op jit(solution)/shard_map/pallas_call | solution.py:265
  49.7 1.1 %collective-permute-done.12.back3 = bf16[128,256]{1,0:T(8,128)(2,1)S(1)} collective-permute-done((bf16[128,256]{1,0:T(8,128)(2,1)S(1)}, bf16[128,256]{1,0:T(8,128)(2,1)S(1)}, u32[]{:S(2)}, u32[]{:S(2)}) %collective-permute-start.12) | collective-permute-done | bytes 65568 | tf_op jit(solution)/shard_map/ppermute | solution.py:278
  50.9 1.2 %collective-permute-done.13.back1 = bf16[128,256]{1,0:T(8,128)(2,1)S(1)} collective-permute-done((bf16[128,256]{1,0:T(8,128)(2,1)S(1)}, bf16[128,256]{1,0:T(8,128)(2,1)S(1)}, u32[]{:S(2)}, u32[]{:S(2)}) %collective-permute-start.13) | collective-permute-done | bytes 65568 | tf_op jit(solution)/shard_map/ppermute | solution.py:278
  52.0 0.9 %collective-permute-done.14.back2 = bf16[128,256]{1,0:T(8,128)(2,1)S(1)} collective-permute-done((bf16[128,256]{1,0:T(8,128)(2,1)S(1)}, bf16[128,256]{1,0:T(8,128)(2,1)S(1)}, u32[]{:S(2)}, u32[]{:S(2)}) %collective-permute-start.14) | collective-permute-done | bytes 65568 | tf_op jit(solution)/shard_map/ppermute | solution.py:278
  53.0 0.7 %shard_map.131 = bf16[128,1024]{1,0:T(8,128)(2,1)} custom-call(bf16[128,256]{1,0:T(8,128)(2,1)S(1)} %get-tuple-element.132.own_ref, bf16[128,256]{1,0:T(8,128)(2,1)S(1)} %collective-permute-done.12.back3, bf16[128,256]{1,0:T(8,128)(2,1)S(1)} %collective-permute-done.13.back1, bf16[128,256]{1,0:T(8,128)(2,1)S(1)} %collective-permute-done.14.back2), custom_call_target="tpu_custom_call" | custom-call | tf_op jit(solution)/shard_map/pallas_call | solution.py:749
  (3 shorter events, 0.1 us)
Async XLA Ops:
  1.5 8.3 %collective-permute-start = (bf16[128,256]{1,0:T(8,128)(2,1)S(1)}, bf16[128,256]{1,0:T(8,128)(2,1)S(1)}, u32[]{:S(2)}, u32[]{:S(2)}) collective-permute-start(bf16[128,256]{1,0:T(8,128)(2,1)S(1)} %shard_map.113), channel_id=1, source_target_pairs={{0,12},{4,8},{8,4},{12,0},{1,13},{5,9},{9,5},{13,1},{2,14},{6,10},... | collective-permute-start | bytes 196616 | tf_op jit(solution)/shard_map/ppermute | solution.py:278
  6.6 5.6 %collective-permute-start.2 = (bf16[128,256]{1,0:T(8,128)(2,1)S(1)}, bf16[128,256]{1,0:T(8,128)(2,1)S(1)}, u32[]{:S(2)}, u32[]{:S(2)}) collective-permute-start(bf16[128,256]{1,0:T(8,128)(2,1)S(1)} %shard_map.113), channel_id=1, source_target_pairs={{0,8},{4,12},{8,0},{12,4},{1,9},{5,13},{9,1},{13,5},{2,10},{6,14},... | collective-permute-start | bytes 196616 | tf_op jit(solution)/shard_map/ppermute | solution.py:278
  6.6 4.3 %collective-permute-start.1 = (bf16[128,256]{1,0:T(8,128)(2,1)S(1)}, bf16[128,256]{1,0:T(8,128)(2,1)S(1)}, u32[]{:S(2)}, u32[]{:S(2)}) collective-permute-start(bf16[128,256]{1,0:T(8,128)(2,1)S(1)} %shard_map.113), channel_id=1, source_target_pairs={{0,4},{4,0},{8,12},{12,8},{1,5},{5,1},{9,13},{13,9},{2,6},{6,2},{1... | collective-permute-start | bytes 196616 | tf_op jit(solution)/shard_map/ppermute | solution.py:278
  9.8 2.5 %collective-permute-start.3 = (bf16[128,256]{1,0:T(8,128)(2,1)S(1)}, bf16[128,256]{1,0:T(8,128)(2,1)S(1)}, u32[]{:S(2)}, u32[]{:S(2)}) collective-permute-start(bf16[128,256]{1,0:T(8,128)(2,1)S(1)} %collective-permute-done.mine3), channel_id=1, source_target_pairs={{0,1},{1,0},{2,3},{3,2},{4,5},{5,4},{6,7},{7,6},{8,9},{9,8},{10,11... | collective-permute-start | bytes 196616 | tf_op jit(solution)/shard_map/ppermute | solution.py:278
  10.9 1.3 %collective-permute-start.4 = (bf16[128,256]{1,0:T(8,128)(2,1)S(1)}, bf16[128,256]{1,0:T(8,128)(2,1)S(1)}, u32[]{:S(2)}, u32[]{:S(2)}) collective-permute-start(bf16[128,256]{1,0:T(8,128)(2,1)S(1)} %collective-permute-done.1.mine1), channel_id=1, source_target_pairs={{0,1},{1,0},{2,3},{3,2},{4,5},{5,4},{6,7},{7,6},{8,9},{9,8},{10,11... | collective-permute-start | bytes 196616 | tf_op jit(solution)/shard_map/ppermute | solution.py:278
  12.2 1.3 %collective-permute-start.5 = (bf16[128,256]{1,0:T(8,128)(2,1)S(1)}, bf16[128,256]{1,0:T(8,128)(2,1)S(1)}, u32[]{:S(2)}, u32[]{:S(2)}) collective-permute-start(bf16[128,256]{1,0:T(8,128)(2,1)S(1)} %collective-permute-done.2.mine2), channel_id=1, source_target_pairs={{0,1},{1,0},{2,3},{3,2},{4,5},{5,4},{6,7},{7,6},{8,9},{9,8},{10,11... | collective-permute-start | bytes 196616 | tf_op jit(solution)/shard_map/ppermute | solution.py:278
  14.7 1.6 %collective-permute-start.6 = (bf16[128,1024]{1,0:T(8,128)(2,1)S(1)}, bf16[128,1024]{1,0:T(8,128)(2,1)S(1)}, u32[]{:S(2)}, u32[]{:S(2)}) collective-permute-start(bf16[128,1024]{1,0:T(8,128)(2,1)S(1)} %get-tuple-element.86), channel_id=1, source_target_pairs={{0,1},{1,0},{2,3},{3,2},{4,5},{5,4},{6,7},{7,6},{8,9},{9,8},{10,11... | collective-permute-start | bytes 786440 | tf_op jit(solution)/shard_map/ppermute | solution.py:278
  16.4 8.5 %collective-permute-start.7 = (bf16[128,1024]{1,0:T(8,128)(2,1)S(1)}, bf16[128,1024]{1,0:T(8,128)(2,1)S(1)}, u32[]{:S(2)}, u32[]{:S(2)}) collective-permute-start(bf16[128,1024]{1,0:T(8,128)(2,1)S(1)} %get-tuple-element.91), channel_id=1, source_target_pairs={{0,2},{2,0},{1,3},{3,1},{4,6},{6,4},{5,7},{7,5},{8,10},{10,8},{9,1... | collective-permute-start | bytes 786440 | tf_op jit(solution)/shard_map/ppermute | solution.py:278
  24.9 1.6 %collective-permute-start.8 = (bf16[128,1024]{1,0:T(8,128)(2,1)S(1)}, bf16[128,1024]{1,0:T(8,128)(2,1)S(1)}, u32[]{:S(2)}, u32[]{:S(2)}) collective-permute-start(bf16[128,1024]{1,0:T(8,128)(2,1)S(1)} %shard_map.119.own_ref), channel_id=1, source_target_pairs={{0,1},{1,0},{2,3},{3,2},{4,5},{5,4},{6,7},{7,6},{8,9},{9,8},{10,11... | collective-permute-start | bytes 786440 | tf_op jit(solution)/shard_map/ppermute | solution.py:278
  27.1 11.0 %collective-permute-start.11 = (bf16[528,128]{1,0:T(8,128)(2,1)S(1)}, bf16[528,128]{1,0:T(8,128)(2,1)S(1)}, u32[]{:S(2)}, u32[]{:S(2)}) collective-permute-start(bf16[528,128]{1,0:T(8,128)(2,1)S(1)} %get-tuple-element.115), channel_id=1, source_target_pairs={{0,8},{4,12},{8,0},{12,4},{1,9},{5,13},{9,1},{13,5},{2,10},{6,14},... | collective-permute-start | bytes 405512 | tf_op jit(solution)/shard_map/ppermute | solution.py:278
  29.5 10.3 %collective-permute-start.10 = (bf16[528,128]{1,0:T(8,128)(2,1)S(1)}, bf16[528,128]{1,0:T(8,128)(2,1)S(1)}, u32[]{:S(2)}, u32[]{:S(2)}) collective-permute-start(bf16[528,128]{1,0:T(8,128)(2,1)S(1)} %shard_map.124), channel_id=1, source_target_pairs={{0,4},{4,0},{8,12},{12,8},{1,5},{5,1},{9,13},{13,9},{2,6},{6,2},{1... | collective-permute-start | bytes 405512 | tf_op jit(solution)/shard_map/ppermute | solution.py:278
  31.4 12.0 %copy-start = (f32[128]{0:T(128)S(1)}, f32[128]{0:T(128)}, u32[]{:S(2)}) copy-start(f32[128]{0:T(128)} %param.19) | copy-start | bytes 1540
  31.4 10.2 %collective-permute-start.9 = (bf16[528,128]{1,0:T(8,128)(2,1)S(1)}, bf16[528,128]{1,0:T(8,128)(2,1)S(1)}, u32[]{:S(2)}, u32[]{:S(2)}) collective-permute-start(bf16[528,128]{1,0:T(8,128)(2,1)S(1)} %shard_map.123), channel_id=1, source_target_pairs={{0,12},{4,8},{8,4},{12,0},{1,13},{5,9},{9,5},{13,1},{2,14},{6,10},... | collective-permute-start | bytes 405512 | tf_op jit(solution)/shard_map/ppermute | solution.py:278
  44.6 6.2 %collective-permute-start.12 = (bf16[128,256]{1,0:T(8,128)(2,1)S(1)}, bf16[128,256]{1,0:T(8,128)(2,1)S(1)}, u32[]{:S(2)}, u32[]{:S(2)}) collective-permute-start(bf16[128,256]{1,0:T(8,128)(2,1)S(1)} %get-tuple-element.133), channel_id=1, source_target_pairs={{0,12},{4,8},{8,4},{12,0},{1,13},{5,9},{9,5},{13,1},{2,14},{6,10},... | collective-permute-start | bytes 196616 | tf_op jit(solution)/shard_map/ppermute | solution.py:278
  47.0 5.1 %collective-permute-start.13 = (bf16[128,256]{1,0:T(8,128)(2,1)S(1)}, bf16[128,256]{1,0:T(8,128)(2,1)S(1)}, u32[]{:S(2)}, u32[]{:S(2)}) collective-permute-start(bf16[128,256]{1,0:T(8,128)(2,1)S(1)} %get-tuple-element.134), channel_id=1, source_target_pairs={{0,4},{4,0},{8,12},{12,8},{1,5},{5,1},{9,13},{13,9},{2,6},{6,2},{1... | collective-permute-start | bytes 196616 | tf_op jit(solution)/shard_map/ppermute | solution.py:278
  47.8 5.2 %collective-permute-start.14 = (bf16[128,256]{1,0:T(8,128)(2,1)S(1)}, bf16[128,256]{1,0:T(8,128)(2,1)S(1)}, u32[]{:S(2)}, u32[]{:S(2)}) collective-permute-start(bf16[128,256]{1,0:T(8,128)(2,1)S(1)} %get-tuple-element.135), channel_id=1, source_target_pairs={{0,8},{4,12},{8,0},{12,4},{1,9},{5,13},{9,1},{13,5},{2,10},{6,14},... | collective-permute-start | bytes 196616 | tf_op jit(solution)/shard_map/ppermute | solution.py:278

commit v9 on v8

--- a/solution.py
+++ b/solution.py
@@ -614,18 +614,23 @@
     count = offset_ref.shape[0]
     half = local_ref.shape[2] // 2
     rank = lax.axis_index("ctx")
+    order = [(n, 0) for n in range(count)] + [(n, 1) for n in reversed(range(count))]
+    before = []
     states = [None, None]
-    for number in range(2 * count):
-        source, block = (number, 0) if number < count else (2 * count - 1 - number, 1)
+    for source, block in order:
+        before.append([None if state is None else state.astype(jnp.bfloat16) for state in states])
+        for head in range(2):
+            state = offset_ref[source, head, block]
+            if states[head] is not None:
+                moved = dot(linear_ref[source, head, block, 0:DK], before[-1][head])
+                state = state - moved + growth_ref[source, head, block, 0:1] * states[head]
+            states[head] = state
+    for (source, block), entering in zip(order, before):
         block_rows = slice(block * half, (block + 1) * half)
         for head in range(2):
             out = local_ref[source, head, block_rows]
-            state = offset_ref[source, head, block]
-            if states[head] is not None:
-                moved = dot(linear_ref[source, head, block], states[head].astype(jnp.bfloat16))
-                out = out + moved[DK:]
-                state = state - moved[:DK] + growth_ref[source, head, block, 0:1] * states[head]
-            states[head] = state
+            if entering[head] is not None:
+                out = out + dot(linear_ref[source, head, block, DK : DK + half], entering[head])
             scale = lax.rsqrt(jnp.mean(out * out, axis=1, keepdims=True) + EPSILON)
             outs[source, block_rows, head * DV : (head + 1) * DV] = (out * scale * gain_ref[...]).astype(jnp.bfloat16)
     own_ref[...] = outs[rank]

time: 53.9 us -> 53.9 us (level)
  no operation moved by 1% of the time
where the time goes in v9:
time: 53.9 us; the launch traced here: 53.7 us
  Pallas kernels  21 us (39%)
  starting transfers between devices  16.8 us (31%)
  waiting for transfers between devices  15.1 us (28%)
  between operations  0.81 us (2%)
    ppermute x15, starting transfers between devices, swapped(): lax.ppermute(value, axis, [(i, i ^ mask) for i in range(lax.axis_size(axi...  16.8 us
    ppermute x15, waiting for transfers between devices, swapped(): lax.ppermute(value, axis, [(i, i ^ mask) for i in range(lax.axis_size(axi...  15.1 us
    pallas_call x15, Pallas kernels, vmem_call(): pl.pallas_call(kernel, out_shape=[make(shape, dtype) for shape, dtype in...  13.5 us
    pallas_call x2, Pallas kernels, fetched(): pl.pallas_call(fetch_kernel, out_shape=[pltpu.VMEM(array.shape, array.dty...  5.9 us
  transfers between devices with their start and end apart: 15, of which 10 were waited for; matrix products, arithmetic and copies ran while one was open for 0% of the time, Pallas kernels for 27%

profile of v9, /device:TPU:0, one launch (start us, length us, event | category | flops | bytes accessed | tf_op | source)
XLA Modules:
  0.0 53.7 jit_solution(15447039794270899931)
XLA Ops:
  0.6 0.9 %shard_map.113 = bf16[128,256]{1,0:T(8,128)(2,1)S(1)} custom-call(bf16[128,1024]{1,0:T(8,128)(2,1)} %refs_2_), custom_call_target="tpu_custom_call" | custom-call | tf_op jit(solution)/shard_map/pallas_call | solution.py:671
  1.5 5.1 %collective-permute-start = (bf16[128,256]{1,0:T(8,128)(2,1)S(1)}, bf16[128,256]{1,0:T(8,128)(2,1)S(1)}, u32[]{:S(2)}, u32[]{:S(2)}) collective-permute-start(bf16[128,256]{1,0:T(8,128)(2,1)S(1)} %shard_map.113), channel_id=1, source_target_pairs={{0,12},{4,8},{8,4},{12,0},{1,13},{5,9},{9,5},{13,1},{2,14},{6,10},... | collective-permute-start | bytes 196616 | tf_op jit(solution)/shard_map/ppermute | solution.py:278
  6.6 0.0 collective-permute-start.2
  6.6 0.6 %collective-permute-start.1 = (bf16[128,256]{1,0:T(8,128)(2,1)S(1)}, bf16[128,256]{1,0:T(8,128)(2,1)S(1)}, u32[]{:S(2)}, u32[]{:S(2)}) collective-permute-start(bf16[128,256]{1,0:T(8,128)(2,1)S(1)} %shard_map.113), channel_id=1, source_target_pairs={{0,4},{4,0},{8,12},{12,8},{1,5},{5,1},{9,13},{13,9},{2,6},{6,2},{1... | collective-permute-start | bytes 196616 | tf_op jit(solution)/shard_map/ppermute | solution.py:278
  7.3 2.5 %shard_map.114 = (bf16[128,1024]{1,0:T(8,128)(2,1)S(1)}, bf16[128,1024]{1,0:T(8,128)(2,1)S(1)}, bf16[128,1024]{1,0:T(8,128)(2,1)S(1)}, bf16[1024,2048]{1,0:T(8,128)(2,1)S(1)}, bf16[128,512]{1,0:T(8,128)(2,1)S(1)}) custom-call(bf16[128,1024]{1,0:T(8,128)(2,1)} %refs_0_, bf16[128,1024]{1,0:T(8,128)(2,1)} %refs_1_, bf16[128,1024]{1,0:T(8,128)(2,1)} %refs_2_, ...), custom_call_target="tpu_custom_call" | custom-call | bytes 5111808 | tf_op jit(solution)/shard_map/pallas_call | solution.py:318
  9.7 0.0 collective-permute-done.mine3
  9.8 0.1 collective-permute-start.3
  9.8 1.0 %collective-permute-done.1.mine1 = bf16[128,256]{1,0:T(8,128)(2,1)S(1)} collective-permute-done((bf16[128,256]{1,0:T(8,128)(2,1)S(1)}, bf16[128,256]{1,0:T(8,128)(2,1)S(1)}, u32[]{:S(2)}, u32[]{:S(2)}) %collective-permute-start.1) | collective-permute-done | bytes 65568 | tf_op jit(solution)/shard_map/ppermute | solution.py:278
  10.9 0.0 collective-permute-start.4
  10.9 1.3 %collective-permute-done.2.mine2 = bf16[128,256]{1,0:T(8,128)(2,1)S(1)} collective-permute-done((bf16[128,256]{1,0:T(8,128)(2,1)S(1)}, bf16[128,256]{1,0:T(8,128)(2,1)S(1)}, u32[]{:S(2)}, u32[]{:S(2)}) %collective-permute-start.2) | collective-permute-done | bytes 65568 | tf_op jit(solution)/shard_map/ppermute | solution.py:278
  12.2 0.0 collective-permute-done.3.twin3
  12.2 0.0 collective-permute-start.5
  12.2 0.0 collective-permute-done.4.twin1
  12.2 1.2 %collective-permute-done.5.twin2 = bf16[128,256]{1,0:T(8,128)(2,1)S(1)} collective-permute-done((bf16[128,256]{1,0:T(8,128)(2,1)S(1)}, bf16[128,256]{1,0:T(8,128)(2,1)S(1)}, u32[]{:S(2)}, u32[]{:S(2)}) %collective-permute-start.5) | collective-permute-done | bytes 65568 | tf_op jit(solution)/shard_map/ppermute | solution.py:278
  13.5 1.2 %shard_map.115 = (bf16[128,1024]{1,0:T(8,128)(2,1)S(1)}, bf16[128,1024]{1,0:T(8,128)(2,1)S(1)}) custom-call(bf16[128,1024]{1,0:T(8,128)(2,1)S(1)} %get-tuple-element.79.query_ref, bf16[128,1024]{1,0:T(8,128)(2,1)S(1)} %get-tuple-element.80.gate_ref, bf16[128,1024]{1,0:T(8,128)(2,1)S(1)} %get-tuple-element.81.kv_ref, ...), custom_call_target="tpu_custom_call" | custom-call | tf_op jit(solution)/shard_map/pallas_call | solution.py:265
  14.7 0.2 collective-permute-start.6
  14.9 0.5 shard_map.116.keep_ref
  15.4 0.9 %collective-permute-done.6.came_ref = bf16[128,1024]{1,0:T(8,128)(2,1)S(1)} collective-permute-done((bf16[128,1024]{1,0:T(8,128)(2,1)S(1)}, bf16[128,1024]{1,0:T(8,128)(2,1)S(1)}, u32[]{:S(2)}, u32[]{:S(2)}) %collective-permute-start.6) | collective-permute-done | bytes 262176 | tf_op jit(solution)/shard_map/ppermute | solution.py:278
  16.3 0.1 shard_map.117
  16.4 1.6 %collective-permute-start.7 = (bf16[128,1024]{1,0:T(8,128)(2,1)S(1)}, bf16[128,1024]{1,0:T(8,128)(2,1)S(1)}, u32[]{:S(2)}, u32[]{:S(2)}) collective-permute-start(bf16[128,1024]{1,0:T(8,128)(2,1)S(1)} %get-tuple-element.91), channel_id=1, source_target_pairs={{0,2},{2,0},{1,3},{3,1},{4,6},{6,4},{5,7},{7,5},{8,10},{10,8},{9,1... | collective-permute-start | bytes 786440 | tf_op jit(solution)/shard_map/ppermute | solution.py:278
  18.0 3.4 %shard_map.118 = (bf16[2048,2048]{1,0:T(8,128)(2,1)S(1)}, f32[1,2048]{1,0:T(1,128)S(1)}, bf16[8,2048]{1,0:T(8,128)(2,1)S(1)}, f32[8,128]{1,0:T(8,128)S(1)}) custom-call(bf16[2048,2048]{1,0:T(8,128)(2,1)} %refs_0_.1, f32[1,2048]{1,0:T(1,128)} %bitcast.6, bf16[8,2048]{1,0:T(8,128)(2,1)} %bitcast.5, f32[8,128]{1,0:T(8,128)} %bitcast.7), custom_call_target="tpu_custom_call" | custom-call | bytes 8433664 | tf_op jit(solution)/shard_map/pallas_call | solution.py:318
  21.4 3.5 %collective-permute-done.7.came_ref = bf16[128,1024]{1,0:T(8,128)(2,1)S(1)} collective-permute-done((bf16[128,1024]{1,0:T(8,128)(2,1)S(1)}, bf16[128,1024]{1,0:T(8,128)(2,1)S(1)}, u32[]{:S(2)}, u32[]{:S(2)}) %collective-permute-start.7) | collective-permute-done | bytes 262176 | tf_op jit(solution)/shard_map/ppermute | solution.py:278
  24.9 0.1 collective-permute-start.8
  25.0 0.8 %shard_map.120 = (f32[128,2048]{1,0:T(8,128)S(1)}, f32[8,128]{1,0:T(8,128)S(1)}, f32[128,128]{1,0:T(8,128)S(1)}) custom-call(bf16[128,1024]{1,0:T(8,128)(2,1)S(1)} %shard_map.119.own_ref, f32[1,2048]{1,0:T(1,128)S(1)} %get-tuple-element.101.gain_ref, bf16[2048,2048]{1,0:T(8,128)(2,1)S(1)} %get-tuple-element.102.weight_ref, ...), custom_call_target="tpu_custom_call" | custom-call | tf_op jit(solution)/shard_map/pallas_call | solution.py:265
  25.8 0.7 %collective-permute-done.8.twin_ref = bf16[128,1024]{1,0:T(8,128)(2,1)S(1)} collective-permute-done((bf16[128,1024]{1,0:T(8,128)(2,1)S(1)}, bf16[128,1024]{1,0:T(8,128)(2,1)S(1)}, u32[]{:S(2)}, u32[]{:S(2)}) %collective-permute-start.8) | collective-permute-done | bytes 262176 | tf_op jit(solution)/shard_map/ppermute | solution.py:278
  26.5 0.6 %shard_map.122 = (bf16[128,1024]{1,0:T(8,128)(2,1)S(1)}, f32[128,128]{1,0:T(8,128)S(1)}, f32[16,128]{1,0:T(8,128)S(1)}, bf16[528,128]{1,0:T(8,128)(2,1)S(1)}) custom-call(bf16[128,1024]{1,0:T(8,128)(2,1)S(1)} %collective-permute-done.8.twin_ref, f32[1,2048]{1,0:T(1,128)S(1)} %get-tuple-element.101.gain_ref, bf16[8,2048]{1,0:T(8,128)(2,1)S(1)} %get-tuple-element.103.beta_ref, ...), custom_call_target="tpu_custom_call" | custom-call | tf_op jit(solution)/shard_map/pallas_call | solution.py:265
  27.1 2.0 %collective-permute-start.11 = (bf16[528,128]{1,0:T(8,128)(2,1)S(1)}, bf16[528,128]{1,0:T(8,128)(2,1)S(1)}, u32[]{:S(2)}, u32[]{:S(2)}) collective-permute-start(bf16[528,128]{1,0:T(8,128)(2,1)S(1)} %get-tuple-element.115), channel_id=1, source_target_pairs={{0,8},{4,12},{8,0},{12,4},{1,9},{5,13},{9,1},{13,5},{2,10},{6,14},... | collective-permute-start | bytes 405512 | tf_op jit(solution)/shard_map/ppermute | solution.py:278
  29.1 0.5 shard_map.124
  29.5 1.4 %collective-permute-start.10 = (bf16[528,128]{1,0:T(8,128)(2,1)S(1)}, bf16[528,128]{1,0:T(8,128)(2,1)S(1)}, u32[]{:S(2)}, u32[]{:S(2)}) collective-permute-start(bf16[528,128]{1,0:T(8,128)(2,1)S(1)} %shard_map.124), channel_id=1, source_target_pairs={{0,4},{4,0},{8,12},{12,8},{1,5},{5,1},{9,13},{13,9},{2,6},{6,2},{1... | collective-permute-start | bytes 405512 | tf_op jit(solution)/shard_map/ppermute | solution.py:278
  30.9 0.5 shard_map.123
  31.4 0.0 copy-start
  31.4 1.2 %collective-permute-start.9 = (bf16[528,128]{1,0:T(8,128)(2,1)S(1)}, bf16[528,128]{1,0:T(8,128)(2,1)S(1)}, u32[]{:S(2)}, u32[]{:S(2)}) collective-permute-start(bf16[528,128]{1,0:T(8,128)(2,1)S(1)} %shard_map.123), channel_id=1, source_target_pairs={{0,12},{4,8},{8,4},{12,0},{1,13},{5,9},{9,5},{13,1},{2,14},{6,10},... | collective-permute-start | bytes 405512 | tf_op jit(solution)/shard_map/ppermute | solution.py:278
  32.6 0.5 shard_map.125.refs_0_
  33.0 1.8 %shard_map.126 = (f32[4,2,2,128,128]{4,3,2,1,0:T(8,128)S(1)}, bf16[4,2,2,192,128]{4,3,2,1,0:T(8,128)(2,1)S(1)}, f32[4,2,128,128]{3,2,1,0:T(8,128)S(1)}, f32[4,2,2,8,128]{4,3,2,1,0:T(8,128)S(1)}) custom-call(bf16[528,128]{1,0:T(8,128)(2,1)S(1)} %shard_map.125.refs_0_), custom_call_target="tpu_custom_call" | custom-call | tf_op jit(solution)/shard_map/pallas_call | solution.py:265
  34.8 3.2 %collective-permute-done.11.refs_0_ = bf16[528,128]{1,0:T(8,128)(2,1)S(1)} collective-permute-done((bf16[528,128]{1,0:T(8,128)(2,1)S(1)}, bf16[528,128]{1,0:T(8,128)(2,1)S(1)}, u32[]{:S(2)}, u32[]{:S(2)}) %collective-permute-start.11) | collective-permute-done | bytes 135200 | tf_op jit(solution)/shard_map/ppermute | solution.py:278
  38.0 1.8 %shard_map.127 = (f32[4,2,2,128,128]{4,3,2,1,0:T(8,128)S(1)}, bf16[4,2,2,192,128]{4,3,2,1,0:T(8,128)(2,1)S(1)}, f32[4,2,128,128]{3,2,1,0:T(8,128)S(1)}, f32[4,2,2,8,128]{4,3,2,1,0:T(8,128)S(1)}) custom-call(bf16[528,128]{1,0:T(8,128)(2,1)S(1)} %collective-permute-done.11.refs_0_, ...), custom_call_target="tpu_custom_call", output_to_operand_aliasing={{0}: (1, {}), {1}: (2, {}), {2}: (3, {}), {3}: (4, {})} | custom-call | tf_op jit(solution)/shard_map/pallas_call | solution.py:265
  39.8 0.0 collective-permute-done.10.refs_0_
  39.8 1.8 %shard_map.128 = (f32[4,2,2,128,128]{4,3,2,1,0:T(8,128)S(1)}, bf16[4,2,2,192,128]{4,3,2,1,0:T(8,128)(2,1)S(1)}, f32[4,2,128,128]{3,2,1,0:T(8,128)S(1)}, f32[4,2,2,8,128]{4,3,2,1,0:T(8,128)S(1)}) custom-call(bf16[528,128]{1,0:T(8,128)(2,1)S(1)} %collective-permute-done.10.refs_0_, ...), custom_call_target="tpu_custom_call", output_to_operand_aliasing={{0}: (1, {}), {1}: (2, {}), {2}: (3, {}), {3}: (4, {})} | custom-call | tf_op jit(solution)/shard_map/pallas_call | solution.py:265
  41.6 1.8 %shard_map.129 = (f32[4,2,2,128,128]{4,3,2,1,0:T(8,128)S(1)}, bf16[4,2,2,192,128]{4,3,2,1,0:T(8,128)(2,1)S(1)}, f32[4,2,128,128]{3,2,1,0:T(8,128)S(1)}, f32[4,2,2,8,128]{4,3,2,1,0:T(8,128)S(1)}) custom-call(bf16[528,128]{1,0:T(8,128)(2,1)S(1)} %collective-permute-done.9.refs_0_, ...), custom_call_target="tpu_custom_call", output_to_operand_aliasing={{0}: (1, {}), {1}: (2, {}), {2}: (3, {}), {3}: (4, {})} | custom-call | tf_op jit(solution)/shard_map/pallas_call | solution.py:265
  43.4 1.2 %shard_map.130 = (bf16[128,256]{1,0:T(8,128)(2,1)S(1)}, bf16[128,256]{1,0:T(8,128)(2,1)S(1)}, bf16[128,256]{1,0:T(8,128)(2,1)S(1)}, bf16[128,256]{1,0:T(8,128)(2,1)S(1)}) custom-call(f32[4,2,2,128,128]{4,3,2,1,0:T(8,128)S(1)} %get-tuple-element.128.offset_ref, bf16[4,2,2,192,128]{4,3,2,1,0:T(8,128)(2,1)S(1)} %get-tuple-element.129.linear_ref, ...), custom_call_target="tpu_custom_call" | custom-call | tf_op jit(solution)/shard_map/pallas_call | solution.py:265
  44.6 2.4 %collective-permute-start.12 = (bf16[128,256]{1,0:T(8,128)(2,1)S(1)}, bf16[128,256]{1,0:T(8,128)(2,1)S(1)}, u32[]{:S(2)}, u32[]{:S(2)}) collective-permute-start(bf16[128,256]{1,0:T(8,128)(2,1)S(1)} %get-tuple-element.133), channel_id=1, source_target_pairs={{0,12},{4,8},{8,4},{12,0},{1,13},{5,9},{9,5},{13,1},{2,14},{6,10},... | collective-permute-start | bytes 196616 | tf_op jit(solution)/shard_map/ppermute | solution.py:278
  47.0 0.8 %collective-permute-start.13 = (bf16[128,256]{1,0:T(8,128)(2,1)S(1)}, bf16[128,256]{1,0:T(8,128)(2,1)S(1)}, u32[]{:S(2)}, u32[]{:S(2)}) collective-permute-start(bf16[128,256]{1,0:T(8,128)(2,1)S(1)} %get-tuple-element.134), channel_id=1, source_target_pairs={{0,4},{4,0},{8,12},{12,8},{1,5},{5,1},{9,13},{13,9},{2,6},{6,2},{1... | collective-permute-start | bytes 196616 | tf_op jit(solution)/shard_map/ppermute | solution.py:278
  47.8 1.3 %collective-permute-start.14 = (bf16[128,256]{1,0:T(8,128)(2,1)S(1)}, bf16[128,256]{1,0:T(8,128)(2,1)S(1)}, u32[]{:S(2)}, u32[]{:S(2)}) collective-permute-start(bf16[128,256]{1,0:T(8,128)(2,1)S(1)} %get-tuple-element.135), channel_id=1, source_target_pairs={{0,8},{4,12},{8,0},{12,4},{1,9},{5,13},{9,1},{13,5},{2,10},{6,14},... | collective-permute-start | bytes 196616 | tf_op jit(solution)/shard_map/ppermute | solution.py:278
  49.1 0.7 %shard_map.121 = bf16[128,512]{1,0:T(8,128)(2,1)} custom-call(bf16[128,1024]{1,0:T(8,128)(2,1)S(1)} %shard_map.119.own_ref, bf16[128,1024]{1,0:T(8,128)(2,1)S(1)} %collective-permute-done.8.twin_ref), custom_call_target="tpu_custom_call" | custom-call | tf_op jit(solution)/shard_map/pallas_call | solution.py:265
  49.7 1.1 %collective-permute-done.12.back3 = bf16[128,256]{1,0:T(8,128)(2,1)S(1)} collective-permute-done((bf16[128,256]{1,0:T(8,128)(2,1)S(1)}, bf16[128,256]{1,0:T(8,128)(2,1)S(1)}, u32[]{:S(2)}, u32[]{:S(2)}) %collective-permute-start.12) | collective-permute-done | bytes 65568 | tf_op jit(solution)/shard_map/ppermute | solution.py:278
  50.9 1.2 %collective-permute-done.13.back1 = bf16[128,256]{1,0:T(8,128)(2,1)S(1)} collective-permute-done((bf16[128,256]{1,0:T(8,128)(2,1)S(1)}, bf16[128,256]{1,0:T(8,128)(2,1)S(1)}, u32[]{:S(2)}, u32[]{:S(2)}) %collective-permute-start.13) | collective-permute-done | bytes 65568 | tf_op jit(solution)/shard_map/ppermute | solution.py:278
  52.0 0.9 %collective-permute-done.14.back2 = bf16[128,256]{1,0:T(8,128)(2,1)S(1)} collective-permute-done((bf16[128,256]{1,0:T(8,128)(2,1)S(1)}, bf16[128,256]{1,0:T(8,128)(2,1)S(1)}, u32[]{:S(2)}, u32[]{:S(2)}) %collective-permute-start.14) | collective-permute-done | bytes 65568 | tf_op jit(solution)/shard_map/ppermute | solution.py:278
  53.0 0.7 %shard_map.131 = bf16[128,1024]{1,0:T(8,128)(2,1)} custom-call(bf16[128,256]{1,0:T(8,128)(2,1)S(1)} %get-tuple-element.132.own_ref, bf16[128,256]{1,0:T(8,128)(2,1)S(1)} %collective-permute-done.12.back3, bf16[128,256]{1,0:T(8,128)(2,1)S(1)} %collective-permute-done.13.back1, bf16[128,256]{1,0:T(8,128)(2,1)S(1)} %collective-permute-done.14.back2), custom_call_target="tpu_custom_call" | custom-call | tf_op jit(solution)/shard_map/pallas_call | solution.py:754
  (3 shorter events, 0.1 us)
Async XLA Ops:
  1.5 8.3 %collective-permute-start = (bf16[128,256]{1,0:T(8,128)(2,1)S(1)}, bf16[128,256]{1,0:T(8,128)(2,1)S(1)}, u32[]{:S(2)}, u32[]{:S(2)}) collective-permute-start(bf16[128,256]{1,0:T(8,128)(2,1)S(1)} %shard_map.113), channel_id=1, source_target_pairs={{0,12},{4,8},{8,4},{12,0},{1,13},{5,9},{9,5},{13,1},{2,14},{6,10},... | collective-permute-start | bytes 196616 | tf_op jit(solution)/shard_map/ppermute | solution.py:278
  6.6 5.6 %collective-permute-start.2 = (bf16[128,256]{1,0:T(8,128)(2,1)S(1)}, bf16[128,256]{1,0:T(8,128)(2,1)S(1)}, u32[]{:S(2)}, u32[]{:S(2)}) collective-permute-start(bf16[128,256]{1,0:T(8,128)(2,1)S(1)} %shard_map.113), channel_id=1, source_target_pairs={{0,8},{4,12},{8,0},{12,4},{1,9},{5,13},{9,1},{13,5},{2,10},{6,14},... | collective-permute-start | bytes 196616 | tf_op jit(solution)/shard_map/ppermute | solution.py:278
  6.6 4.3 %collective-permute-start.1 = (bf16[128,256]{1,0:T(8,128)(2,1)S(1)}, bf16[128,256]{1,0:T(8,128)(2,1)S(1)}, u32[]{:S(2)}, u32[]{:S(2)}) collective-permute-start(bf16[128,256]{1,0:T(8,128)(2,1)S(1)} %shard_map.113), channel_id=1, source_target_pairs={{0,4},{4,0},{8,12},{12,8},{1,5},{5,1},{9,13},{13,9},{2,6},{6,2},{1... | collective-permute-start | bytes 196616 | tf_op jit(solution)/shard_map/ppermute | solution.py:278
  9.8 2.5 %collective-permute-start.3 = (bf16[128,256]{1,0:T(8,128)(2,1)S(1)}, bf16[128,256]{1,0:T(8,128)(2,1)S(1)}, u32[]{:S(2)}, u32[]{:S(2)}) collective-permute-start(bf16[128,256]{1,0:T(8,128)(2,1)S(1)} %collective-permute-done.mine3), channel_id=1, source_target_pairs={{0,1},{1,0},{2,3},{3,2},{4,5},{5,4},{6,7},{7,6},{8,9},{9,8},{10,11... | collective-permute-start | bytes 196616 | tf_op jit(solution)/shard_map/ppermute | solution.py:278
  10.9 1.3 %collective-permute-start.4 = (bf16[128,256]{1,0:T(8,128)(2,1)S(1)}, bf16[128,256]{1,0:T(8,128)(2,1)S(1)}, u32[]{:S(2)}, u32[]{:S(2)}) collective-permute-start(bf16[128,256]{1,0:T(8,128)(2,1)S(1)} %collective-permute-done.1.mine1), channel_id=1, source_target_pairs={{0,1},{1,0},{2,3},{3,2},{4,5},{5,4},{6,7},{7,6},{8,9},{9,8},{10,11... | collective-permute-start | bytes 196616 | tf_op jit(solution)/shard_map/ppermute | solution.py:278
  12.2 1.3 %collective-permute-start.5 = (bf16[128,256]{1,0:T(8,128)(2,1)S(1)}, bf16[128,256]{1,0:T(8,128)(2,1)S(1)}, u32[]{:S(2)}, u32[]{:S(2)}) collective-permute-start(bf16[128,256]{1,0:T(8,128)(2,1)S(1)} %collective-permute-done.2.mine2), channel_id=1, source_target_pairs={{0,1},{1,0},{2,3},{3,2},{4,5},{5,4},{6,7},{7,6},{8,9},{9,8},{10,11... | collective-permute-start | bytes 196616 | tf_op jit(solution)/shard_map/ppermute | solution.py:278
  14.7 1.6 %collective-permute-start.6 = (bf16[128,1024]{1,0:T(8,128)(2,1)S(1)}, bf16[128,1024]{1,0:T(8,128)(2,1)S(1)}, u32[]{:S(2)}, u32[]{:S(2)}) collective-permute-start(bf16[128,1024]{1,0:T(8,128)(2,1)S(1)} %get-tuple-element.86), channel_id=1, source_target_pairs={{0,1},{1,0},{2,3},{3,2},{4,5},{5,4},{6,7},{7,6},{8,9},{9,8},{10,11... | collective-permute-start | bytes 786440 | tf_op jit(solution)/shard_map/ppermute | solution.py:278
  16.4 8.5 %collective-permute-start.7 = (bf16[128,1024]{1,0:T(8,128)(2,1)S(1)}, bf16[128,1024]{1,0:T(8,128)(2,1)S(1)}, u32[]{:S(2)}, u32[]{:S(2)}) collective-permute-start(bf16[128,1024]{1,0:T(8,128)(2,1)S(1)} %get-tuple-element.91), channel_id=1, source_target_pairs={{0,2},{2,0},{1,3},{3,1},{4,6},{6,4},{5,7},{7,5},{8,10},{10,8},{9,1... | collective-permute-start | bytes 786440 | tf_op jit(solution)/shard_map/ppermute | solution.py:278
  24.9 1.6 %collective-permute-start.8 = (bf16[128,1024]{1,0:T(8,128)(2,1)S(1)}, bf16[128,1024]{1,0:T(8,128)(2,1)S(1)}, u32[]{:S(2)}, u32[]{:S(2)}) collective-permute-start(bf16[128,1024]{1,0:T(8,128)(2,1)S(1)} %shard_map.119.own_ref), channel_id=1, source_target_pairs={{0,1},{1,0},{2,3},{3,2},{4,5},{5,4},{6,7},{7,6},{8,9},{9,8},{10,11... | collective-permute-start | bytes 786440 | tf_op jit(solution)/shard_map/ppermute | solution.py:278
  27.1 11.0 %collective-permute-start.11 = (bf16[528,128]{1,0:T(8,128)(2,1)S(1)}, bf16[528,128]{1,0:T(8,128)(2,1)S(1)}, u32[]{:S(2)}, u32[]{:S(2)}) collective-permute-start(bf16[528,128]{1,0:T(8,128)(2,1)S(1)} %get-tuple-element.115), channel_id=1, source_target_pairs={{0,8},{4,12},{8,0},{12,4},{1,9},{5,13},{9,1},{13,5},{2,10},{6,14},... | collective-permute-start | bytes 405512 | tf_op jit(solution)/shard_map/ppermute | solution.py:278
  29.5 10.3 %collective-permute-start.10 = (bf16[528,128]{1,0:T(8,128)(2,1)S(1)}, bf16[528,128]{1,0:T(8,128)(2,1)S(1)}, u32[]{:S(2)}, u32[]{:S(2)}) collective-permute-start(bf16[528,128]{1,0:T(8,128)(2,1)S(1)} %shard_map.124), channel_id=1, source_target_pairs={{0,4},{4,0},{8,12},{12,8},{1,5},{5,1},{9,13},{13,9},{2,6},{6,2},{1... | collective-permute-start | bytes 405512 | tf_op jit(solution)/shard_map/ppermute | solution.py:278
  31.4 12.0 %copy-start = (f32[128]{0:T(128)S(1)}, f32[128]{0:T(128)}, u32[]{:S(2)}) copy-start(f32[128]{0:T(128)} %param.19) | copy-start | bytes 1540
  31.4 10.2 %collective-permute-start.9 = (bf16[528,128]{1,0:T(8,128)(2,1)S(1)}, bf16[528,128]{1,0:T(8,128)(2,1)S(1)}, u32[]{:S(2)}, u32[]{:S(2)}) collective-permute-start(bf16[528,128]{1,0:T(8,128)(2,1)S(1)} %shard_map.123), channel_id=1, source_target_pairs={{0,12},{4,8},{8,4},{12,0},{1,13},{5,9},{9,5},{13,1},{2,14},{6,10},... | collective-permute-start | bytes 405512 | tf_op jit(solution)/shard_map/ppermute | solution.py:278
  44.6 6.3 %collective-permute-start.12 = (bf16[128,256]{1,0:T(8,128)(2,1)S(1)}, bf16[128,256]{1,0:T(8,128)(2,1)S(1)}, u32[]{:S(2)}, u32[]{:S(2)}) collective-permute-start(bf16[128,256]{1,0:T(8,128)(2,1)S(1)} %get-tuple-element.133), channel_id=1, source_target_pairs={{0,12},{4,8},{8,4},{12,0},{1,13},{5,9},{9,5},{13,1},{2,14},{6,10},... | collective-permute-start | bytes 196616 | tf_op jit(solution)/shard_map/ppermute | solution.py:278
  47.0 5.1 %collective-permute-start.13 = (bf16[128,256]{1,0:T(8,128)(2,1)S(1)}, bf16[128,256]{1,0:T(8,128)(2,1)S(1)}, u32[]{:S(2)}, u32[]{:S(2)}) collective-permute-start(bf16[128,256]{1,0:T(8,128)(2,1)S(1)} %get-tuple-element.134), channel_id=1, source_target_pairs={{0,4},{4,0},{8,12},{12,8},{1,5},{5,1},{9,13},{13,9},{2,6},{6,2},{1... | collective-permute-start | bytes 196616 | tf_op jit(solution)/shard_map/ppermute | solution.py:278
  47.8 5.2 %collective-permute-start.14 = (bf16[128,256]{1,0:T(8,128)(2,1)S(1)}, bf16[128,256]{1,0:T(8,128)(2,1)S(1)}, u32[]{:S(2)}, u32[]{:S(2)}) collective-permute-start(bf16[128,256]{1,0:T(8,128)(2,1)S(1)} %get-tuple-element.135), channel_id=1, source_target_pairs={{0,8},{4,12},{8,0},{12,4},{1,9},{5,13},{9,1},{13,5},{2,10},{6,14},... | collective-permute-start | bytes 196616 | tf_op jit(solution)/shard_map/ppermute | solution.py:278
